TPU v7x, 512 devices: a whole 4x4x16 slice. The times are simulated.
512 devices in a mesh: dp: 16 (over y, z_lo), fsdp: 32 (over x, z_hi, core).
Axes of the slice: x: 4, y: 4, z: 16 (z_hi: 4, z_lo: 4; z = z_hi * 4 + z_lo), core: 2. Of those that a mesh axis runs over, the one named last changes fastest.
Arguments:
- hidden: bfloat16 [8192, 16384], P('dp', 'fsdp'), may hold values from -200 to 200
- upstream: bfloat16 [8192, 4096], P('dp', 'fsdp'), may hold values from -16 to 16
- down_weight: bfloat16 [16384, 4096], P('fsdp', 'dp'), may hold values from -0.09375 to 0.09375
- mask_logits: float32 [4096, 6, 4096], P('fsdp', None, 'dp'), may hold values from -10 to 610
- gumbel_noise: float32 [4096, 6, 4096], P('fsdp', None, 'dp'), may hold values from -3 to 14
Outputs:
- grad_hidden: bfloat16 [8192, 16384], P('dp', 'fsdp')
- logit_step: float32 [4096, 6, 4096], P('fsdp', None, 'dp')
All inputs are finite; a program needn't handle non-finite values.
Results may differ from a plain program's by a relative error of at most 0.02.
Values may be sent and summed in bfloat16 or wider, within the bound.
No kernel may reach another device: no remote copies, remote signals or barrier semaphores. Data moves between devices by JAX's collectives and lax.ppermute only.
A program may use at most 128 MiB of HBM per device.

v0:
```python
import jax
import jax.numpy as jnp
import numpy as np
from jax import lax
from jax.sharding import PartitionSpec as P

CANDIDATES = np.array(
    [[1, 1, 0, 0], [1, 0, 1, 0], [1, 0, 0, 1], [0, 1, 1, 0], [0, 1, 0, 1], [0, 0, 1, 1]], np.float32
)
TEMPER = 2.0


def build_masked(weight_groups, rounded):
    table = jnp.asarray(CANDIDATES, jnp.float32)
    keep = jnp.einsum("gkc,kj->gjc", rounded.astype(jnp.float32), table)
    return (weight_groups.astype(jnp.float32) * keep).astype(jnp.bfloat16)


def body(hidden, upstream, down_weight, mask_logits, gumbel_noise):
    group_count, _, col_count = mask_logits.shape
    row_count = down_weight.shape[0]
    probs = jax.nn.softmax((mask_logits + gumbel_noise) / TEMPER, axis=1)
    rounded = probs.astype(jnp.bfloat16)
    upstream_all = lax.all_gather(upstream, "fsdp", axis=1, tiled=True)
    built = build_masked(
        lax.all_gather(down_weight.reshape(group_count, 4, col_count), "dp", axis=2, tiled=True),
        lax.all_gather(rounded, "dp", axis=2, tiled=True),
    ).reshape(row_count, -1)
    segment = upstream_all
    carried = lax.dot_general(
        segment, built, (((1,), (1,)), ((), ())), preferred_element_type=jnp.float32
    )
    grad_hidden = carried.astype(jnp.bfloat16)
    segment = upstream_all
    grad_masked = (
        lax.psum_scatter(
            lax.dot_general(
                segment, hidden, (((0,), (0,)), ((), ())), preferred_element_type=jnp.float32
            ).astype(jnp.bfloat16),
            "dp",
            scatter_dimension=0,
            tiled=True,
        )
        .astype(jnp.float32)
        .T
    )
    table = jnp.asarray(CANDIDATES, jnp.float32)
    product = (grad_masked * down_weight.astype(jnp.float32)).reshape(group_count, 4, col_count)
    grad_probs = jnp.einsum("gjc,kj->gkc", product, table)
    grad_logits = probs * (grad_probs - jnp.sum(probs * grad_probs, axis=1, keepdims=True)) / TEMPER
    square_sum = lax.psum(jnp.sum(grad_logits * grad_logits), ("dp", "fsdp"))
    entries = group_count * 6 * col_count * lax.axis_size("dp") * lax.axis_size("fsdp")
    logit_step = grad_logits * lax.rsqrt(square_sum / entries + 1e-06)
    return (grad_hidden, logit_step)


def solution(mesh):
    return jax.shard_map(
        body,
        mesh=mesh,
        in_specs=(
            P("dp", "fsdp"),
            P("dp", "fsdp"),
            P("fsdp", "dp"),
            P("fsdp", None, "dp"),
            P("fsdp", None, "dp"),
        ),
        out_specs=(P("dp", "fsdp"), P("fsdp", None, "dp")),
        check_vma=False,
    )
```

profile of v0, /device:TPU:1, one launch (start us, length us, event | category | flops | bytes accessed | tf_op | source)
XLA Modules:
  0.0 659.2 jit_solution(16788763165892010354)
XLA Ops:
  7.2 0.0 copy-start
  7.2 0.0 all-gather.8.cloned.1.call-start
  7.2 0.7 all-gather.8.cloned.1.call-update
  7.9 0.0 all-gather.4.cloned.1.call-start
  8.0 1.7 reshape.16
  9.7 0.0 all-gather.4.cloned.1.call-update
  9.7 0.0 all-gather.6.cloned.1.call-start
  9.8 2.8 fusion.15
  12.6 1.0 fusion.14
  13.6 0.0 all-gather.6.cloned.1.call-update
  13.6 0.0 reduce-scatter.2.cloned.1.call-start
  13.6 106.8 %all-gather.8.cloned.1.call-done = bf16[512,4096]{1,0:T(8,128)(2,1)} async-done(((bf16[512,128]{1,0:T(8,128)(2,1)}), bf16[512,4096]{1,0:T(8,128)(2,1)}) %all-gather.8.cloned.1.call-update) | async-done | bytes 4194320 | tf_op jit(solution)/shard_map/all_gather | solution.py:24
  120.4 0.0 copy-done
  120.4 6.5 convolution_convert_fusion
  126.9 0.0 copy-start.1
  126.9 0.0 copy-start.2
  126.9 0.0 reduce-scatter.2.cloned.1.call-update
  127.0 0.9 copy-done.1
  127.9 0.1 copy.17
  128.0 101.1 %all-gather.4.cloned.1.call-done = bf16[128,4,4096]{2,1,0:T(4,128)(2,1)} async-done(((bf16[128,4,256]{2,1,0:T(4,128)(2,1)}), bf16[128,4,4096]{2,1,0:T(4,128)(2,1)}) %all-gather.4.cloned.1.call-update) | async-done | bytes 4194320 | tf_op jit(solution)/shard_map/all_gather | solution.py:26
  229.2 200.8 %all-gather.6.cloned.1.call-done = bf16[128,6,4096]{2,1,0:T(8,128)(2,1)} async-done(((bf16[128,6,256]{2,1,0:T(8,128)(2,1)}), bf16[128,6,4096]{2,1,0:T(8,128)(2,1)}) %all-gather.6.cloned.1.call-update) | async-done | bytes 6291472 | tf_op jit(solution)/shard_map/all_gather | solution.py:27
  430.0 0.0 copy-done.2
  430.0 10.9 %fusion.2 = bf16[128,4,4096]{2,1,0:T(4,128)(2,1)} fusion(bf16[128,4,4096]{2,1,0:T(4,128)(2,1)} %all-gather.4.cloned.1.call-done, bf16[128,6,4096]{2,1,0:T(8,128)(2,1)} %all-gather.6.cloned.1.call-done, bf16[6,4,1]{0,1,2:T(4,128)(2,1)S(1)} %copy-done.2), kind=kOutput, calls=%fused_computation.3 | convolution fusion | flops 31457280 | bytes 14680112 | tf_op jit(solution)/shard_map/gkc,kj->gjc/dot_general | solution.py:15
  440.8 7.0 %reshape.17 = bf16[512,4096]{1,0:T(8,128)(2,1)} reshape(bf16[128,4,4096]{2,1,0:T(4,128)(2,1)} %fusion.2) | data formatting | bytes 8388608 | tf_op jit(solution)/shard_map/reshape | solution.py:28
  447.8 5.8 fusion.7
  453.7 1.0 copy.19
  454.7 80.4 %reduce-scatter.2.cloned.1.call-done = bf16[256,512]{1,0:T(8,128)(2,1)} async-done(((bf16[4096,512]{1,0:T(8,128)(2,1)}), bf16[256,512]{1,0:T(8,128)(2,1)}) %reduce-scatter.2.cloned.1.call-update) | async-done | bytes 262160 | tf_op jit(solution)/shard_map/reduce_scatter | solution.py:36
  535.0 1.0 bitcast_multiply_fusion.1
  536.1 0.1 copy.18
  536.2 0.1 reshape.18
  536.3 0.3 convolution_bitcast_fusion
  536.6 8.3 %multiply_reduce_fusion = (f32[]{:T(128)}, f32[128,6,256]{2,1,0:T(8,128)S(1)}) fusion(f32[128,6,256]{2,1,0:T(8,128)S(1)} %convolution_bitcast_fusion, f32[128,6,256]{2,1,0:T(8,128)S(1)} %get-tuple-element.7, f32[128,256]{1,0:T(8,128)S(1)} %get-tuple-element.6), kind=kOutput, calls=%fused_computation.14 | output fusion | flops 1605636 | bytes 2490372 | tf_op jit(solution)/shard_map/sub | solution.py:50
  544.9 105.8 %psum.7 = f32[]{:T(128)} all-reduce(f32[]{:T(128)} %get-tuple-element.8), channel_id=1, replica_groups=mesh['dp'=16,'fsdp'=32] {'dp','fsdp'}, use_global_device_ids=true, to_apply=%region_5.0 | all-reduce | flops 1 | bytes 8 | tf_op jit(solution)/shard_map/psum | solution.py:51
  651.4 0.1 broadcast_multiply_fusion
  651.5 1.1 copy.20
Async XLA Ops:
  7.2 113.2 %copy-start = (bf16[512,512]{1,0:T(8,128)(2,1)S(1)}, bf16[512,512]{1,0:T(8,128)(2,1)}, u32[]{:S(2)}) copy-start(bf16[512,512]{1,0:T(8,128)(2,1)} %param.7) | copy-start | bytes 1572868
  7.2 113.2 %all-gather.8.cloned.1.call-start = ((), (), s32[]{:S(2)}) async-start(), calls=%async_computation.3 | async-start | bytes 4325376 | tf_op jit(solution)/shard_map/all_gather | solution.py:24
  7.9 221.3 %all-gather.4.cloned.1.call-start = ((), (), s32[]{:S(2)}) async-start(), calls=%async_computation.1 | async-start | bytes 4456448 | tf_op jit(solution)/shard_map/all_gather | solution.py:26
  9.7 420.2 %all-gather.6.cloned.1.call-start = ((), (), s32[]{:S(2)}) async-start(), calls=%async_computation.2 | async-start | bytes 8912896 | tf_op jit(solution)/shard_map/all_gather | solution.py:27
  13.6 521.5 %reduce-scatter.2.cloned.1.call-start = ((), (), s32[]{:S(2)}) async-start(), calls=%async_computation.4 | async-start | bytes 4456448 | tf_op jit(solution)/shard_map/reduce_scatter | solution.py:36
  126.9 0.9 copy-start.1
  126.9 303.0 %copy-start.2 = (bf16[6,4,1]{0,1,2:T(4,128)(2,1)S(1)}, bf16[6,4,1]{0,1,2:T(4,128)(2,1)}, u32[]{:S(2)}) copy-start(bf16[6,4,1]{0,1,2:T(4,128)(2,1)} %constant.32) | copy-start | bytes 148
Sparse Core Ops, SparseCore 0:
  11.1 109.2 all-gather.7
  123.0 106.1 all-gather.3
  231.8 198.1 all-gather.5
  432.6 102.3 reduce-scatter.1
where the time goes:
time: 660 us; the launch traced here: 659 us
  waiting for transfers between devices  490 us (74%)
  blocking collectives  106 us (16%)
  matrix products  23.6 us (4%)
  between operations  14.5 us (2%)
  other arithmetic  13.2 us (2%)
  local copies, waits for them, and re-layouts  12.1 us (2%)
    all_gather x1, waiting for transfers between devices, body(): lax.all_gather(rounded, 'dp', axis=2, tiled=True)  201 us
    all_gather x1, waiting for transfers between devices, body(): upstream_all = lax.all_gather(upstream, 'fsdp', axis=1, tiled=True)  107 us
    psum x1, blocking collectives, body(): square_sum = lax.psum(jnp.sum(grad_logits * grad_logits), ('dp', 'fsdp'))  106 us
    all_gather x1, waiting for transfers between devices, body(): lax.all_gather(down_weight.reshape(group_count, 4, col_count), 'dp', axis...  101 us
    reduce_scatter x1, waiting for transfers between devices, body(): lax.psum_scatter(lax.dot_general(segment, hidden, (((0,), (0,)), ((), ())...  80.4 us
  transfers between devices with their start and end apart: 4, of which 4 were waited for; matrix products, arithmetic and copies ran while one was open for 6% of the time, Pallas kernels for 0%

commit v1 on v0

v1 whole, which is shorter than its diff:
```python
import jax
import jax.numpy as jnp
import numpy as np
from jax import lax
from jax.experimental import pallas as pl
from jax.experimental.pallas import tpu as pltpu
from jax.sharding import Mesh, PartitionSpec as P

PAIRS = ((0, 1), (0, 2), (0, 3), (1, 2), (1, 3), (2, 3))
TEMPER = 2.0
VMEM = 48 * 1024 * 1024


def grad_masked_kernel(place, hid, a0, a1, a2, a3, b0, b1, b2, b3, o0, o1, o2, o3):
    l, x, c = place[0], place[1], place[2]
    own, other = (a0, a1, a2, a3), (b0, b1, b2, b3)
    for e, out in enumerate((o0, o1, o2, o3)):
        col = lax.rem(l + e, 4)
        total = None
        for k in range(4):
            tok = lax.rem(x + 4 - k, 4)
            mine, theirs = own[k][col], other[k][col]
            first = jnp.where(c == 0, mine, theirs)
            second = jnp.where(c == 0, theirs, mine)
            part = jnp.dot(
                hid[tok], jnp.concatenate([first, second], axis=1), preferred_element_type=jnp.float32
            )
            total = part if total is None else total + part
        out[...] = total.astype(out.dtype)


def grad_hidden_kernel(place, mt, a0, a1, a2, a3, b0, b1, b2, b3, out):
    x, c = place[1], place[2]
    own, other = (a0, a1, a2, a3), (b0, b1, b2, b3)
    for k in range(4):
        tok = lax.rem(x + 4 - k, 4)
        pieces = []
        for col in range(4):
            mine, theirs = own[k][col], other[k][col]
            pieces += [jnp.where(c == 0, mine, theirs), jnp.where(c == 0, theirs, mine)]
        out[tok] = jnp.dot(
            jnp.concatenate(pieces, axis=1), mt[...], preferred_element_type=jnp.float32
        ).astype(out.dtype)


def grad_logits_kernel(g0, g1, g2, g3, w, probs, out, squares):
    prod = []
    for j in range(4):
        rows = pl.ds(128 * j, 128)
        total = (
            g0[rows, :]
            + g1[rows, :].astype(jnp.float32)
            + g2[rows, :].astype(jnp.float32)
            + g3[rows, :].astype(jnp.float32)
        )
        prod.append(total * w[rows, :].astype(jnp.float32))
    grads = [prod[a] + prod[b] for a, b in PAIRS]
    mean = sum(probs[k] * grads[k] for k in range(6))
    sums = jnp.zeros((128, 256), jnp.float32)
    for k in range(6):
        value = probs[k] * (grads[k] - mean) * (1.0 / TEMPER)
        out[k] = value
        sums = sums + value * value
    sums = jnp.sum(sums, axis=0, keepdims=True)
    squares[...] = sums[:, :128] + sums[:, 128:]


def body(hidden, upstream, down_weight, mask_logits, gumbel_noise):
    y, l, x, h, c = (lax.axis_index(a) for a in ("y", "l", "x", "h", "c"))
    place = jnp.stack([l, x, c, y]).astype(jnp.int32)

    up = lax.all_to_all(jnp.broadcast_to(upstream[None], (4, 512, 128)), "h", 0, 0)

    order = np.zeros((512, 512), np.float32)
    for j in range(4):
        for g in range(128):
            order[j * 128 + g, 4 * g + j] = 1.0
    order = jnp.asarray(order, jnp.bfloat16)
    hid_t = lax.dot_general(
        order, hidden, (((1,), (1,)), ((), ())), preferred_element_type=jnp.float32
    ).astype(jnp.bfloat16)
    hid_all = lax.all_to_all(jnp.broadcast_to(hid_t[None], (4, 512, 512)), "y", 0, 0)

    weight = jnp.dot(order, down_weight, preferred_element_type=jnp.float32).astype(jnp.bfloat16)
    logits = jnp.transpose(mask_logits, (1, 0, 2)) + jnp.transpose(gumbel_noise, (1, 0, 2))
    probs = jax.nn.softmax(logits / TEMPER, axis=0)
    rounded = probs.astype(jnp.bfloat16).astype(jnp.float32)
    keep = [sum(rounded[k] for k in range(6) if j in PAIRS[k]) for j in range(4)]
    masked = jnp.concatenate(
        [(weight[128 * j : 128 * j + 128].astype(jnp.float32) * keep[j]).astype(jnp.bfloat16) for j in range(4)]
    )
    masked_t = lax.dot_general(
        masked, order, (((0,), (0,)), ((), ())), preferred_element_type=jnp.float32
    ).astype(jnp.bfloat16)
    mt = lax.all_to_all(jnp.broadcast_to(masked_t[None], (4, 256, 512)), "l", 0, 0).reshape(1024, 512)

    own = [
        lax.ppermute(up, ("y", "x"), [(b * 4 + a, a * 4 + (b + k) % 4) for b in range(4) for a in range(4)])
        for k in range(4)
    ]
    other = [lax.ppermute(u, "c", [(0, 1), (1, 0)]) for u in own]

    smem = pl.BlockSpec(memory_space=pltpu.SMEM)
    vmem = pl.BlockSpec(memory_space=pltpu.VMEM)
    params = pltpu.CompilerParams(vmem_limit_bytes=VMEM)
    g = pl.pallas_call(
        grad_masked_kernel,
        out_shape=[jax.ShapeDtypeStruct((512, 256), jnp.float32)]
        + [jax.ShapeDtypeStruct((512, 256), jnp.bfloat16)] * 3,
        in_specs=[smem] + [vmem] * 9,
        out_specs=[vmem] * 4,
        compiler_params=params,
        cost_estimate=pl.CostEstimate(flops=2 * 512 * 2048 * 1024, bytes_accessed=7 << 20, transcendentals=0),
        name="grad_masked",
    )(place, hid_all, *own, *other)
    got = [lax.ppermute(g[e], "l", [(i, (i + e) % 4) for i in range(4)]) for e in (1, 2, 3)]

    gh = pl.pallas_call(
        grad_hidden_kernel,
        out_shape=jax.ShapeDtypeStruct((4, 512, 512), jnp.bfloat16),
        in_specs=[smem] + [vmem] * 9,
        out_specs=vmem,
        compiler_params=params,
        cost_estimate=pl.CostEstimate(flops=2 * 512 * 2048 * 1024, bytes_accessed=7 << 20, transcendentals=0),
        name="grad_hidden",
    )(place, mt, *own, *other)
    gh = lax.all_to_all(gh, "y", 0, 0)
    grad_hidden = jnp.sum(gh.astype(jnp.float32), axis=0).astype(jnp.bfloat16)

    grad_logits, squares = pl.pallas_call(
        grad_logits_kernel,
        out_shape=[
            jax.ShapeDtypeStruct((6, 128, 256), jnp.float32),
            jax.ShapeDtypeStruct((1, 128), jnp.float32),
        ],
        in_specs=[vmem] * 6,
        out_specs=[vmem] * 2,
        compiler_params=params,
        cost_estimate=pl.CostEstimate(flops=1 << 21, bytes_accessed=3 << 20, transcendentals=0),
        name="grad_logits",
    )(g[0], *got, weight, probs)
    squares = lax.all_to_all(jnp.broadcast_to(squares, (32, 128)), ("x", "y", "c"), 0, 0, tiled=True)
    squares = jnp.sum(squares, axis=0, keepdims=True)
    squares = lax.all_to_all(jnp.broadcast_to(squares, (16, 128)), ("l", "h"), 0, 0, tiled=True)
    scale = lax.rsqrt(jnp.sum(squares) / (4096 * 6 * 4096) + 1e-06)
    logit_step = jnp.transpose(grad_logits * scale, (1, 0, 2))
    return grad_hidden, logit_step


def solution(mesh):
    fine = Mesh(mesh.devices.reshape(4, 4, 4, 4, 2), ("y", "l", "x", "h", "c"))
    dp, fsdp = ("y", "l"), ("x", "h", "c")
    return jax.shard_map(
        body,
        mesh=fine,
        in_specs=(
            P(dp, fsdp),
            P(dp, fsdp),
            P(fsdp, dp),
            P(fsdp, None, dp),
            P(fsdp, None, dp),
        ),
        out_specs=(P(dp, fsdp), P(fsdp, None, dp)),
        check_vma=False,
    )
```

time: 660 us -> 244 us (0.37)
  waiting for transfers between devices: 490 us -> 120 us
  blocking collectives: 106 us -> 0 us
  starting transfers between devices: 0.16 us -> 87.2 us
  matrix products: 23.6 us -> 7.76 us
  between operations: 14.5 us -> 1.67 us
  Pallas kernels: 0 us -> 10.4 us
    all_gather x3 -> x0, waiting for transfers between devices: 409 us -> none  [the longest x1 201 us: body(): lax.all_gather(rounded, 'dp', axis=2, tiled=True)]
    psum x1 -> x0, blocking collectives: 106 us -> none  [body(): square_sum = lax.psum(jnp.sum(grad_logits * grad_logits), ('dp', 'fsdp'))]
    reduce_scatter x1 -> x0, waiting for transfers between devices: 80.4 us -> none  [body(): lax.psum_scatter(lax.dot_general(segment, hidden, (((0,), (0,)), ((), ())...]
    all_to_all x0 -> x6, waiting for transfers between devices: none -> 80.4 us  [the longest x1 24.5 us: body(): lax.all_to_all(jnp.broadcast_to(masked_t[None], (4, 256, 512)), 'l', 0, 0)]
    all_to_all x0 -> x6, starting transfers between devices: none -> 43.6 us  [the longest x1 15.6 us: body(): lax.all_to_all(jnp.broadcast_to(upstream[None], (4, 512, 128)), 'h', 0, 0)]
    ppermute x0 -> x11, starting transfers between devices: none -> 43.6 us  [the longest x4 16.3 us: body(): lax.ppermute(up, ('y', 'x'), [(b * 4 + a, a * 4 + (b + k) % 4) for b in r...]
    ppermute x0 -> x11, waiting for transfers between devices: none -> 39.3 us  [the longest x4 23.8 us: body(): lax.ppermute(up, ('y', 'x'), [(b * 4 + a, a * 4 + (b + k) % 4) for b in r...]
    dot_general x4 -> x6, matrix products: 23.6 us -> 7.76 us  [the longest x4 5.96 us: body(): lax.dot_general(masked, order, (((0,), (0,)), ((), ())), preferred_elemen...]
  transfers between devices with their start and end apart: 4 -> 17, of which waited for: 4 -> 11; matrix products, arithmetic and copies ran while one was open for 6% -> 5% of each run, Pallas kernels for 0% -> 2%
where the time goes in v1:
time: 244 us; the launch traced here: 242 us
  waiting for transfers between devices  120 us (49%)
  starting transfers between devices  87.2 us (36%)
  Pallas kernels  10.4 us (4%)
  other arithmetic  8.05 us (3%)
  matrix products  7.76 us (3%)
  local copies, waits for them, and re-layouts  6.85 us (3%)
    all_to_all x1, waiting for transfers between devices, body(): lax.all_to_all(jnp.broadcast_to(masked_t[None], (4, 256, 512)), 'l', 0, 0)  24.5 us
    all_to_all x1, waiting for transfers between devices, body(): lax.all_to_all(jnp.broadcast_to(upstream[None], (4, 512, 128)), 'h', 0, 0)  24.5 us
    ppermute x4, waiting for transfers between devices, body(): lax.ppermute(up, ('y', 'x'), [(b * 4 + a, a * 4 + (b + k) % 4) for b in r...  23.8 us
    all_to_all x1, waiting for transfers between devices, body(): gh = lax.all_to_all(gh, 'y', 0, 0)  21.2 us
    ppermute x4, starting transfers between devices, body(): lax.ppermute(up, ('y', 'x'), [(b * 4 + a, a * 4 + (b + k) % 4) for b in r...  16.3 us
    ppermute x4, starting transfers between devices, body(): other = [lax.ppermute(u, 'c', [(0, 1), (1, 0)]) for u in own]  15.7 us
    all_to_all x1, starting transfers between devices, body(): lax.all_to_all(jnp.broadcast_to(upstream[None], (4, 512, 128)), 'h', 0, 0)  15.6 us
    ppermute x3, waiting for transfers between devices, body(): lax.ppermute(g[e], 'l', [(i, (i + e) % 4) for i in range(4)])  15.2 us
  transfers between devices with their start and end apart: 17, of which 11 were waited for; matrix products, arithmetic and copies ran while one was open for 5% of the time, Pallas kernels for 2%

profile of v1, /device:TPU:1, one launch (start us, length us, event | category | flops | bytes accessed | tf_op | source)
XLA Modules:
  0.0 241.7 jit_solution(9581775594298583063)
XLA Ops:
  0.6 0.0 copy-start
  0.6 1.8 broadcast_in_dim.11
  2.5 15.6 %all-to-all-start.1 = ((bf16[4,512,128]{2,1,0:T(8,128)(2,1)}), bf16[4,512,128]{2,1,0:T(8,128)(2,1)}, u32[]{:S(2)}, u32[]{:S(2)}) async-start(bf16[4,512,128]{2,1,0:T(8,128)(2,1)} %broadcast_in_dim.11), calls=%async_computation.1 | async-start | bytes 1048576 | tf_op jit(solution)/shard_map/all_to_all | solution.py:72
  18.1 1.5 convolution_convert_fusion
  19.6 24.5 %all-to-all-done.1 = bf16[4,512,128]{2,1,0:T(8,128)(2,1)} async-done(((bf16[4,512,128]{2,1,0:T(8,128)(2,1)}), bf16[4,512,128]{2,1,0:T(8,128)(2,1)}, u32[]{:S(2)}, u32[]{:S(2)}) %all-to-all-start.1) | async-done | bytes 524320 | tf_op jit(solution)/shard_map/all_to_all | solution.py:72
  44.1 1.5 broadcast_in_dim.12
  45.5 4.6 %all-to-all-start.3 = ((bf16[4,512,512]{2,1,0:T(8,128)(2,1)}), bf16[4,512,512]{2,1,0:T(8,128)(2,1)}, u32[]{:S(2)}, u32[]{:S(2)}) async-start(bf16[4,512,512]{2,1,0:T(8,128)(2,1)} %broadcast_in_dim.12), calls=%async_computation.3 | async-start | bytes 4194304 | tf_op jit(solution)/shard_map/all_to_all | solution.py:82
  50.1 1.7 collective-permute-start
  51.8 4.7 %collective-permute-start.1 = (bf16[4,512,128]{2,1,0:T(8,128)(2,1)}, bf16[4,512,128]{2,1,0:T(8,128)(2,1)S(1)}, u32[]{:S(2)}, u32[]{:S(2)}) collective-permute-start(bf16[4,512,128]{2,1,0:T(8,128)(2,1)} %all-to-all-done.1), channel_id=1, source_target_pairs={{0,8},{8,136},{16,264},{24,392},{128,16},{136,144},{144,272},{152,... | collective-permute-start | bytes 1572872 | tf_op jit(solution)/shard_map/ppermute | solution.py:98
  56.6 6.2 %collective-permute-start.2 = (bf16[4,512,128]{2,1,0:T(8,128)(2,1)}, bf16[4,512,128]{2,1,0:T(8,128)(2,1)S(1)}, u32[]{:S(2)}, u32[]{:S(2)}) collective-permute-start(bf16[4,512,128]{2,1,0:T(8,128)(2,1)} %all-to-all-done.1), channel_id=1, source_target_pairs={{0,16},{8,144},{16,272},{24,400},{128,24},{136,152},{144,280},{152... | collective-permute-start | bytes 1572872 | tf_op jit(solution)/shard_map/ppermute | solution.py:98
  62.7 3.8 %collective-permute-start.3 = (bf16[4,512,128]{2,1,0:T(8,128)(2,1)}, bf16[4,512,128]{2,1,0:T(8,128)(2,1)}, u32[]{:S(2)}, u32[]{:S(2)}) collective-permute-start(bf16[4,512,128]{2,1,0:T(8,128)(2,1)} %all-to-all-done.1), channel_id=1, source_target_pairs={{0,24},{8,152},{16,280},{24,408},{128,0},{136,128},{144,256},{152,... | collective-permute-start | bytes 1572872 | tf_op jit(solution)/shard_map/ppermute | solution.py:98
  66.5 0.0 copy-done.3
  66.5 1.2 bitcast_reduce_fusion
  67.8 0.0 copy-start.4
  67.8 0.0 copy-start.5
  67.8 1.4 fusion.3
  69.2 0.2 copy-done.5
  69.4 0.2 convert_convert_fusion
  69.6 0.0 copy-start.6
  69.6 0.0 collective-permute-done.a0
  69.6 4.2 %collective-permute-start.4 = (bf16[4,512,128]{2,1,0:T(8,128)(2,1)S(1)}, bf16[4,512,128]{2,1,0:T(8,128)(2,1)}, u32[]{:S(2)}, u32[]{:S(2)}) collective-permute-start(bf16[4,512,128]{2,1,0:T(8,128)(2,1)S(1)} %collective-permute-done.a0), channel_id=1, source_target_pairs={{0,1},{1,0},{2,3},{3,2},{4,5},{5,4},{6,7},{7,6},{8,9},{9,8},{10,11... | collective-permute-start | bytes 1572872 | tf_op jit(solution)/shard_map/ppermute | solution.py:101
  73.8 12.6 %collective-permute-done.1.a1 = bf16[4,512,128]{2,1,0:T(8,128)(2,1)S(1)} collective-permute-done((bf16[4,512,128]{2,1,0:T(8,128)(2,1)}, bf16[4,512,128]{2,1,0:T(8,128)(2,1)S(1)}, u32[]{:S(2)}, u32[]{:S(2)}) %collective-permute-start.1) | collective-permute-done | bytes 524320 | tf_op jit(solution)/shard_map/ppermute | solution.py:98
  86.5 3.7 %collective-permute-start.5 = (bf16[4,512,128]{2,1,0:T(8,128)(2,1)S(1)}, bf16[4,512,128]{2,1,0:T(8,128)(2,1)}, u32[]{:S(2)}, u32[]{:S(2)}) collective-permute-start(bf16[4,512,128]{2,1,0:T(8,128)(2,1)S(1)} %collective-permute-done.1.a1), channel_id=1, source_target_pairs={{0,1},{1,0},{2,3},{3,2},{4,5},{5,4},{6,7},{7,6},{8,9},{9,8},{10,11... | collective-permute-start | bytes 1572872 | tf_op jit(solution)/shard_map/ppermute | solution.py:101
  90.2 7.7 %collective-permute-done.2.a2 = bf16[4,512,128]{2,1,0:T(8,128)(2,1)S(1)} collective-permute-done((bf16[4,512,128]{2,1,0:T(8,128)(2,1)}, bf16[4,512,128]{2,1,0:T(8,128)(2,1)S(1)}, u32[]{:S(2)}, u32[]{:S(2)}) %collective-permute-start.2) | collective-permute-done | bytes 524320 | tf_op jit(solution)/shard_map/ppermute | solution.py:98
  97.9 3.9 %collective-permute-start.6 = (bf16[4,512,128]{2,1,0:T(8,128)(2,1)S(1)}, bf16[4,512,128]{2,1,0:T(8,128)(2,1)}, u32[]{:S(2)}, u32[]{:S(2)}) collective-permute-start(bf16[4,512,128]{2,1,0:T(8,128)(2,1)S(1)} %collective-permute-done.2.a2), channel_id=1, source_target_pairs={{0,1},{1,0},{2,3},{3,2},{4,5},{5,4},{6,7},{7,6},{8,9},{9,8},{10,11... | collective-permute-start | bytes 1572872 | tf_op jit(solution)/shard_map/ppermute | solution.py:101
  101.8 3.5 %collective-permute-done.3.a3 = bf16[4,512,128]{2,1,0:T(8,128)(2,1)} collective-permute-done((bf16[4,512,128]{2,1,0:T(8,128)(2,1)}, bf16[4,512,128]{2,1,0:T(8,128)(2,1)}, u32[]{:S(2)}, u32[]{:S(2)}) %collective-permute-start.3) | collective-permute-done | bytes 524320 | tf_op jit(solution)/shard_map/ppermute | solution.py:98
  105.2 3.9 %collective-permute-start.7 = (bf16[4,512,128]{2,1,0:T(8,128)(2,1)}, bf16[4,512,128]{2,1,0:T(8,128)(2,1)}, u32[]{:S(2)}, u32[]{:S(2)}) collective-permute-start(bf16[4,512,128]{2,1,0:T(8,128)(2,1)} %collective-permute-done.3.a3), channel_id=1, source_target_pairs={{0,1},{1,0},{2,3},{3,2},{4,5},{5,4},{6,7},{7,6},{8,9},{9,8},{10,11... | collective-permute-start | bytes 1572872 | tf_op jit(solution)/shard_map/ppermute | solution.py:101
  109.1 0.1 pad_add_fusion.place
  109.2 0.3 convolution_convert_fusion.1.w
  109.5 1.1 fusion.8
  110.6 0.0 all-to-all-done.3.hid
  110.6 0.0 collective-permute-done.4.b0
  110.6 0.0 collective-permute-done.5.b1
  110.6 0.0 collective-permute-done.6.b2
  110.6 0.3 collective-permute-done.7.b3
  111.0 4.7 %grad_masked.1 = (f32[512,256]{1,0:T(8,128)S(1)}, bf16[512,256]{1,0:T(8,128)(2,1)S(1)}, bf16[512,256]{1,0:T(8,128)(2,1)S(1)}, bf16[512,256]{1,0:T(8,128)(2,1)S(1)}) custom-call(s32[4]{0:T(128)S(1)} %pad_add_fusion.place, bf16[4,512,512]{2,1,0:T(8,128)(2,1)} %all-to-all-done.3.hid, bf16[4,512,128]{2,1,0:T(8,128)(2,1)S(1)} %collective-permute-done.a0, ...), custom_call_target="tpu_custom_call" | custom-call | flops 2147483648 | bytes 7340032 | tf_op jit(solution)/shard_map/grad_masked/pallas_call | solution.py:106
  115.7 3.6 %collective-permute-start.10 = (bf16[512,256]{1,0:T(8,128)(2,1)S(1)}, bf16[512,256]{1,0:T(8,128)(2,1)S(1)}, u32[]{:S(2)}, u32[]{:S(2)}) collective-permute-start(bf16[512,256]{1,0:T(8,128)(2,1)S(1)} %get-tuple-element.11), channel_id=1, source_target_pairs={{0,96},{32,0},{64,32},{96,64},{1,97},{33,1},{65,33},{97,65},{2,98}... | collective-permute-start | bytes 786440 | tf_op jit(solution)/shard_map/ppermute | solution.py:116
  119.2 4.2 %collective-permute-start.8 = (bf16[512,256]{1,0:T(8,128)(2,1)S(1)}, bf16[512,256]{1,0:T(8,128)(2,1)S(1)}, u32[]{:S(2)}, u32[]{:S(2)}) collective-permute-start(bf16[512,256]{1,0:T(8,128)(2,1)S(1)} %get-tuple-element.9), channel_id=1, source_target_pairs={{0,32},{32,64},{64,96},{96,0},{1,33},{33,65},{65,97},{97,1},{2,34}... | collective-permute-start | bytes 786440 | tf_op jit(solution)/shard_map/ppermute | solution.py:116
  123.5 3.8 %collective-permute-start.9 = (bf16[512,256]{1,0:T(8,128)(2,1)S(1)}, bf16[512,256]{1,0:T(8,128)(2,1)S(1)}, u32[]{:S(2)}, u32[]{:S(2)}) collective-permute-start(bf16[512,256]{1,0:T(8,128)(2,1)S(1)} %get-tuple-element.10), channel_id=1, source_target_pairs={{0,64},{32,96},{64,0},{96,32},{1,65},{33,97},{65,1},{97,33},{2,66}... | collective-permute-start | bytes 786440 | tf_op jit(solution)/shard_map/ppermute | solution.py:116
  127.3 1.3 convolution_add_fusion.2
  128.6 0.0 copy-start.10
  128.6 2.1 convolution_add_fusion.1
  130.7 0.0 collective-permute-done.10.g3
  130.7 4.1 %collective-permute-done.8.g1 = bf16[512,256]{1,0:T(8,128)(2,1)S(1)} collective-permute-done((bf16[512,256]{1,0:T(8,128)(2,1)S(1)}, bf16[512,256]{1,0:T(8,128)(2,1)S(1)}, u32[]{:S(2)}, u32[]{:S(2)}) %collective-permute-start.8) | collective-permute-done | bytes 262176 | tf_op jit(solution)/shard_map/ppermute | solution.py:116
  134.8 11.1 %collective-permute-done.9.g2 = bf16[512,256]{1,0:T(8,128)(2,1)S(1)} collective-permute-done((bf16[512,256]{1,0:T(8,128)(2,1)S(1)}, bf16[512,256]{1,0:T(8,128)(2,1)S(1)}, u32[]{:S(2)}, u32[]{:S(2)}) %collective-permute-start.9) | collective-permute-done | bytes 262176 | tf_op jit(solution)/shard_map/ppermute | solution.py:116
  145.9 0.4 grad_logits.1
  146.3 0.6 broadcast_in_dim.13
  146.9 9.4 %all-to-all-start.4 = ((f32[32,1,128]{2,1,0:T(1,128)}), f32[32,1,128]{2,1,0:T(1,128)S(1)}, u32[]{:S(2)}, u32[]{:S(2)}) async-start(f32[32,1,128]{2,1,0:T(1,128)} %broadcast_in_dim.13), calls=%async_computation.4 | async-start | bytes 32768 | tf_op jit(solution)/shard_map/all_to_all | solution.py:142
  156.3 1.5 fusion
  157.8 5.4 %all-to-all-done.4 = f32[32,1,128]{2,1,0:T(1,128)S(1)} async-done(((f32[32,1,128]{2,1,0:T(1,128)}), f32[32,1,128]{2,1,0:T(1,128)S(1)}, u32[]{:S(2)}, u32[]{:S(2)}) %all-to-all-start.4) | async-done | bytes 16416 | tf_op jit(solution)/shard_map/all_to_all | solution.py:142
  163.2 1.1 broadcast_in_dim.10
  164.3 3.5 %all-to-all-start = ((bf16[4,256,512]{2,1,0:T(8,128)(2,1)}), bf16[4,256,512]{2,1,0:T(8,128)(2,1)S(1)}, u32[]{:S(2)}, u32[]{:S(2)}) async-start(bf16[4,256,512]{2,1,0:T(8,128)(2,1)} %broadcast_in_dim.10), calls=%async_computation | async-start | bytes 2097152 | tf_op jit(solution)/shard_map/all_to_all | solution.py:95
  167.8 0.7 reduce_sum.41
  168.6 24.5 %all-to-all-done = bf16[4,256,512]{2,1,0:T(8,128)(2,1)S(1)} async-done(((bf16[4,256,512]{2,1,0:T(8,128)(2,1)}), bf16[4,256,512]{2,1,0:T(8,128)(2,1)S(1)}, u32[]{:S(2)}, u32[]{:S(2)}) %all-to-all-start) | async-done | bytes 1048608 | tf_op jit(solution)/shard_map/all_to_all | solution.py:95
  193.1 0.6 broadcast_in_dim.14
  193.7 6.1 %all-to-all-start.5 = ((f32[16,1,128]{2,1,0:T(1,128)}), f32[16,1,128]{2,1,0:T(1,128)S(1)}, u32[]{:S(2)}, u32[]{:S(2)}) async-start(f32[16,1,128]{2,1,0:T(1,128)} %broadcast_in_dim.14), calls=%async_computation.5 | async-start | bytes 16384 | tf_op jit(solution)/shard_map/all_to_all | solution.py:144
  199.7 1.0 copy-done.2
  200.8 5.4 %grad_hidden.1 = bf16[4,512,512]{2,1,0:T(8,128)(2,1)} custom-call(s32[4]{0:T(128)S(1)} %pad_add_fusion.place, bf16[1024,512]{1,0:T(8,128)(2,1)S(1)} %bitcast.48, bf16[4,512,128]{2,1,0:T(8,128)(2,1)S(1)} %collective-permute-done.a0, bf16[4,512,128]{2,1,0:T(8,128)(2,1)S(1)} %collective-permute-done.1.a1, bf16[4,512,128]{2,1,0:T(8,128)(2,1)S(1)} %copy-done.2, ...), custom_call_target="tpu_custom_call" | custom-call | flops 2147483648 | bytes 7340032 | tf_op jit(solution)/shard_map/grad_hidden/pallas_call | solution.py:118
  206.1 4.8 %all-to-all-done.5 = f32[16,1,128]{2,1,0:T(1,128)S(1)} async-done(((f32[16,1,128]{2,1,0:T(1,128)}), f32[16,1,128]{2,1,0:T(1,128)S(1)}, u32[]{:S(2)}, u32[]{:S(2)}) %all-to-all-start.5) | async-done | bytes 8224 | tf_op jit(solution)/shard_map/all_to_all | solution.py:144
  210.9 4.5 %all-to-all-start.2 = ((bf16[4,512,512]{2,1,0:T(8,128)(2,1)}), bf16[4,512,512]{2,1,0:T(8,128)(2,1)}, u32[]{:S(2)}, u32[]{:S(2)}) async-start(bf16[4,512,512]{2,1,0:T(8,128)(2,1)} %grad_hidden.1), calls=%async_computation.2 | async-start | bytes 4194304 | tf_op jit(solution)/shard_map/all_to_all | solution.py:127
  215.4 0.6 reduce_sum.42
  216.7 0.9 multiply_bitcast_fusion
  217.6 21.2 %all-to-all-done.2 = bf16[4,512,512]{2,1,0:T(8,128)(2,1)} async-done(((bf16[4,512,512]{2,1,0:T(8,128)(2,1)}), bf16[4,512,512]{2,1,0:T(8,128)(2,1)}, u32[]{:S(2)}, u32[]{:S(2)}) %all-to-all-start.2) | async-done | bytes 2097184 | tf_op jit(solution)/shard_map/all_to_all | solution.py:127
  238.8 2.9 %reduce_sum.40 = bf16[512,512]{1,0:T(8,128)(2,1)} reduce(bf16[4,512,512]{2,1,0:T(8,128)(2,1)} %all-to-all-done.2, bf16[]{:T(256)} %constant.31.clone.1), dimensions={0}, to_apply=%region_2.0 | reduce | flops 786432 | bytes 2621442 | tf_op jit(solution)/shard_map/reduce_sum | solution.py:128
  (22 shorter events, 0.0 us)
Async XLA Ops:
  0.6 17.5 %copy-start = (bf16[512,512]{1,0:T(8,128)(2,1)S(1)}, bf16[512,512]{1,0:T(8,128)(2,1)}, u32[]{:S(2)}) copy-start(bf16[512,512]{1,0:T(8,128)(2,1)} %param.6) | copy-start | bytes 1572868
  2.5 41.6 %all-to-all-start.1 = ((bf16[4,512,128]{2,1,0:T(8,128)(2,1)}), bf16[4,512,128]{2,1,0:T(8,128)(2,1)}, u32[]{:S(2)}, u32[]{:S(2)}) async-start(bf16[4,512,128]{2,1,0:T(8,128)(2,1)} %broadcast_in_dim.11), calls=%async_computation.1 | async-start | bytes 1048576 | tf_op jit(solution)/shard_map/all_to_all | solution.py:72
  45.5 20.9 %copy-start.3 = (f32[128,6,256]{2,0,1:T(8,128)S(1)}, f32[128,6,256]{2,0,1:T(8,128)}, u32[]{:S(2)}) copy-start(f32[128,6,256]{2,0,1:T(8,128)} %param.9) | copy-start | bytes 2359300
  45.5 65.0 %all-to-all-start.3 = ((bf16[4,512,512]{2,1,0:T(8,128)(2,1)}), bf16[4,512,512]{2,1,0:T(8,128)(2,1)}, u32[]{:S(2)}, u32[]{:S(2)}) async-start(bf16[4,512,512]{2,1,0:T(8,128)(2,1)} %broadcast_in_dim.12), calls=%async_computation.3 | async-start | bytes 4194304 | tf_op jit(solution)/shard_map/all_to_all | solution.py:82
  50.1 19.4 %collective-permute-start = (bf16[4,512,128]{2,1,0:T(8,128)(2,1)}, bf16[4,512,128]{2,1,0:T(8,128)(2,1)S(1)}, u32[]{:S(2)}, u32[]{:S(2)}) collective-permute-start(bf16[4,512,128]{2,1,0:T(8,128)(2,1)} %all-to-all-done.1), channel_id=1, source_target_pairs={{0,0},{8,128},{16,256},{24,384},{128,8},{136,136},{144,264},{152,3... | collective-permute-start | bytes 1572872 | tf_op jit(solution)/shard_map/ppermute | solution.py:98
  51.8 34.6 %collective-permute-start.1 = (bf16[4,512,128]{2,1,0:T(8,128)(2,1)}, bf16[4,512,128]{2,1,0:T(8,128)(2,1)S(1)}, u32[]{:S(2)}, u32[]{:S(2)}) collective-permute-start(bf16[4,512,128]{2,1,0:T(8,128)(2,1)} %all-to-all-done.1), channel_id=1, source_target_pairs={{0,8},{8,136},{16,264},{24,392},{128,16},{136,144},{144,272},{152,... | collective-permute-start | bytes 1572872 | tf_op jit(solution)/shard_map/ppermute | solution.py:98
  56.6 41.3 %collective-permute-start.2 = (bf16[4,512,128]{2,1,0:T(8,128)(2,1)}, bf16[4,512,128]{2,1,0:T(8,128)(2,1)S(1)}, u32[]{:S(2)}, u32[]{:S(2)}) collective-permute-start(bf16[4,512,128]{2,1,0:T(8,128)(2,1)} %all-to-all-done.1), channel_id=1, source_target_pairs={{0,16},{8,144},{16,272},{24,400},{128,24},{136,152},{144,280},{152... | collective-permute-start | bytes 1572872 | tf_op jit(solution)/shard_map/ppermute | solution.py:98
  62.7 42.5 %collective-permute-start.3 = (bf16[4,512,128]{2,1,0:T(8,128)(2,1)}, bf16[4,512,128]{2,1,0:T(8,128)(2,1)}, u32[]{:S(2)}, u32[]{:S(2)}) collective-permute-start(bf16[4,512,128]{2,1,0:T(8,128)(2,1)} %all-to-all-done.1), channel_id=1, source_target_pairs={{0,24},{8,152},{16,280},{24,408},{128,0},{136,128},{144,256},{152,... | collective-permute-start | bytes 1572872 | tf_op jit(solution)/shard_map/ppermute | solution.py:98
  67.8 1.4 copy-start.4
  67.8 1.6 copy-start.5
  69.4 39.8 %copy-start.7 = (bf16[512,512]{1,0:T(8,128)(2,1)S(1)}, bf16[512,512]{1,0:T(8,128)(2,1)}, u32[]{:S(2)}) copy-start(bf16[512,512]{1,0:T(8,128)(2,1)} %constant.34.clone) | copy-start | bytes 1572868
  69.4 39.8 %copy-start.9 = (bf16[512,256]{1,0:T(8,128)(2,1)S(1)}, bf16[512,256]{1,0:T(8,128)(2,1)}, u32[]{:S(2)}) copy-start(bf16[512,256]{1,0:T(8,128)(2,1)} %param.8) | copy-start | bytes 786436
  69.4 40.1 %copy-start.11 = (bf16[128,512]{1,0:T(8,128)(2,1)S(1)}, bf16[128,512]{1,0:T(8,128)(2,1)}, u32[]{:S(2)}) copy-start(bf16[128,512]{1,0:T(8,128)(2,1)} %constant.35) | copy-start | bytes 393220
  69.6 39.9 %copy-start.6 = (f32[6,128,256]{2,1,0:T(8,128)}, f32[6,128,256]{2,1,0:T(8,128)S(1)}, u32[]{:S(2)}) copy-start(f32[6,128,256]{2,1,0:T(8,128)S(1)} %get-tuple-element.14) | copy-start | bytes 2359300
  69.6 41.0 %collective-permute-start.4 = (bf16[4,512,128]{2,1,0:T(8,128)(2,1)S(1)}, bf16[4,512,128]{2,1,0:T(8,128)(2,1)}, u32[]{:S(2)}, u32[]{:S(2)}) collective-permute-start(bf16[4,512,128]{2,1,0:T(8,128)(2,1)S(1)} %collective-permute-done.a0), channel_id=1, source_target_pairs={{0,1},{1,0},{2,3},{3,2},{4,5},{5,4},{6,7},{7,6},{8,9},{9,8},{10,11... | collective-permute-start | bytes 1572872 | tf_op jit(solution)/shard_map/ppermute | solution.py:101
  86.5 24.1 %collective-permute-start.5 = (bf16[4,512,128]{2,1,0:T(8,128)(2,1)S(1)}, bf16[4,512,128]{2,1,0:T(8,128)(2,1)}, u32[]{:S(2)}, u32[]{:S(2)}) collective-permute-start(bf16[4,512,128]{2,1,0:T(8,128)(2,1)S(1)} %collective-permute-done.1.a1), channel_id=1, source_target_pairs={{0,1},{1,0},{2,3},{3,2},{4,5},{5,4},{6,7},{7,6},{8,9},{9,8},{10,11... | collective-permute-start | bytes 1572872 | tf_op jit(solution)/shard_map/ppermute | solution.py:101
  97.9 17.8 %copy-start.1 = (bf16[4,512,128]{2,1,0:T(8,128)(2,1)}, bf16[4,512,128]{2,1,0:T(8,128)(2,1)S(1)}, u32[]{:S(2)}) copy-start(bf16[4,512,128]{2,1,0:T(8,128)(2,1)S(1)} %collective-permute-done.2.a2) | copy-start | bytes 1572868
  97.9 12.7 %collective-permute-start.6 = (bf16[4,512,128]{2,1,0:T(8,128)(2,1)S(1)}, bf16[4,512,128]{2,1,0:T(8,128)(2,1)}, u32[]{:S(2)}, u32[]{:S(2)}) collective-permute-start(bf16[4,512,128]{2,1,0:T(8,128)(2,1)S(1)} %collective-permute-done.2.a2), channel_id=1, source_target_pairs={{0,1},{1,0},{2,3},{3,2},{4,5},{5,4},{6,7},{7,6},{8,9},{9,8},{10,11... | collective-permute-start | bytes 1572872 | tf_op jit(solution)/shard_map/ppermute | solution.py:101
  105.2 5.7 %collective-permute-start.7 = (bf16[4,512,128]{2,1,0:T(8,128)(2,1)}, bf16[4,512,128]{2,1,0:T(8,128)(2,1)}, u32[]{:S(2)}, u32[]{:S(2)}) collective-permute-start(bf16[4,512,128]{2,1,0:T(8,128)(2,1)} %collective-permute-done.3.a3), channel_id=1, source_target_pairs={{0,1},{1,0},{2,3},{3,2},{4,5},{5,4},{6,7},{7,6},{8,9},{9,8},{10,11... | collective-permute-start | bytes 1572872 | tf_op jit(solution)/shard_map/ppermute | solution.py:101
  110.6 16.7 %copy-start.13 = (bf16[128,512]{1,0:T(8,128)(2,1)S(1)}, bf16[128,512]{1,0:T(8,128)(2,1)}, u32[]{:S(2)}) copy-start(bf16[128,512]{1,0:T(8,128)(2,1)} %constant.36) | copy-start | bytes 393220
  110.6 16.7 %copy-start.8 = (f32[256,512]{1,0:T(8,128)S(1)}, f32[256,512]{1,0:T(8,128)}, u32[]{:S(2)}) copy-start(f32[256,512]{1,0:T(8,128)} %fusion.8) | copy-start | bytes 1572868
  110.6 18.0 %copy-start.12 = (bf16[128,512]{1,0:T(8,128)(2,1)S(1)}, bf16[128,512]{1,0:T(8,128)(2,1)}, u32[]{:S(2)}) copy-start(bf16[128,512]{1,0:T(8,128)(2,1)} %constant.37) | copy-start | bytes 393220
  115.7 15.1 %collective-permute-start.10 = (bf16[512,256]{1,0:T(8,128)(2,1)S(1)}, bf16[512,256]{1,0:T(8,128)(2,1)S(1)}, u32[]{:S(2)}, u32[]{:S(2)}) collective-permute-start(bf16[512,256]{1,0:T(8,128)(2,1)S(1)} %get-tuple-element.11), channel_id=1, source_target_pairs={{0,96},{32,0},{64,32},{96,64},{1,97},{33,1},{65,33},{97,65},{2,98}... | collective-permute-start | bytes 786440 | tf_op jit(solution)/shard_map/ppermute | solution.py:116
  119.2 15.6 %collective-permute-start.8 = (bf16[512,256]{1,0:T(8,128)(2,1)S(1)}, bf16[512,256]{1,0:T(8,128)(2,1)S(1)}, u32[]{:S(2)}, u32[]{:S(2)}) collective-permute-start(bf16[512,256]{1,0:T(8,128)(2,1)S(1)} %get-tuple-element.9), channel_id=1, source_target_pairs={{0,32},{32,64},{64,96},{96,0},{1,33},{33,65},{65,97},{97,1},{2,34}... | collective-permute-start | bytes 786440 | tf_op jit(solution)/shard_map/ppermute | solution.py:116
  123.5 22.4 %collective-permute-start.9 = (bf16[512,256]{1,0:T(8,128)(2,1)S(1)}, bf16[512,256]{1,0:T(8,128)(2,1)S(1)}, u32[]{:S(2)}, u32[]{:S(2)}) collective-permute-start(bf16[512,256]{1,0:T(8,128)(2,1)S(1)} %get-tuple-element.10), channel_id=1, source_target_pairs={{0,64},{32,96},{64,0},{96,32},{1,65},{33,97},{65,1},{97,33},{2,66}... | collective-permute-start | bytes 786440 | tf_op jit(solution)/shard_map/ppermute | solution.py:116
  128.6 27.7 %copy-start.10 = (bf16[128,512]{1,0:T(8,128)(2,1)S(1)}, bf16[128,512]{1,0:T(8,128)(2,1)}, u32[]{:S(2)}) copy-start(bf16[128,512]{1,0:T(8,128)(2,1)} %constant.38) | copy-start | bytes 393220
  146.9 16.3 %all-to-all-start.4 = ((f32[32,1,128]{2,1,0:T(1,128)}), f32[32,1,128]{2,1,0:T(1,128)S(1)}, u32[]{:S(2)}, u32[]{:S(2)}) async-start(f32[32,1,128]{2,1,0:T(1,128)} %broadcast_in_dim.13), calls=%async_computation.4 | async-start | bytes 32768 | tf_op jit(solution)/shard_map/all_to_all | solution.py:142
  163.2 1.1 copy-start.14
  164.3 28.8 %all-to-all-start = ((bf16[4,256,512]{2,1,0:T(8,128)(2,1)}), bf16[4,256,512]{2,1,0:T(8,128)(2,1)S(1)}, u32[]{:S(2)}, u32[]{:S(2)}) async-start(bf16[4,256,512]{2,1,0:T(8,128)(2,1)} %broadcast_in_dim.10), calls=%async_computation | async-start | bytes 2097152 | tf_op jit(solution)/shard_map/all_to_all | solution.py:95
  193.7 17.2 %all-to-all-start.5 = ((f32[16,1,128]{2,1,0:T(1,128)}), f32[16,1,128]{2,1,0:T(1,128)S(1)}, u32[]{:S(2)}, u32[]{:S(2)}) async-start(f32[16,1,128]{2,1,0:T(1,128)} %broadcast_in_dim.14), calls=%async_computation.5 | async-start | bytes 16384 | tf_op jit(solution)/shard_map/all_to_all | solution.py:144
  199.7 1.0 copy-start.2
  210.9 27.9 %all-to-all-start.2 = ((bf16[4,512,512]{2,1,0:T(8,128)(2,1)}), bf16[4,512,512]{2,1,0:T(8,128)(2,1)}, u32[]{:S(2)}, u32[]{:S(2)}) async-start(bf16[4,512,512]{2,1,0:T(8,128)(2,1)} %grad_hidden.1), calls=%async_computation.2 | async-start | bytes 4194304 | tf_op jit(solution)/shard_map/all_to_all | solution.py:127

commit v2 on v1

v2 whole, which is shorter than its diff:
```python
import jax
import jax.numpy as jnp
import numpy as np
from jax import lax
from jax.experimental import pallas as pl
from jax.experimental.pallas import tpu as pltpu
from jax.sharding import Mesh, PartitionSpec as P

PAIRS = ((0, 1), (0, 2), (0, 3), (1, 2), (1, 3), (2, 3))
TEMPER = 2.0
VMEM = 60 * 1024 * 1024


def stack_kernel(r0, r1, r2, r3, out):
    for d, piece in enumerate((r0, r1, r2, r3)):
        out[d] = piece[...]


def grad_masked_kernel(
    place, hid, a0, a1, a2, a3, b0, b1, b2, b3, o0, o1, o2, o3
):
    l, x, c, y, h = (place[i] for i in range(5))
    own, other = (a0, a1, a2, a3), (b0, b1, b2, b3)
    for e, out in enumerate((o0, o1, o2, o3)):
        col = lax.rem(h + 8 - l - e, 4)
        total = None
        for k in range(4):
            tok = lax.rem(x + 4 - k, 4)
            mine, theirs = own[k][col], other[k][col]
            first = jnp.where(c == 0, mine, theirs)
            second = jnp.where(c == 0, theirs, mine)
            part = jnp.dot(
                hid[tok], jnp.concatenate([first, second], axis=1), preferred_element_type=jnp.float32
            )
            total = part if total is None else total + part
        out[...] = total.astype(out.dtype)


def grad_hidden_kernel(place, m, a0, a1, a2, a3, b0, b1, b2, b3, ahead, out, mt):
    del ahead
    x, c, h = place[1], place[2], place[4]
    own, other = (a0, a1, a2, a3), (b0, b1, b2, b3)
    for d in range(4):
        mt[256 * d : 256 * d + 256, :] = m[lax.rem(h + 4 - d, 4)]
    for k in range(4):
        tok = lax.rem(x + 4 - k, 4)
        pieces = []
        for d in range(4):
            mine, theirs = own[k][d], other[k][d]
            pieces += [jnp.where(c == 0, mine, theirs), jnp.where(c == 0, theirs, mine)]
        out[tok] = jnp.dot(
            jnp.concatenate(pieces, axis=1), mt[...], preferred_element_type=jnp.float32
        ).astype(out.dtype)


def grad_logits_kernel(g0, g1, g2, g3, w, probs, ahead, out, squares):
    del ahead
    prod = []
    for j in range(4):
        rows = pl.ds(128 * j, 128)
        total = (
            g0[rows, :]
            + g1[rows, :].astype(jnp.float32)
            + g2[rows, :].astype(jnp.float32)
            + g3[rows, :].astype(jnp.float32)
        )
        prod.append(total * w[rows, :].astype(jnp.float32))
    grads = [prod[a] + prod[b] for a, b in PAIRS]
    mean = sum(probs[k] * grads[k] for k in range(6))
    sums = jnp.zeros((128, 256), jnp.float32)
    for k in range(6):
        value = probs[k] * (grads[k] - mean) * (1.0 / TEMPER)
        out[k] = value
        sums = sums + value * value
    sums = jnp.sum(sums, axis=0, keepdims=True)
    squares[...] = jnp.broadcast_to(sums[:, :128] + sums[:, 128:], squares.shape)


def shift(value, axis, by):
    return lax.ppermute(value, axis, [(i, (i + by) % 4) for i in range(4)])


def whole(*shape):
    return pl.BlockSpec(shape, lambda i: (0,) * len(shape))


def body(hidden, upstream, down_weight, mask_logits, gumbel_noise):
    y, l, x, h, c = (lax.axis_index(a) for a in ("y", "l", "x", "h", "c"))
    place = jnp.stack([l, x, c, y, h]).astype(jnp.int32)

    with jax.named_scope("up"):
        up = [upstream] + [shift(upstream, "h", d) for d in (1, 2, 3)]
    up = pl.pallas_call(
        stack_kernel,
        out_shape=jax.ShapeDtypeStruct((4, 512, 128), jnp.bfloat16),
        grid=(1,),
        in_specs=[whole(512, 128)] * 4,
        out_specs=whole(4, 512, 128),
        cost_estimate=pl.CostEstimate(flops=10**12, bytes_accessed=1 << 30, transcendentals=0),
        name="stack_upstream",
    )(*up)

    order = np.zeros((512, 512), np.float32)
    for j in range(4):
        for g in range(128):
            order[j * 128 + g, 4 * g + j] = 1.0
    order = jnp.asarray(order, jnp.bfloat16)
    hid_t = lax.dot_general(
        order, hidden, (((1,), (1,)), ((), ())), preferred_element_type=jnp.float32
    ).astype(jnp.bfloat16)
    with jax.named_scope("hidden"):
        hid_all = lax.all_gather(hid_t, "y")

    weight = jnp.dot(order, down_weight, preferred_element_type=jnp.float32).astype(jnp.bfloat16)
    logits = jnp.transpose(mask_logits, (1, 0, 2)) + jnp.transpose(gumbel_noise, (1, 0, 2))
    probs = jax.nn.softmax(logits / TEMPER, axis=0)
    rounded = probs.astype(jnp.bfloat16).astype(jnp.float32)
    keep = [sum(rounded[k] for k in range(6) if j in PAIRS[k]) for j in range(4)]
    masked = jnp.concatenate(
        [(weight[128 * j : 128 * j + 128].astype(jnp.float32) * keep[j]).astype(jnp.bfloat16) for j in range(4)]
    )
    masked_t = lax.dot_general(
        masked, order, (((0,), (0,)), ((), ())), preferred_element_type=jnp.float32
    ).astype(jnp.bfloat16)
    with jax.named_scope("masked"):
        mt = lax.all_gather(masked_t, "l")

    with jax.named_scope("upstream_xy"):
        own = [
            lax.ppermute(up, ("y", "x"), [(b * 4 + a, a * 4 + (b + k) % 4) for b in range(4) for a in range(4)])
            for k in range(4)
        ]
    with jax.named_scope("upstream_core"):
        other = [lax.ppermute(u, "c", [(0, 1), (1, 0)]) for u in own]

    smem = pl.BlockSpec(memory_space=pltpu.SMEM)
    tall, block = whole(512, 512), whole(4, 512, 128)
    params = pltpu.CompilerParams(vmem_limit_bytes=VMEM)
    g = pl.pallas_call(
        grad_masked_kernel,
        out_shape=[jax.ShapeDtypeStruct((512, 256), jnp.float32)]
        + [jax.ShapeDtypeStruct((512, 256), jnp.bfloat16)] * 3,
        grid=(1,),
        in_specs=[smem, whole(4, 512, 512)] + [block] * 8,
        out_specs=[whole(512, 256)] * 4,
        compiler_params=params,
        cost_estimate=pl.CostEstimate(flops=2 * 512 * 2048 * 1024, bytes_accessed=7 << 20, transcendentals=0),
        name="grad_masked",
    )(place, hid_all, *own, *other)
    with jax.named_scope("grad_masked_sum"):
        got = [shift(g[e], "l", e) for e in (1, 2, 3)]

    gh = pl.pallas_call(
        grad_hidden_kernel,
        out_shape=jax.ShapeDtypeStruct((4, 512, 512), jnp.bfloat16),
        grid=(1,),
        in_specs=[smem, whole(4, 256, 512)] + [block] * 8 + [pl.BlockSpec(memory_space=pl.ANY)],
        out_specs=whole(4, 512, 512),
        scratch_shapes=[pltpu.VMEM((1024, 512), jnp.bfloat16)],
        compiler_params=params,
        cost_estimate=pl.CostEstimate(flops=2 * 512 * 2048 * 1024, bytes_accessed=7 << 20, transcendentals=0),
        name="grad_hidden",
    )(place, mt, *own, *other, g[0])
    with jax.named_scope("grad_hidden_sum"):
        grad_hidden = lax.psum_scatter(gh.reshape(2048, 512), "y", scatter_dimension=0, tiled=True)

    grad_logits, squares = pl.pallas_call(
        grad_logits_kernel,
        out_shape=[
            jax.ShapeDtypeStruct((6, 128, 256), jnp.float32),
            jax.ShapeDtypeStruct((16, 128), jnp.float32),
        ],
        grid=(1,),
        in_specs=[whole(512, 256)] * 5 + [whole(6, 128, 256), pl.BlockSpec(memory_space=pl.ANY)],
        out_specs=[whole(6, 128, 256), whole(16, 128)],
        compiler_params=params,
        cost_estimate=pl.CostEstimate(flops=10**12, bytes_accessed=1 << 30, transcendentals=0),
        name="grad_logits",
    )(g[0], *got, weight, probs, g[0])
    with jax.named_scope("mean_square"):
        squares = lax.all_to_all(squares, ("l", "h"), 0, 0, tiled=True)
        squares = jnp.broadcast_to(jnp.sum(squares, axis=0, keepdims=True), (32, 128))
        squares = lax.all_to_all(squares, ("x", "y", "c"), 0, 0, tiled=True)
    scale = lax.rsqrt(jnp.sum(squares) / (4096 * 6 * 4096) + 1e-06)
    logit_step = jnp.transpose(grad_logits * scale, (1, 0, 2))
    return grad_hidden, logit_step


def solution(mesh):
    fine = Mesh(mesh.devices.reshape(4, 4, 4, 4, 2), ("y", "l", "x", "h", "c"))
    dp, fsdp = ("y", "l"), ("x", "h", "c")
    return jax.shard_map(
        body,
        mesh=fine,
        in_specs=(
            P(dp, fsdp),
            P(dp, fsdp),
            P(fsdp, dp),
            P(fsdp, None, dp),
            P(fsdp, None, dp),
        ),
        out_specs=(P(dp, fsdp), P(fsdp, None, dp)),
        check_vma=False,
    )
```

time: 244 us -> 192 us (0.79)
  waiting for transfers between devices: 120 us -> 43.6 us
  blocking collectives: 0 us -> 45.6 us
  starting transfers between devices: 87.2 us -> 58.2 us
  between operations: 1.67 us -> 14.8 us
  Pallas kernels: 10.4 us -> 17.1 us
  other arithmetic: 8.05 us -> 4.05 us
  local copies, waits for them, and re-layouts: 6.85 us -> 3.29 us
  matrix products: 7.76 us -> 4.32 us
    all_to_all x6 -> x0, waiting for transfers between devices: 80.4 us -> none  [the longest x1 24.5 us: body(): lax.all_to_all(jnp.broadcast_to(masked_t[None], (4, 256, 512)), 'l', 0, 0)]
    all_to_all x0 -> x2, blocking collectives: none -> 45.6 us  [the longest x1 28.9 us: body(): squares = lax.all_to_all(squares, ('l', 'h'), 0, 0, tiled=True)]
    all_to_all x6 -> x0, starting transfers between devices: 43.6 us -> none  [the longest x1 15.6 us: body(): lax.all_to_all(jnp.broadcast_to(upstream[None], (4, 512, 128)), 'h', 0, 0)]
    ppermute x3 -> x6, starting transfers between devices: 11.6 us -> 34.6 us  [shift(): return lax.ppermute(value, axis, [(i, (i + by) % 4) for i in range(4)])]
    all_gather x0 -> x2, waiting for transfers between devices: none -> 15.2 us  [the longest x1 15.2 us: body(): mt = lax.all_gather(masked_t, 'l')]
    ppermute x4, waiting for transfers between devices: 23.8 us -> 14.1 us  [body(): lax.ppermute(up, ('y', 'x'), [(b * 4 + a, a * 4 + (b + k) % 4) for b in r...]
    ppermute x4, starting transfers between devices: 15.7 us -> 9.78 us  [body(): other = [lax.ppermute(u, 'c', [(0, 1), (1, 0)]) for u in own]]
    broadcast_in_dim x5 -> x1, local copies, waits for them, and re-layouts: 5.6 us -> 0.01 us  [body(): jnp.broadcast_to(jnp.sum(squares, axis=0, keepdims=True), (32, 128))]
  transfers between devices with their start and end apart: 17 -> 17, of which waited for: 11 -> 6; matrix products, arithmetic and copies ran while one was open for 5% -> 4% of each run, Pallas kernels for 2% -> 9%
where the time goes in v2:
time: 192 us; the launch traced here: 191 us
  starting transfers between devices  58.2 us (30%)
  blocking collectives  45.6 us (24%)
  waiting for transfers between devices  43.6 us (23%)
  Pallas kernels  17.1 us (9%)
  between operations  14.8 us (8%)
  matrix products  4.32 us (2%)
  other arithmetic  4.05 us (2%)
  local copies, waits for them, and re-layouts  3.29 us (2%)
    ppermute x6, starting transfers between devices, shift(): return lax.ppermute(value, axis, [(i, (i + by) % 4) for i in range(4)])  34.6 us
    all_to_all x1, blocking collectives, body(): squares = lax.all_to_all(squares, ('l', 'h'), 0, 0, tiled=True)  28.9 us
    all_to_all x1, blocking collectives, body(): squares = lax.all_to_all(squares, ('x', 'y', 'c'), 0, 0, tiled=True)  16.7 us
    all_gather x1, waiting for transfers between devices, body(): mt = lax.all_gather(masked_t, 'l')  15.2 us
    ppermute x4, waiting for transfers between devices, body(): lax.ppermute(up, ('y', 'x'), [(b * 4 + a, a * 4 + (b + k) % 4) for b in r...  14.1 us
    ppermute x4, starting transfers between devices, body(): lax.ppermute(up, ('y', 'x'), [(b * 4 + a, a * 4 + (b + k) % 4) for b in r...  13.7 us
    ppermute x6, waiting for transfers between devices, shift(): return lax.ppermute(value, axis, [(i, (i + by) % 4) for i in range(4)])  12.9 us
    ppermute x4, starting transfers between devices, body(): other = [lax.ppermute(u, 'c', [(0, 1), (1, 0)]) for u in own]  9.78 us
  transfers between devices with their start and end apart: 17, of which 6 were waited for; matrix products, arithmetic and copies ran while one was open for 4% of the time, Pallas kernels for 9%

profile of v2, /device:TPU:1, one launch (start us, length us, event | category | flops | bytes accessed | tf_op | source)
XLA Modules:
  0.0 191.0 jit_solution(12748785926509871389)
XLA Ops:
  7.2 0.0 copy-start
  7.2 0.0 copy-start.18
  7.2 0.0 all-gather.7.cloned.1.call-start
  7.3 1.0 copy-done
  8.2 2.3 %convolution_convert_fusion = bf16[512,512]{1,0:T(8,128)(2,1)} fusion(bf16[512,512]{1,0:T(8,128)(2,1)} %constant.34.clone, bf16[512,512]{1,0:T(8,128)(2,1)S(1)} %copy-done), kind=kOutput, calls=%fused_computation | convolution fusion | flops 268697600 | bytes 1572864 | tf_op jit(solution)/shard_map/dot_general | solution.py:108
  10.5 0.0 all-gather.7.cloned.1.call-update
  10.6 0.0 all-gather.5.cloned.1.call-start
  10.6 16.4 %collective-permute-start.1 = (bf16[512,128]{1,0:T(8,128)(2,1)S(1)}, bf16[512,128]{1,0:T(8,128)(2,1)S(1)}, u32[]{:S(2)}, u32[]{:S(2)}) collective-permute-start(bf16[512,128]{1,0:T(8,128)(2,1)S(1)} %copy-done.18), channel_id=1, source_target_pairs={{0,4},{2,6},{4,0},{6,2},{1,5},{3,7},{5,1},{7,3},{8,12},{10,14},{12... | collective-permute-start | bytes 393224 | tf_op jit(solution)/shard_map/up/ppermute | solution.py:80
  27.0 4.0 %collective-permute-start = (bf16[512,128]{1,0:T(8,128)(2,1)S(1)}, bf16[512,128]{1,0:T(8,128)(2,1)S(1)}, u32[]{:S(2)}, u32[]{:S(2)}) collective-permute-start(bf16[512,128]{1,0:T(8,128)(2,1)S(1)} %copy-done.18), channel_id=1, source_target_pairs={{0,2},{2,4},{4,6},{6,0},{1,3},{3,5},{5,7},{7,1},{8,10},{10,12},{12... | collective-permute-start | bytes 393224 | tf_op jit(solution)/shard_map/up/ppermute | solution.py:80
  31.0 5.2 %collective-permute-start.2 = (bf16[512,128]{1,0:T(8,128)(2,1)S(1)}, bf16[512,128]{1,0:T(8,128)(2,1)S(1)}, u32[]{:S(2)}, u32[]{:S(2)}) collective-permute-start(bf16[512,128]{1,0:T(8,128)(2,1)S(1)} %copy-done.18), channel_id=1, source_target_pairs={{0,6},{2,0},{4,2},{6,4},{1,7},{3,1},{5,3},{7,5},{8,14},{10,8},{12,... | collective-permute-start | bytes 393224 | tf_op jit(solution)/shard_map/up/ppermute | solution.py:80
  36.2 0.1 bitcast_reduce_fusion
  36.4 0.2 fusion.3
  36.5 0.0 copy-start.7
  36.6 0.3 convolution_convert_fusion.1.w
  36.9 0.0 copy-start.9
  36.9 0.0 copy-start.8
  36.9 1.0 convert_convert_fusion
  37.9 0.2 fusion.8
  38.2 0.3 convolution_add_fusion.2
  38.5 0.3 convolution_add_fusion.1
  38.7 0.1 copy-done.6
  38.9 1.0 fusion
  39.8 0.0 all-gather.5.cloned.1.call-update
  39.8 0.0 reduce-scatter.2.cloned.1.call-start
  39.9 0.0 collective-permute-done.1.r2
  39.9 0.0 collective-permute-done.r1
  39.9 11.2 %collective-permute-done.2.r3 = bf16[512,128]{1,0:T(8,128)(2,1)S(1)} collective-permute-done((bf16[512,128]{1,0:T(8,128)(2,1)S(1)}, bf16[512,128]{1,0:T(8,128)(2,1)S(1)}, u32[]{:S(2)}, u32[]{:S(2)}) %collective-permute-start.2) | collective-permute-done | bytes 131104 | tf_op jit(solution)/shard_map/up/ppermute | solution.py:80
  51.1 0.6 copy-done.21
  51.8 1.9 %stack_upstream.1 = bf16[4,512,128]{2,1,0:T(8,128)(2,1)} custom-call(bf16[512,128]{1,0:T(8,128)(2,1)} %r0.1, bf16[512,128]{1,0:T(8,128)(2,1)} %copy-done.20, bf16[512,128]{1,0:T(8,128)(2,1)} %copy-done.19, bf16[512,128]{1,0:T(8,128)(2,1)} %copy-done.21), custom_call_target="tpu_custom_call" | custom-call | flops 999999995904 | bytes 1073741824 | tf_op jit(solution)/shard_map/stack_upstream/pallas_call | solution.py:93
  53.7 4.4 %collective-permute-start.6 = (bf16[4,512,128]{2,1,0:T(8,128)(2,1)}, bf16[4,512,128]{2,1,0:T(8,128)(2,1)S(1)}, u32[]{:S(2)}, u32[]{:S(2)}) collective-permute-start(bf16[4,512,128]{2,1,0:T(8,128)(2,1)} %stack_upstream.1), channel_id=1, source_target_pairs={{0,24},{8,152},{16,280},{24,408},{128,0},{136,128},{144,256},{152,... | collective-permute-start | bytes 1572872 | tf_op jit(solution)/shard_map/upstream_xy/ppermute | solution.py:130
  58.1 5.7 %collective-permute-start.5 = (bf16[4,512,128]{2,1,0:T(8,128)(2,1)}, bf16[4,512,128]{2,1,0:T(8,128)(2,1)S(1)}, u32[]{:S(2)}, u32[]{:S(2)}) collective-permute-start(bf16[4,512,128]{2,1,0:T(8,128)(2,1)} %stack_upstream.1), channel_id=1, source_target_pairs={{0,16},{8,144},{16,272},{24,400},{128,24},{136,152},{144,280},{152... | collective-permute-start | bytes 1572872 | tf_op jit(solution)/shard_map/upstream_xy/ppermute | solution.py:130
  63.8 1.9 %collective-permute-start.4 = (bf16[4,512,128]{2,1,0:T(8,128)(2,1)}, bf16[4,512,128]{2,1,0:T(8,128)(2,1)S(1)}, u32[]{:S(2)}, u32[]{:S(2)}) collective-permute-start(bf16[4,512,128]{2,1,0:T(8,128)(2,1)} %stack_upstream.1), channel_id=1, source_target_pairs={{0,8},{8,136},{16,264},{24,392},{128,16},{136,144},{144,272},{152,... | collective-permute-start | bytes 1572872 | tf_op jit(solution)/shard_map/upstream_xy/ppermute | solution.py:130
  65.7 1.7 collective-permute-start.3
  67.4 12.8 %collective-permute-done.6.a3 = bf16[4,512,128]{2,1,0:T(8,128)(2,1)S(1)} collective-permute-done((bf16[4,512,128]{2,1,0:T(8,128)(2,1)}, bf16[4,512,128]{2,1,0:T(8,128)(2,1)S(1)}, u32[]{:S(2)}, u32[]{:S(2)}) %collective-permute-start.6) | collective-permute-done | bytes 524320 | tf_op jit(solution)/shard_map/upstream_xy/ppermute | solution.py:130
  80.2 3.4 %collective-permute-start.10 = (bf16[4,512,128]{2,1,0:T(8,128)(2,1)S(1)}, bf16[4,512,128]{2,1,0:T(8,128)(2,1)S(1)}, u32[]{:S(2)}, u32[]{:S(2)}) collective-permute-start(bf16[4,512,128]{2,1,0:T(8,128)(2,1)S(1)} %collective-permute-done.6.a3), channel_id=1, source_target_pairs={{0,1},{1,0},{2,3},{3,2},{4,5},{5,4},{6,7},{7,6},{8,9},{9,8},{10,11... | collective-permute-start | bytes 1572872 | tf_op jit(solution)/shard_map/upstream_core/ppermute | solution.py:134
  83.6 0.0 collective-permute-done.5.a2
  83.7 1.9 %collective-permute-start.9 = (bf16[4,512,128]{2,1,0:T(8,128)(2,1)S(1)}, bf16[4,512,128]{2,1,0:T(8,128)(2,1)}, u32[]{:S(2)}, u32[]{:S(2)}) collective-permute-start(bf16[4,512,128]{2,1,0:T(8,128)(2,1)S(1)} %collective-permute-done.5.a2), channel_id=1, source_target_pairs={{0,1},{1,0},{2,3},{3,2},{4,5},{5,4},{6,7},{7,6},{8,9},{9,8},{10,11... | collective-permute-start | bytes 1572872 | tf_op jit(solution)/shard_map/upstream_core/ppermute | solution.py:134
  85.6 1.3 collective-permute-done.4.a1
  86.9 2.5 %collective-permute-start.8 = (bf16[4,512,128]{2,1,0:T(8,128)(2,1)S(1)}, bf16[4,512,128]{2,1,0:T(8,128)(2,1)}, u32[]{:S(2)}, u32[]{:S(2)}) collective-permute-start(bf16[4,512,128]{2,1,0:T(8,128)(2,1)S(1)} %collective-permute-done.4.a1), channel_id=1, source_target_pairs={{0,1},{1,0},{2,3},{3,2},{4,5},{5,4},{6,7},{7,6},{8,9},{9,8},{10,11... | collective-permute-start | bytes 1572872 | tf_op jit(solution)/shard_map/upstream_core/ppermute | solution.py:134
  89.4 0.0 collective-permute-done.3.a0
  89.4 0.0 copy-start.13
  89.4 1.9 %collective-permute-start.7 = (bf16[4,512,128]{2,1,0:T(8,128)(2,1)S(1)}, bf16[4,512,128]{2,1,0:T(8,128)(2,1)}, u32[]{:S(2)}, u32[]{:S(2)}) collective-permute-start(bf16[4,512,128]{2,1,0:T(8,128)(2,1)S(1)} %collective-permute-done.3.a0), channel_id=1, source_target_pairs={{0,1},{1,0},{2,3},{3,2},{4,5},{5,4},{6,7},{7,6},{8,9},{9,8},{10,11... | collective-permute-start | bytes 1572872 | tf_op jit(solution)/shard_map/upstream_core/ppermute | solution.py:134
  91.4 0.7 stack.23.place
  92.0 0.0 collective-permute-done.10.b3
  92.1 0.0 collective-permute-done.9.b2
  92.1 0.0 collective-permute-done.8.b1
  92.1 1.3 collective-permute-done.7.b0
  93.4 6.1 %grad_masked.1 = (f32[512,256]{1,0:T(8,128)}, bf16[512,256]{1,0:T(8,128)(2,1)}, bf16[512,256]{1,0:T(8,128)(2,1)}, bf16[512,256]{1,0:T(8,128)(2,1)}) custom-call(s32[5]{0:T(128)} %stack.23.place, bf16[4,512,512]{2,1,0:T(8,128)(2,1)} %bitcast.55, bf16[4,512,128]{2,1,0:T(8,128)(2,1)} %copy-done.13, bf16[4,512,128]{2,1,0:T(8,128)(2,1)} %copy-done.12, ...), custom_call_target="tpu_custom_call" | custom-call | flops 2147483648 | bytes 7340032 | tf_op jit(solution)/shard_map/grad_masked/pallas_call | solution.py:139
  99.5 1.9 collective-permute-start.11
  101.5 3.9 %collective-permute-start.12 = (bf16[512,256]{1,0:T(8,128)(2,1)}, bf16[512,256]{1,0:T(8,128)(2,1)S(1)}, u32[]{:S(2)}, u32[]{:S(2)}) collective-permute-start(bf16[512,256]{1,0:T(8,128)(2,1)} %get-tuple-element.10), channel_id=1, source_target_pairs={{0,64},{32,96},{64,0},{96,32},{1,65},{33,97},{65,1},{97,33},{2,66}... | collective-permute-start | bytes 786440 | tf_op jit(solution)/shard_map/grad_masked_sum/ppermute | solution.py:80
  105.4 3.2 %collective-permute-start.13 = (bf16[512,256]{1,0:T(8,128)(2,1)}, bf16[512,256]{1,0:T(8,128)(2,1)S(1)}, u32[]{:S(2)}, u32[]{:S(2)}) collective-permute-start(bf16[512,256]{1,0:T(8,128)(2,1)} %get-tuple-element.11), channel_id=1, source_target_pairs={{0,96},{32,0},{64,32},{96,64},{1,97},{33,1},{65,33},{97,65},{2,98}... | collective-permute-start | bytes 786440 | tf_op jit(solution)/shard_map/grad_masked_sum/ppermute | solution.py:80
  108.6 15.2 %all-gather.5.cloned.1.call-done = bf16[1024,512]{1,0:T(8,128)(2,1)} async-done(((bf16[256,512]{1,0:T(8,128)(2,1)}), bf16[1024,512]{1,0:T(8,128)(2,1)}) %all-gather.5.cloned.1.call-update) | async-done | bytes 1048592 | tf_op jit(solution)/shard_map/masked/all_gather | solution.py:126
  123.8 6.2 %grad_hidden.1 = bf16[4,512,512]{2,1,0:T(8,128)(2,1)} custom-call(s32[5]{0:T(128)} %stack.23.place, bf16[4,256,512]{2,1,0:T(8,128)(2,1)} %bitcast.56, bf16[4,512,128]{2,1,0:T(8,128)(2,1)} %copy-done.13, bf16[4,512,128]{2,1,0:T(8,128)(2,1)} %copy-done.12, bf16[4,512,128]{2,1,0:T(8,128)(2,1)} %copy-done.11, bf16[4,512,128]{2,1,0:T(8,128)(2,1)} %copy-done.10, ...), custom_call_target="tpu_custom_call" | custom-call | flops 2147483648 | bytes 7340032 | tf_op jit(solution)/shard_map/grad_hidden/pallas_call | solution.py:153
  130.0 0.0 reduce-scatter.2.cloned.1.call-update
  130.0 0.0 collective-permute-done.11.g1
  130.0 1.7 collective-permute-done.12.g2
  131.7 0.0 collective-permute-done.13.g3
  131.8 0.7 copy-done.16
  132.5 0.1 copy-done.17
  132.6 2.8 %grad_logits.1 = (f32[6,128,256]{2,1,0:T(8,128)}, f32[16,128]{1,0:T(8,128)}) custom-call(f32[512,256]{1,0:T(8,128)} %get-tuple-element.8.ahead.g0, bf16[512,256]{1,0:T(8,128)(2,1)} %copy-done.15, bf16[512,256]{1,0:T(8,128)(2,1)} %copy-done.16, bf16[512,256]{1,0:T(8,128)(2,1)} %copy-done.17, bf16[512,256]{1,0:T(8,128)(2,1)} %copy-done.4, ...), custom_call_target="tpu_custom_call" | custom-call | flops 999999995904 | bytes 1073741824 | tf_op jit(solution)/shard_map/grad_logits/pallas_call | solution.py:167
  135.4 28.9 %all_to_all.15 = f32[16,1,128]{2,1,0:T(1,128)S(1)} all-to-all(f32[16,1,128]{2,1,0:T(1,128)} %bitcast.54), channel_id=1, replica_groups=mesh['y'=4,'l'=4,'x'=4,'h'=4,'c'=2] {'l','h'}, dimensions={0} | all-to-all | bytes 16384 | tf_op jit(solution)/shard_map/mean_square/all_to_all | solution.py:181
  164.4 16.7 %all_to_all.16 = f32[32,1,128]{2,1,0:T(1,128)S(1)} all-to-all(f32[32,1,128]{2,1,0:T(1,128)S(1)} %broadcast_in_dim.2), channel_id=1, replica_groups=mesh['y'=4,'l'=4,'x'=4,'h'=4,'c'=2] {'x','y','c'}, dimensions={0} | all-to-all | bytes 32768 | tf_op jit(solution)/shard_map/mean_square/all_to_all | solution.py:183
  181.0 0.6 reduce_sum.29
  182.3 2.1 %multiply_bitcast_fusion = f32[128,6,256]{2,0,1:T(8,128)} fusion(f32[6,128,256]{2,1,0:T(8,128)} %get-tuple-element.12, f32[]{:T(128)S(6)} %rsqrt.3), kind=kLoop, calls=%fused_computation.9 | loop fusion | flops 196608 | bytes 1572868 | tf_op jit(solution)/shard_map/transpose | solution.py:185
  (37 shorter events, 0.1 us)
Async XLA Ops:
  7.2 1.0 copy-start
  7.2 3.4 %copy-start.18 = (bf16[512,128]{1,0:T(8,128)(2,1)S(1)}, bf16[512,128]{1,0:T(8,128)(2,1)}, u32[]{:S(2)}) copy-start(bf16[512,128]{1,0:T(8,128)(2,1)} %r0.1) | copy-start | bytes 393220
  7.2 29.0 %copy-start.2 = (f32[128,6,256]{2,0,1:T(8,128)S(1)}, f32[128,6,256]{2,0,1:T(8,128)}, u32[]{:S(2)}) copy-start(f32[128,6,256]{2,0,1:T(8,128)} %param.10) | copy-start | bytes 2359300
  7.2 29.0 %copy-start.1 = (f32[128,6,256]{2,0,1:T(8,128)S(1)}, f32[128,6,256]{2,0,1:T(8,128)}, u32[]{:S(2)}) copy-start(f32[128,6,256]{2,0,1:T(8,128)} %param.9) | copy-start | bytes 2359300
  7.2 86.2 %all-gather.7.cloned.1.call-start = ((), (), s32[]{:S(2)}) async-start(), calls=%async_computation.5 | async-start | bytes 2621440 | tf_op jit(solution)/shard_map/hidden/all_gather | solution.py:112
  10.5 26.0 %copy-start.3 = (bf16[512,512]{1,0:T(8,128)(2,1)S(1)}, bf16[512,512]{1,0:T(8,128)(2,1)}, u32[]{:S(2)}) copy-start(bf16[512,512]{1,0:T(8,128)(2,1)} %constant.34.clone) | copy-start | bytes 1572868
  10.5 26.0 %copy-start.5 = (bf16[512,256]{1,0:T(8,128)(2,1)S(1)}, bf16[512,256]{1,0:T(8,128)(2,1)}, u32[]{:S(2)}) copy-start(bf16[512,256]{1,0:T(8,128)(2,1)} %param.8) | copy-start | bytes 786436
  10.6 113.2 %all-gather.5.cloned.1.call-start = ((), (), s32[]{:S(2)}) async-start(), calls=%async_computation.4 | async-start | bytes 1310720 | tf_op jit(solution)/shard_map/masked/all_gather | solution.py:126
  10.6 29.3 %collective-permute-start.1 = (bf16[512,128]{1,0:T(8,128)(2,1)S(1)}, bf16[512,128]{1,0:T(8,128)(2,1)S(1)}, u32[]{:S(2)}, u32[]{:S(2)}) collective-permute-start(bf16[512,128]{1,0:T(8,128)(2,1)S(1)} %copy-done.18), channel_id=1, source_target_pairs={{0,4},{2,6},{4,0},{6,2},{1,5},{3,7},{5,1},{7,3},{8,12},{10,14},{12... | collective-permute-start | bytes 393224 | tf_op jit(solution)/shard_map/up/ppermute | solution.py:80
  27.0 12.9 %collective-permute-start = (bf16[512,128]{1,0:T(8,128)(2,1)S(1)}, bf16[512,128]{1,0:T(8,128)(2,1)S(1)}, u32[]{:S(2)}, u32[]{:S(2)}) collective-permute-start(bf16[512,128]{1,0:T(8,128)(2,1)S(1)} %copy-done.18), channel_id=1, source_target_pairs={{0,2},{2,4},{4,6},{6,0},{1,3},{3,5},{5,7},{7,1},{8,10},{10,12},{12... | collective-permute-start | bytes 393224 | tf_op jit(solution)/shard_map/up/ppermute | solution.py:80
  31.0 20.1 %collective-permute-start.2 = (bf16[512,128]{1,0:T(8,128)(2,1)S(1)}, bf16[512,128]{1,0:T(8,128)(2,1)S(1)}, u32[]{:S(2)}, u32[]{:S(2)}) collective-permute-start(bf16[512,128]{1,0:T(8,128)(2,1)S(1)} %copy-done.18), channel_id=1, source_target_pairs={{0,6},{2,0},{4,2},{6,4},{1,7},{3,1},{5,3},{7,5},{8,14},{10,8},{12,... | collective-permute-start | bytes 393224 | tf_op jit(solution)/shard_map/up/ppermute | solution.py:80
  36.5 1.4 copy-start.7
  36.9 1.9 copy-start.4
  36.9 1.3 copy-start.9
  36.9 1.6 copy-start.8
  37.9 0.9 copy-start.6
  39.8 144.6 %reduce-scatter.2.cloned.1.call-start = ((), (), s32[]{:S(2)}) async-start(), calls=%async_computation.3 | async-start | bytes 2621440 | tf_op jit(solution)/shard_map/grad_hidden_sum/reduce_scatter | solution.py:165
  39.9 11.2 %copy-start.19 = (bf16[512,128]{1,0:T(8,128)(2,1)}, bf16[512,128]{1,0:T(8,128)(2,1)S(1)}, u32[]{:S(2)}) copy-start(bf16[512,128]{1,0:T(8,128)(2,1)S(1)} %collective-permute-done.1.r2) | copy-start | bytes 393220
  39.9 11.2 %copy-start.20 = (bf16[512,128]{1,0:T(8,128)(2,1)}, bf16[512,128]{1,0:T(8,128)(2,1)S(1)}, u32[]{:S(2)}) copy-start(bf16[512,128]{1,0:T(8,128)(2,1)S(1)} %collective-permute-done.r1) | copy-start | bytes 393220
  51.1 0.7 copy-start.21
  53.7 26.6 %collective-permute-start.6 = (bf16[4,512,128]{2,1,0:T(8,128)(2,1)}, bf16[4,512,128]{2,1,0:T(8,128)(2,1)S(1)}, u32[]{:S(2)}, u32[]{:S(2)}) collective-permute-start(bf16[4,512,128]{2,1,0:T(8,128)(2,1)} %stack_upstream.1), channel_id=1, source_target_pairs={{0,24},{8,152},{16,280},{24,408},{128,0},{136,128},{144,256},{152,... | collective-permute-start | bytes 1572872 | tf_op jit(solution)/shard_map/upstream_xy/ppermute | solution.py:130
  58.1 25.6 %collective-permute-start.5 = (bf16[4,512,128]{2,1,0:T(8,128)(2,1)}, bf16[4,512,128]{2,1,0:T(8,128)(2,1)S(1)}, u32[]{:S(2)}, u32[]{:S(2)}) collective-permute-start(bf16[4,512,128]{2,1,0:T(8,128)(2,1)} %stack_upstream.1), channel_id=1, source_target_pairs={{0,16},{8,144},{16,272},{24,400},{128,24},{136,152},{144,280},{152... | collective-permute-start | bytes 1572872 | tf_op jit(solution)/shard_map/upstream_xy/ppermute | solution.py:130
  63.8 23.1 %collective-permute-start.4 = (bf16[4,512,128]{2,1,0:T(8,128)(2,1)}, bf16[4,512,128]{2,1,0:T(8,128)(2,1)S(1)}, u32[]{:S(2)}, u32[]{:S(2)}) collective-permute-start(bf16[4,512,128]{2,1,0:T(8,128)(2,1)} %stack_upstream.1), channel_id=1, source_target_pairs={{0,8},{8,136},{16,264},{24,392},{128,16},{136,144},{144,272},{152,... | collective-permute-start | bytes 1572872 | tf_op jit(solution)/shard_map/upstream_xy/ppermute | solution.py:130
  65.7 23.7 %collective-permute-start.3 = (bf16[4,512,128]{2,1,0:T(8,128)(2,1)}, bf16[4,512,128]{2,1,0:T(8,128)(2,1)S(1)}, u32[]{:S(2)}, u32[]{:S(2)}) collective-permute-start(bf16[4,512,128]{2,1,0:T(8,128)(2,1)} %stack_upstream.1), channel_id=1, source_target_pairs={{0,0},{8,128},{16,256},{24,384},{128,8},{136,136},{144,264},{152,3... | collective-permute-start | bytes 1572872 | tf_op jit(solution)/shard_map/upstream_xy/ppermute | solution.py:130
  80.2 13.1 %copy-start.10 = (bf16[4,512,128]{2,1,0:T(8,128)(2,1)}, bf16[4,512,128]{2,1,0:T(8,128)(2,1)S(1)}, u32[]{:S(2)}) copy-start(bf16[4,512,128]{2,1,0:T(8,128)(2,1)S(1)} %collective-permute-done.6.a3) | copy-start | bytes 1572868
  80.2 11.8 %collective-permute-start.10 = (bf16[4,512,128]{2,1,0:T(8,128)(2,1)S(1)}, bf16[4,512,128]{2,1,0:T(8,128)(2,1)S(1)}, u32[]{:S(2)}, u32[]{:S(2)}) collective-permute-start(bf16[4,512,128]{2,1,0:T(8,128)(2,1)S(1)} %collective-permute-done.6.a3), channel_id=1, source_target_pairs={{0,1},{1,0},{2,3},{3,2},{4,5},{5,4},{6,7},{7,6},{8,9},{9,8},{10,11... | collective-permute-start | bytes 1572872 | tf_op jit(solution)/shard_map/upstream_core/ppermute | solution.py:134
  83.6 9.7 %copy-start.11 = (bf16[4,512,128]{2,1,0:T(8,128)(2,1)}, bf16[4,512,128]{2,1,0:T(8,128)(2,1)S(1)}, u32[]{:S(2)}) copy-start(bf16[4,512,128]{2,1,0:T(8,128)(2,1)S(1)} %collective-permute-done.5.a2) | copy-start | bytes 1572868
  83.7 8.4 %collective-permute-start.9 = (bf16[4,512,128]{2,1,0:T(8,128)(2,1)S(1)}, bf16[4,512,128]{2,1,0:T(8,128)(2,1)}, u32[]{:S(2)}, u32[]{:S(2)}) collective-permute-start(bf16[4,512,128]{2,1,0:T(8,128)(2,1)S(1)} %collective-permute-done.5.a2), channel_id=1, source_target_pairs={{0,1},{1,0},{2,3},{3,2},{4,5},{5,4},{6,7},{7,6},{8,9},{9,8},{10,11... | collective-permute-start | bytes 1572872 | tf_op jit(solution)/shard_map/upstream_core/ppermute | solution.py:134
  86.9 6.5 %copy-start.12 = (bf16[4,512,128]{2,1,0:T(8,128)(2,1)}, bf16[4,512,128]{2,1,0:T(8,128)(2,1)S(1)}, u32[]{:S(2)}) copy-start(bf16[4,512,128]{2,1,0:T(8,128)(2,1)S(1)} %collective-permute-done.4.a1) | copy-start | bytes 1572868
  86.9 5.2 %collective-permute-start.8 = (bf16[4,512,128]{2,1,0:T(8,128)(2,1)S(1)}, bf16[4,512,128]{2,1,0:T(8,128)(2,1)}, u32[]{:S(2)}, u32[]{:S(2)}) collective-permute-start(bf16[4,512,128]{2,1,0:T(8,128)(2,1)S(1)} %collective-permute-done.4.a1), channel_id=1, source_target_pairs={{0,1},{1,0},{2,3},{3,2},{4,5},{5,4},{6,7},{7,6},{8,9},{9,8},{10,11... | collective-permute-start | bytes 1572872 | tf_op jit(solution)/shard_map/upstream_core/ppermute | solution.py:134
  89.4 4.0 %copy-start.13 = (bf16[4,512,128]{2,1,0:T(8,128)(2,1)}, bf16[4,512,128]{2,1,0:T(8,128)(2,1)S(1)}, u32[]{:S(2)}) copy-start(bf16[4,512,128]{2,1,0:T(8,128)(2,1)S(1)} %collective-permute-done.3.a0) | copy-start | bytes 1572868
  89.4 3.9 %collective-permute-start.7 = (bf16[4,512,128]{2,1,0:T(8,128)(2,1)S(1)}, bf16[4,512,128]{2,1,0:T(8,128)(2,1)}, u32[]{:S(2)}, u32[]{:S(2)}) collective-permute-start(bf16[4,512,128]{2,1,0:T(8,128)(2,1)S(1)} %collective-permute-done.3.a0), channel_id=1, source_target_pairs={{0,1},{1,0},{2,3},{3,2},{4,5},{5,4},{6,7},{7,6},{8,9},{9,8},{10,11... | collective-permute-start | bytes 1572872 | tf_op jit(solution)/shard_map/upstream_core/ppermute | solution.py:134
  92.1 1.3 copy-start.14
  99.5 30.4 %collective-permute-start.11 = (bf16[512,256]{1,0:T(8,128)(2,1)}, bf16[512,256]{1,0:T(8,128)(2,1)S(1)}, u32[]{:S(2)}, u32[]{:S(2)}) collective-permute-start(bf16[512,256]{1,0:T(8,128)(2,1)} %get-tuple-element.9), channel_id=1, source_target_pairs={{0,32},{32,64},{64,96},{96,0},{1,33},{33,65},{65,97},{97,1},{2,34}... | collective-permute-start | bytes 786440 | tf_op jit(solution)/shard_map/grad_masked_sum/ppermute | solution.py:80
  101.5 30.3 %collective-permute-start.12 = (bf16[512,256]{1,0:T(8,128)(2,1)}, bf16[512,256]{1,0:T(8,128)(2,1)S(1)}, u32[]{:S(2)}, u32[]{:S(2)}) collective-permute-start(bf16[512,256]{1,0:T(8,128)(2,1)} %get-tuple-element.10), channel_id=1, source_target_pairs={{0,64},{32,96},{64,0},{96,32},{1,65},{33,97},{65,1},{97,33},{2,66}... | collective-permute-start | bytes 786440 | tf_op jit(solution)/shard_map/grad_masked_sum/ppermute | solution.py:80
  105.4 26.4 %collective-permute-start.13 = (bf16[512,256]{1,0:T(8,128)(2,1)}, bf16[512,256]{1,0:T(8,128)(2,1)S(1)}, u32[]{:S(2)}, u32[]{:S(2)}) collective-permute-start(bf16[512,256]{1,0:T(8,128)(2,1)} %get-tuple-element.11), channel_id=1, source_target_pairs={{0,96},{32,0},{64,32},{96,64},{1,97},{33,1},{65,33},{97,65},{2,98}... | collective-permute-start | bytes 786440 | tf_op jit(solution)/shard_map/grad_masked_sum/ppermute | solution.py:80
  130.0 1.8 copy-start.15
  131.7 0.7 copy-start.16
  131.7 0.8 copy-start.17
Sparse Core Ops, SparseCore 0:
  10.7 43.8 all-gather.6
  56.7 67.0 all-gather.4
  130.1 46.4 reduce-scatter.1

commit v3 on v2

--- a/solution.py
+++ b/solution.py
@@ -25,8 +25,8 @@
         col = lax.rem(h + 8 - l - e, 4)
         total = None
         for k in range(4):
-            tok = lax.rem(x + 4 - k, 4)
-            mine, theirs = own[k][col], other[k][col]
+            tok = lax.rem(x + 16 - y - k - 2 * c, 4)
+            mine, theirs = own[k][col], other[(k + 2) % 4][col]
             first = jnp.where(c == 0, mine, theirs)
             second = jnp.where(c == 0, theirs, mine)
             part = jnp.dot(
@@ -38,15 +38,15 @@
 
 def grad_hidden_kernel(place, m, a0, a1, a2, a3, b0, b1, b2, b3, ahead, out, mt):
     del ahead
-    x, c, h = place[1], place[2], place[4]
+    x, c, y, h = (place[i] for i in range(1, 5))
     own, other = (a0, a1, a2, a3), (b0, b1, b2, b3)
     for d in range(4):
         mt[256 * d : 256 * d + 256, :] = m[lax.rem(h + 4 - d, 4)]
     for k in range(4):
-        tok = lax.rem(x + 4 - k, 4)
+        tok = lax.rem(x + 16 - y - k - 2 * c, 4)
         pieces = []
         for d in range(4):
-            mine, theirs = own[k][d], other[k][d]
+            mine, theirs = own[k][d], other[(k + 2) % 4][d]
             pieces += [jnp.where(c == 0, mine, theirs), jnp.where(c == 0, theirs, mine)]
         out[tok] = jnp.dot(
             jnp.concatenate(pieces, axis=1), mt[...], preferred_element_type=jnp.float32
@@ -123,11 +123,20 @@
         masked, order, (((0,), (0,)), ((), ())), preferred_element_type=jnp.float32
     ).astype(jnp.bfloat16)
     with jax.named_scope("masked"):
-        mt = lax.all_gather(masked_t, "l")
+        mt = lax.all_to_all(jnp.broadcast_to(masked_t[None], (4, 256, 512)), "l", 0, 0)
 
     with jax.named_scope("upstream_xy"):
         own = [
-            lax.ppermute(up, ("y", "x"), [(b * 4 + a, a * 4 + (b + k) % 4) for b in range(4) for a in range(4)])
+            lax.ppermute(
+                up,
+                ("y", "x", "c"),
+                [
+                    ((b * 4 + a) * 2 + core, (a * 4 + (a + b + k + 2 * core) % 4) * 2 + core)
+                    for b in range(4)
+                    for a in range(4)
+                    for core in range(2)
+                ],
+            )
             for k in range(4)
         ]
     with jax.named_scope("upstream_core"):

time: 192 us -> 184 us (0.958)
  waiting for transfers between devices: 43.6 us -> 22.9 us
  starting transfers between devices: 58.2 us -> 75.2 us
  blocking collectives: 45.6 us -> 41.3 us
    all_gather x1 -> x0, waiting for transfers between devices: 15.2 us -> none  [body(): mt = lax.all_gather(masked_t, 'l')]
    ppermute x4, starting transfers between devices: 9.78 us -> 17.9 us  [body(): other = [lax.ppermute(u, 'c', [(0, 1), (1, 0)]) for u in own]]
    all_to_all x1, blocking collectives: 28.9 us -> 24.4 us  [body(): squares = lax.all_to_all(squares, ('l', 'h'), 0, 0, tiled=True)]
    all_to_all x0 -> x1, starting transfers between devices: none -> 4.24 us  [body(): lax.all_to_all(jnp.broadcast_to(masked_t[None], (4, 256, 512)), 'l', 0, 0)]
    ppermute x4, starting transfers between devices: 13.7 us -> 17.8 us  [body(): lax.ppermute(up, ('y', 'x', 'c'), [((b * 4 + a) * 2 + core, (a * 4 + (a +...]
    ppermute x4, waiting for transfers between devices: 14.1 us -> 10.5 us  [body(): lax.ppermute(up, ('y', 'x', 'c'), [((b * 4 + a) * 2 + core, (a * 4 + (a +...]
  transfers between devices with their start and end apart: 17 -> 17, of which waited for: 6 -> 4; matrix products, arithmetic and copies ran while one was open for 4% -> 5% of each run, Pallas kernels for 9% -> 9%
where the time goes in v3:
time: 184 us; the launch traced here: 183 us
  starting transfers between devices  75.2 us (41%)
  blocking collectives  41.3 us (22%)
  waiting for transfers between devices  22.9 us (12%)
  Pallas kernels  17 us (9%)
  between operations  15.1 us (8%)
  local copies, waits for them, and re-layouts  4.06 us (2%)
  other arithmetic  4.05 us (2%)
  matrix products  3.62 us (2%)
    ppermute x6, starting transfers between devices, shift(): return lax.ppermute(value, axis, [(i, (i + by) % 4) for i in range(4)])  35.1 us
    all_to_all x1, blocking collectives, body(): squares = lax.all_to_all(squares, ('l', 'h'), 0, 0, tiled=True)  24.4 us
    ppermute x4, starting transfers between devices, body(): other = [lax.ppermute(u, 'c', [(0, 1), (1, 0)]) for u in own]  17.9 us
    ppermute x4, starting transfers between devices, body(): lax.ppermute(up, ('y', 'x', 'c'), [((b * 4 + a) * 2 + core, (a * 4 + (a +...  17.8 us
    all_to_all x1, blocking collectives, body(): squares = lax.all_to_all(squares, ('x', 'y', 'c'), 0, 0, tiled=True)  16.9 us
    ppermute x6, waiting for transfers between devices, shift(): return lax.ppermute(value, axis, [(i, (i + by) % 4) for i in range(4)])  11.3 us
    ppermute x4, waiting for transfers between devices, body(): lax.ppermute(up, ('y', 'x', 'c'), [((b * 4 + a) * 2 + core, (a * 4 + (a +...  10.5 us
    pallas_call x1, Pallas kernels, body(): pl.pallas_call(grad_hidden_kernel, out_shape=jax.ShapeDtypeStruct((4, 512...  6.17 us
  transfers between devices with their start and end apart: 17, of which 4 were waited for; matrix products, arithmetic and copies ran while one was open for 5% of the time, Pallas kernels for 9%

profile of v3, /device:TPU:1, one launch (start us, length us, event | category | flops | bytes accessed | tf_op | source)
XLA Modules:
  0.0 183.2 jit_solution(9305584818520638831)
XLA Ops:
  7.2 0.0 copy-start
  7.2 0.0 all-gather.3.cloned.1.call-start
  7.2 16.4 %collective-permute-start.1 = (bf16[512,128]{1,0:T(8,128)(2,1)}, bf16[512,128]{1,0:T(8,128)(2,1)S(1)}, u32[]{:S(2)}, u32[]{:S(2)}) collective-permute-start(bf16[512,128]{1,0:T(8,128)(2,1)} %r0.1), channel_id=1, source_target_pairs={{0,4},{2,6},{4,0},{6,2},{1,5},{3,7},{5,1},{7,3},{8,12},{10,14},{12... | collective-permute-start | bytes 393224 | tf_op jit(solution)/shard_map/up/ppermute | solution.py:80
  23.7 4.0 %collective-permute-start = (bf16[512,128]{1,0:T(8,128)(2,1)}, bf16[512,128]{1,0:T(8,128)(2,1)S(1)}, u32[]{:S(2)}, u32[]{:S(2)}) collective-permute-start(bf16[512,128]{1,0:T(8,128)(2,1)} %r0.1), channel_id=1, source_target_pairs={{0,2},{2,4},{4,6},{6,0},{1,3},{3,5},{5,7},{7,1},{8,10},{10,12},{12... | collective-permute-start | bytes 393224 | tf_op jit(solution)/shard_map/up/ppermute | solution.py:80
  27.7 5.2 %collective-permute-start.2 = (bf16[512,128]{1,0:T(8,128)(2,1)}, bf16[512,128]{1,0:T(8,128)(2,1)S(1)}, u32[]{:S(2)}, u32[]{:S(2)}) collective-permute-start(bf16[512,128]{1,0:T(8,128)(2,1)} %r0.1), channel_id=1, source_target_pairs={{0,6},{2,0},{4,2},{6,4},{1,7},{3,1},{5,3},{7,5},{8,14},{10,8},{12,... | collective-permute-start | bytes 393224 | tf_op jit(solution)/shard_map/up/ppermute | solution.py:80
  32.9 0.0 copy-done
  32.9 2.3 %convolution_convert_fusion = bf16[512,512]{1,0:T(8,128)(2,1)} fusion(bf16[512,512]{1,0:T(8,128)(2,1)} %constant.34.clone, bf16[512,512]{1,0:T(8,128)(2,1)S(1)} %copy-done), kind=kOutput, calls=%fused_computation | convolution fusion | flops 268697600 | bytes 1572864 | tf_op jit(solution)/shard_map/dot_general | solution.py:108
  35.2 0.0 all-gather.3.cloned.1.call-update
  35.3 0.1 bitcast_reduce_fusion
  35.4 0.2 fusion.3
  35.5 0.7 copy-done.3
  36.3 0.1 copy-done.5
  36.3 0.3 convolution_convert_fusion.1.w
  36.6 0.0 copy-start.9
  36.6 0.0 copy-start.8
  36.7 1.0 convert_convert_fusion
  37.7 0.2 fusion.8
  38.0 0.3 convolution_add_fusion.2
  38.2 0.3 convolution_add_fusion.1
  38.5 0.1 copy-done.6
  38.6 0.2 fusion
  38.9 1.0 broadcast_in_dim.4
  39.9 4.2 %all-to-all-start = ((bf16[4,256,512]{2,1,0:T(8,128)(2,1)}), bf16[4,256,512]{2,1,0:T(8,128)(2,1)}, u32[]{:S(2)}, u32[]{:S(2)}) async-start(bf16[4,256,512]{2,1,0:T(8,128)(2,1)} %broadcast_in_dim.4), calls=%async_computation | async-start | bytes 2097152 | tf_op jit(solution)/shard_map/masked/all_to_all | solution.py:126
  44.2 0.0 reduce-scatter.2.cloned.1.call-start
  44.2 0.0 collective-permute-done.1.r2
  44.2 0.0 collective-permute-done.r1
  44.3 3.7 %collective-permute-done.2.r3 = bf16[512,128]{1,0:T(8,128)(2,1)S(1)} collective-permute-done((bf16[512,128]{1,0:T(8,128)(2,1)}, bf16[512,128]{1,0:T(8,128)(2,1)S(1)}, u32[]{:S(2)}, u32[]{:S(2)}) %collective-permute-start.2) | collective-permute-done | bytes 131104 | tf_op jit(solution)/shard_map/up/ppermute | solution.py:80
  48.0 0.7 copy-done.20
  48.6 2.0 %stack_upstream.1 = bf16[4,512,128]{2,1,0:T(8,128)(2,1)} custom-call(bf16[512,128]{1,0:T(8,128)(2,1)} %r0.1, bf16[512,128]{1,0:T(8,128)(2,1)} %copy-done.19, bf16[512,128]{1,0:T(8,128)(2,1)} %copy-done.18, bf16[512,128]{1,0:T(8,128)(2,1)} %copy-done.20), custom_call_target="tpu_custom_call" | custom-call | flops 999999995904 | bytes 1073741824 | tf_op jit(solution)/shard_map/stack_upstream/pallas_call | solution.py:93
  50.6 3.0 %collective-permute-start.6 = (bf16[4,512,128]{2,1,0:T(8,128)(2,1)}, bf16[4,512,128]{2,1,0:T(8,128)(2,1)S(1)}, u32[]{:S(2)}, u32[]{:S(2)}) collective-permute-start(bf16[4,512,128]{2,1,0:T(8,128)(2,1)} %stack_upstream.1), channel_id=1, source_target_pairs={{0,24},{1,9},{8,128},{9,145},{16,264},{17,281},{24,400},{25,385},{... | collective-permute-start | bytes 1572872 | tf_op jit(solution)/shard_map/upstream_xy/ppermute | solution.py:130
  53.7 1.7 collective-permute-start.5
  55.4 6.1 %collective-permute-start.4 = (bf16[4,512,128]{2,1,0:T(8,128)(2,1)}, bf16[4,512,128]{2,1,0:T(8,128)(2,1)S(1)}, u32[]{:S(2)}, u32[]{:S(2)}) collective-permute-start(bf16[4,512,128]{2,1,0:T(8,128)(2,1)} %stack_upstream.1), channel_id=1, source_target_pairs={{0,8},{1,25},{8,144},{9,129},{16,280},{17,265},{24,384},{25,401},{... | collective-permute-start | bytes 1572872 | tf_op jit(solution)/shard_map/upstream_xy/ppermute | solution.py:130
  61.5 7.0 %collective-permute-start.3 = (bf16[4,512,128]{2,1,0:T(8,128)(2,1)}, bf16[4,512,128]{2,1,0:T(8,128)(2,1)S(1)}, u32[]{:S(2)}, u32[]{:S(2)}) collective-permute-start(bf16[4,512,128]{2,1,0:T(8,128)(2,1)} %stack_upstream.1), channel_id=1, source_target_pairs={{0,0},{1,17},{8,136},{9,153},{16,272},{17,257},{24,408},{25,393},{... | collective-permute-start | bytes 1572872 | tf_op jit(solution)/shard_map/upstream_xy/ppermute | solution.py:130
  68.5 10.5 %collective-permute-done.6.a3 = bf16[4,512,128]{2,1,0:T(8,128)(2,1)S(1)} collective-permute-done((bf16[4,512,128]{2,1,0:T(8,128)(2,1)}, bf16[4,512,128]{2,1,0:T(8,128)(2,1)S(1)}, u32[]{:S(2)}, u32[]{:S(2)}) %collective-permute-start.6) | collective-permute-done | bytes 524320 | tf_op jit(solution)/shard_map/upstream_xy/ppermute | solution.py:130
  79.0 9.8 %collective-permute-start.10 = (bf16[4,512,128]{2,1,0:T(8,128)(2,1)S(1)}, bf16[4,512,128]{2,1,0:T(8,128)(2,1)S(1)}, u32[]{:S(2)}, u32[]{:S(2)}) collective-permute-start(bf16[4,512,128]{2,1,0:T(8,128)(2,1)S(1)} %collective-permute-done.6.a3), channel_id=1, source_target_pairs={{0,1},{1,0},{2,3},{3,2},{4,5},{5,4},{6,7},{7,6},{8,9},{9,8},{10,11... | collective-permute-start | bytes 1572872 | tf_op jit(solution)/shard_map/upstream_core/ppermute | solution.py:143
  88.8 0.0 collective-permute-done.5.a2
  88.8 3.8 %collective-permute-start.9 = (bf16[4,512,128]{2,1,0:T(8,128)(2,1)S(1)}, bf16[4,512,128]{2,1,0:T(8,128)(2,1)}, u32[]{:S(2)}, u32[]{:S(2)}) collective-permute-start(bf16[4,512,128]{2,1,0:T(8,128)(2,1)S(1)} %collective-permute-done.5.a2), channel_id=1, source_target_pairs={{0,1},{1,0},{2,3},{3,2},{4,5},{5,4},{6,7},{7,6},{8,9},{9,8},{10,11... | collective-permute-start | bytes 1572872 | tf_op jit(solution)/shard_map/upstream_core/ppermute | solution.py:143
  92.6 0.0 collective-permute-done.4.a1
  92.6 1.9 %collective-permute-start.8 = (bf16[4,512,128]{2,1,0:T(8,128)(2,1)S(1)}, bf16[4,512,128]{2,1,0:T(8,128)(2,1)}, u32[]{:S(2)}, u32[]{:S(2)}) collective-permute-start(bf16[4,512,128]{2,1,0:T(8,128)(2,1)S(1)} %collective-permute-done.4.a1), channel_id=1, source_target_pairs={{0,1},{1,0},{2,3},{3,2},{4,5},{5,4},{6,7},{7,6},{8,9},{9,8},{10,11... | collective-permute-start | bytes 1572872 | tf_op jit(solution)/shard_map/upstream_core/ppermute | solution.py:143
  94.5 0.0 collective-permute-done.3.a0
  94.5 0.0 copy-start.13
  94.5 2.4 %collective-permute-start.7 = (bf16[4,512,128]{2,1,0:T(8,128)(2,1)S(1)}, bf16[4,512,128]{2,1,0:T(8,128)(2,1)}, u32[]{:S(2)}, u32[]{:S(2)}) collective-permute-start(bf16[4,512,128]{2,1,0:T(8,128)(2,1)S(1)} %collective-permute-done.3.a0), channel_id=1, source_target_pairs={{0,1},{1,0},{2,3},{3,2},{4,5},{5,4},{6,7},{7,6},{8,9},{9,8},{10,11... | collective-permute-start | bytes 1572872 | tf_op jit(solution)/shard_map/upstream_core/ppermute | solution.py:143
  97.0 0.6 stack.23.place
  97.5 0.0 collective-permute-done.10.b3
  97.5 0.0 collective-permute-done.9.b2
  97.5 0.0 collective-permute-done.8.b1
  97.5 1.0 collective-permute-done.7.b0
  98.6 6.0 %grad_masked.1 = (f32[512,256]{1,0:T(8,128)}, bf16[512,256]{1,0:T(8,128)(2,1)}, bf16[512,256]{1,0:T(8,128)(2,1)}, bf16[512,256]{1,0:T(8,128)(2,1)}) custom-call(s32[5]{0:T(128)} %stack.23.place, bf16[4,512,512]{2,1,0:T(8,128)(2,1)} %bitcast.54, bf16[4,512,128]{2,1,0:T(8,128)(2,1)} %copy-done.13, bf16[4,512,128]{2,1,0:T(8,128)(2,1)} %copy-done.12, ...), custom_call_target="tpu_custom_call" | custom-call | flops 2147483648 | bytes 7340032 | tf_op jit(solution)/shard_map/grad_masked/pallas_call | solution.py:148
  104.6 2.4 %collective-permute-start.11 = (bf16[512,256]{1,0:T(8,128)(2,1)}, bf16[512,256]{1,0:T(8,128)(2,1)S(1)}, u32[]{:S(2)}, u32[]{:S(2)}) collective-permute-start(bf16[512,256]{1,0:T(8,128)(2,1)} %get-tuple-element.9), channel_id=1, source_target_pairs={{0,32},{32,64},{64,96},{96,0},{1,33},{33,65},{65,97},{97,1},{2,34}... | collective-permute-start | bytes 786440 | tf_op jit(solution)/shard_map/grad_masked_sum/ppermute | solution.py:80
  107.0 4.2 %collective-permute-start.12 = (bf16[512,256]{1,0:T(8,128)(2,1)}, bf16[512,256]{1,0:T(8,128)(2,1)S(1)}, u32[]{:S(2)}, u32[]{:S(2)}) collective-permute-start(bf16[512,256]{1,0:T(8,128)(2,1)} %get-tuple-element.10), channel_id=1, source_target_pairs={{0,64},{32,96},{64,0},{96,32},{1,65},{33,97},{65,1},{97,33},{2,66}... | collective-permute-start | bytes 786440 | tf_op jit(solution)/shard_map/grad_masked_sum/ppermute | solution.py:80
  111.1 3.0 %collective-permute-start.13 = (bf16[512,256]{1,0:T(8,128)(2,1)}, bf16[512,256]{1,0:T(8,128)(2,1)S(1)}, u32[]{:S(2)}, u32[]{:S(2)}) collective-permute-start(bf16[512,256]{1,0:T(8,128)(2,1)} %get-tuple-element.11), channel_id=1, source_target_pairs={{0,96},{32,0},{64,32},{96,64},{1,97},{33,1},{65,33},{97,65},{2,98}... | collective-permute-start | bytes 786440 | tf_op jit(solution)/shard_map/grad_masked_sum/ppermute | solution.py:80
  114.1 0.0 all-to-all-done.m
  114.2 6.2 %grad_hidden.1 = bf16[4,512,512]{2,1,0:T(8,128)(2,1)} custom-call(s32[5]{0:T(128)} %stack.23.place, bf16[4,256,512]{2,1,0:T(8,128)(2,1)} %all-to-all-done.m, bf16[4,512,128]{2,1,0:T(8,128)(2,1)} %copy-done.13, bf16[4,512,128]{2,1,0:T(8,128)(2,1)} %copy-done.12, bf16[4,512,128]{2,1,0:T(8,128)(2,1)} %copy-done.11, bf16[4,512,128]{2,1,0:T(8,128)(2,1)} %copy-done.10, ...), custom_call_target="tpu_custom_call" | custom-call | flops 2147483648 | bytes 7340032 | tf_op jit(solution)/shard_map/grad_hidden/pallas_call | solution.py:162
  120.3 0.0 reduce-scatter.2.cloned.1.call-update
  120.3 0.0 collective-permute-done.11.g1
  120.4 7.6 %collective-permute-done.12.g2 = bf16[512,256]{1,0:T(8,128)(2,1)S(1)} collective-permute-done((bf16[512,256]{1,0:T(8,128)(2,1)}, bf16[512,256]{1,0:T(8,128)(2,1)S(1)}, u32[]{:S(2)}, u32[]{:S(2)}) %collective-permute-start.12) | collective-permute-done | bytes 262176 | tf_op jit(solution)/shard_map/grad_masked_sum/ppermute | solution.py:80
  127.9 0.0 collective-permute-done.13.g3
  128.0 0.7 copy-done.16
  128.6 0.1 copy-done.17
  128.8 2.9 %grad_logits.1 = (f32[6,128,256]{2,1,0:T(8,128)}, f32[16,128]{1,0:T(8,128)}) custom-call(f32[512,256]{1,0:T(8,128)} %get-tuple-element.8.ahead.g0, bf16[512,256]{1,0:T(8,128)(2,1)} %copy-done.15, bf16[512,256]{1,0:T(8,128)(2,1)} %copy-done.16, bf16[512,256]{1,0:T(8,128)(2,1)} %copy-done.17, bf16[512,256]{1,0:T(8,128)(2,1)} %copy-done.4, ...), custom_call_target="tpu_custom_call" | custom-call | flops 999999995904 | bytes 1073741824 | tf_op jit(solution)/shard_map/grad_logits/pallas_call | solution.py:176
  131.6 24.4 %all_to_all.20 = f32[16,1,128]{2,1,0:T(1,128)S(1)} all-to-all(f32[16,1,128]{2,1,0:T(1,128)} %bitcast.53), channel_id=1, replica_groups=mesh['y'=4,'l'=4,'x'=4,'h'=4,'c'=2] {'l','h'}, dimensions={0} | all-to-all | bytes 16384 | tf_op jit(solution)/shard_map/mean_square/all_to_all | solution.py:190
  156.1 16.9 %all_to_all.21 = f32[32,1,128]{2,1,0:T(1,128)S(1)} all-to-all(f32[32,1,128]{2,1,0:T(1,128)S(1)} %broadcast_in_dim.5), channel_id=1, replica_groups=mesh['y'=4,'l'=4,'x'=4,'h'=4,'c'=2] {'x','y','c'}, dimensions={0} | all-to-all | bytes 32768 | tf_op jit(solution)/shard_map/mean_square/all_to_all | solution.py:192
  173.0 0.6 reduce_sum.29
  174.3 2.1 %multiply_bitcast_fusion = f32[128,6,256]{2,0,1:T(8,128)} fusion(f32[6,128,256]{2,1,0:T(8,128)} %get-tuple-element.12, f32[]{:T(128)S(6)} %rsqrt.3), kind=kLoop, calls=%fused_computation.9 | loop fusion | flops 196608 | bytes 1572868 | tf_op jit(solution)/shard_map/transpose | solution.py:194
  (35 shorter events, 0.1 us)
Async XLA Ops:
  7.2 25.7 %copy-start = (bf16[512,512]{1,0:T(8,128)(2,1)S(1)}, bf16[512,512]{1,0:T(8,128)(2,1)}, u32[]{:S(2)}) copy-start(bf16[512,512]{1,0:T(8,128)(2,1)} %param.6) | copy-start | bytes 1572868
  7.2 28.1 %copy-start.2 = (f32[128,6,256]{2,0,1:T(8,128)S(1)}, f32[128,6,256]{2,0,1:T(8,128)}, u32[]{:S(2)}) copy-start(f32[128,6,256]{2,0,1:T(8,128)} %param.10) | copy-start | bytes 2359300
  7.2 28.1 %copy-start.1 = (f32[128,6,256]{2,0,1:T(8,128)S(1)}, f32[128,6,256]{2,0,1:T(8,128)}, u32[]{:S(2)}) copy-start(f32[128,6,256]{2,0,1:T(8,128)} %param.9) | copy-start | bytes 2359300
  7.2 91.4 %all-gather.3.cloned.1.call-start = ((), (), s32[]{:S(2)}) async-start(), calls=%async_computation.5 | async-start | bytes 2621440 | tf_op jit(solution)/shard_map/hidden/all_gather | solution.py:112
  7.2 37.0 %collective-permute-start.1 = (bf16[512,128]{1,0:T(8,128)(2,1)}, bf16[512,128]{1,0:T(8,128)(2,1)S(1)}, u32[]{:S(2)}, u32[]{:S(2)}) collective-permute-start(bf16[512,128]{1,0:T(8,128)(2,1)} %r0.1), channel_id=1, source_target_pairs={{0,4},{2,6},{4,0},{6,2},{1,5},{3,7},{5,1},{7,3},{8,12},{10,14},{12... | collective-permute-start | bytes 393224 | tf_op jit(solution)/shard_map/up/ppermute | solution.py:80
  23.7 20.6 %collective-permute-start = (bf16[512,128]{1,0:T(8,128)(2,1)}, bf16[512,128]{1,0:T(8,128)(2,1)S(1)}, u32[]{:S(2)}, u32[]{:S(2)}) collective-permute-start(bf16[512,128]{1,0:T(8,128)(2,1)} %r0.1), channel_id=1, source_target_pairs={{0,2},{2,4},{4,6},{6,0},{1,3},{3,5},{5,7},{7,1},{8,10},{10,12},{12... | collective-permute-start | bytes 393224 | tf_op jit(solution)/shard_map/up/ppermute | solution.py:80
  27.7 20.3 %collective-permute-start.2 = (bf16[512,128]{1,0:T(8,128)(2,1)}, bf16[512,128]{1,0:T(8,128)(2,1)S(1)}, u32[]{:S(2)}, u32[]{:S(2)}) collective-permute-start(bf16[512,128]{1,0:T(8,128)(2,1)} %r0.1), channel_id=1, source_target_pairs={{0,6},{2,0},{4,2},{6,4},{1,7},{3,1},{5,3},{7,5},{8,14},{10,8},{12,... | collective-permute-start | bytes 393224 | tf_op jit(solution)/shard_map/up/ppermute | solution.py:80
  35.2 1.0 copy-start.3
  35.2 1.1 copy-start.5
  36.3 1.4 copy-start.7
  36.6 1.9 %copy-start.4 = (bf16[512,256]{1,0:T(8,128)(2,1)}, bf16[512,256]{1,0:T(8,128)(2,1)S(1)}, u32[]{:S(2)}) copy-start(bf16[512,256]{1,0:T(8,128)(2,1)S(1)} %convolution_convert_fusion.1.w) | copy-start | bytes 786436
  36.6 1.3 copy-start.9
  36.6 1.6 copy-start.8
  37.7 0.9 copy-start.6
  39.9 74.2 %all-to-all-start = ((bf16[4,256,512]{2,1,0:T(8,128)(2,1)}), bf16[4,256,512]{2,1,0:T(8,128)(2,1)}, u32[]{:S(2)}, u32[]{:S(2)}) async-start(bf16[4,256,512]{2,1,0:T(8,128)(2,1)} %broadcast_in_dim.4), calls=%async_computation | async-start | bytes 2097152 | tf_op jit(solution)/shard_map/masked/all_to_all | solution.py:126
  44.2 132.2 %reduce-scatter.2.cloned.1.call-start = ((), (), s32[]{:S(2)}) async-start(), calls=%async_computation.4 | async-start | bytes 2621440 | tf_op jit(solution)/shard_map/grad_hidden_sum/reduce_scatter | solution.py:174
  44.2 3.7 %copy-start.18 = (bf16[512,128]{1,0:T(8,128)(2,1)}, bf16[512,128]{1,0:T(8,128)(2,1)S(1)}, u32[]{:S(2)}) copy-start(bf16[512,128]{1,0:T(8,128)(2,1)S(1)} %collective-permute-done.1.r2) | copy-start | bytes 393220
  44.2 3.7 %copy-start.19 = (bf16[512,128]{1,0:T(8,128)(2,1)}, bf16[512,128]{1,0:T(8,128)(2,1)S(1)}, u32[]{:S(2)}) copy-start(bf16[512,128]{1,0:T(8,128)(2,1)S(1)} %collective-permute-done.r1) | copy-start | bytes 393220
  48.0 0.7 copy-start.20
  50.6 28.4 %collective-permute-start.6 = (bf16[4,512,128]{2,1,0:T(8,128)(2,1)}, bf16[4,512,128]{2,1,0:T(8,128)(2,1)S(1)}, u32[]{:S(2)}, u32[]{:S(2)}) collective-permute-start(bf16[4,512,128]{2,1,0:T(8,128)(2,1)} %stack_upstream.1), channel_id=1, source_target_pairs={{0,24},{1,9},{8,128},{9,145},{16,264},{17,281},{24,400},{25,385},{... | collective-permute-start | bytes 1572872 | tf_op jit(solution)/shard_map/upstream_xy/ppermute | solution.py:130
  53.7 35.1 %collective-permute-start.5 = (bf16[4,512,128]{2,1,0:T(8,128)(2,1)}, bf16[4,512,128]{2,1,0:T(8,128)(2,1)S(1)}, u32[]{:S(2)}, u32[]{:S(2)}) collective-permute-start(bf16[4,512,128]{2,1,0:T(8,128)(2,1)} %stack_upstream.1), channel_id=1, source_target_pairs={{0,16},{1,1},{8,152},{9,137},{16,256},{17,273},{24,392},{25,409},{... | collective-permute-start | bytes 1572872 | tf_op jit(solution)/shard_map/upstream_xy/ppermute | solution.py:130
  55.4 37.2 %collective-permute-start.4 = (bf16[4,512,128]{2,1,0:T(8,128)(2,1)}, bf16[4,512,128]{2,1,0:T(8,128)(2,1)S(1)}, u32[]{:S(2)}, u32[]{:S(2)}) collective-permute-start(bf16[4,512,128]{2,1,0:T(8,128)(2,1)} %stack_upstream.1), channel_id=1, source_target_pairs={{0,8},{1,25},{8,144},{9,129},{16,280},{17,265},{24,384},{25,401},{... | collective-permute-start | bytes 1572872 | tf_op jit(solution)/shard_map/upstream_xy/ppermute | solution.py:130
  61.5 33.0 %collective-permute-start.3 = (bf16[4,512,128]{2,1,0:T(8,128)(2,1)}, bf16[4,512,128]{2,1,0:T(8,128)(2,1)S(1)}, u32[]{:S(2)}, u32[]{:S(2)}) collective-permute-start(bf16[4,512,128]{2,1,0:T(8,128)(2,1)} %stack_upstream.1), channel_id=1, source_target_pairs={{0,0},{1,17},{8,136},{9,153},{16,272},{17,257},{24,408},{25,393},{... | collective-permute-start | bytes 1572872 | tf_op jit(solution)/shard_map/upstream_xy/ppermute | solution.py:130
  79.0 19.6 %copy-start.10 = (bf16[4,512,128]{2,1,0:T(8,128)(2,1)}, bf16[4,512,128]{2,1,0:T(8,128)(2,1)S(1)}, u32[]{:S(2)}) copy-start(bf16[4,512,128]{2,1,0:T(8,128)(2,1)S(1)} %collective-permute-done.6.a3) | copy-start | bytes 1572868
  79.0 18.5 %collective-permute-start.10 = (bf16[4,512,128]{2,1,0:T(8,128)(2,1)S(1)}, bf16[4,512,128]{2,1,0:T(8,128)(2,1)S(1)}, u32[]{:S(2)}, u32[]{:S(2)}) collective-permute-start(bf16[4,512,128]{2,1,0:T(8,128)(2,1)S(1)} %collective-permute-done.6.a3), channel_id=1, source_target_pairs={{0,1},{1,0},{2,3},{3,2},{4,5},{5,4},{6,7},{7,6},{8,9},{9,8},{10,11... | collective-permute-start | bytes 1572872 | tf_op jit(solution)/shard_map/upstream_core/ppermute | solution.py:143
  88.8 9.8 %copy-start.11 = (bf16[4,512,128]{2,1,0:T(8,128)(2,1)}, bf16[4,512,128]{2,1,0:T(8,128)(2,1)S(1)}, u32[]{:S(2)}) copy-start(bf16[4,512,128]{2,1,0:T(8,128)(2,1)S(1)} %collective-permute-done.5.a2) | copy-start | bytes 1572868
  88.8 8.7 %collective-permute-start.9 = (bf16[4,512,128]{2,1,0:T(8,128)(2,1)S(1)}, bf16[4,512,128]{2,1,0:T(8,128)(2,1)}, u32[]{:S(2)}, u32[]{:S(2)}) collective-permute-start(bf16[4,512,128]{2,1,0:T(8,128)(2,1)S(1)} %collective-permute-done.5.a2), channel_id=1, source_target_pairs={{0,1},{1,0},{2,3},{3,2},{4,5},{5,4},{6,7},{7,6},{8,9},{9,8},{10,11... | collective-permute-start | bytes 1572872 | tf_op jit(solution)/shard_map/upstream_core/ppermute | solution.py:143
  92.6 6.0 %copy-start.12 = (bf16[4,512,128]{2,1,0:T(8,128)(2,1)}, bf16[4,512,128]{2,1,0:T(8,128)(2,1)S(1)}, u32[]{:S(2)}) copy-start(bf16[4,512,128]{2,1,0:T(8,128)(2,1)S(1)} %collective-permute-done.4.a1) | copy-start | bytes 1572868
  92.6 5.0 %collective-permute-start.8 = (bf16[4,512,128]{2,1,0:T(8,128)(2,1)S(1)}, bf16[4,512,128]{2,1,0:T(8,128)(2,1)}, u32[]{:S(2)}, u32[]{:S(2)}) collective-permute-start(bf16[4,512,128]{2,1,0:T(8,128)(2,1)S(1)} %collective-permute-done.4.a1), channel_id=1, source_target_pairs={{0,1},{1,0},{2,3},{3,2},{4,5},{5,4},{6,7},{7,6},{8,9},{9,8},{10,11... | collective-permute-start | bytes 1572872 | tf_op jit(solution)/shard_map/upstream_core/ppermute | solution.py:143
  94.5 4.1 %copy-start.13 = (bf16[4,512,128]{2,1,0:T(8,128)(2,1)}, bf16[4,512,128]{2,1,0:T(8,128)(2,1)S(1)}, u32[]{:S(2)}) copy-start(bf16[4,512,128]{2,1,0:T(8,128)(2,1)S(1)} %collective-permute-done.3.a0) | copy-start | bytes 1572868
  94.5 4.1 %collective-permute-start.7 = (bf16[4,512,128]{2,1,0:T(8,128)(2,1)S(1)}, bf16[4,512,128]{2,1,0:T(8,128)(2,1)}, u32[]{:S(2)}, u32[]{:S(2)}) collective-permute-start(bf16[4,512,128]{2,1,0:T(8,128)(2,1)S(1)} %collective-permute-done.3.a0), channel_id=1, source_target_pairs={{0,1},{1,0},{2,3},{3,2},{4,5},{5,4},{6,7},{7,6},{8,9},{9,8},{10,11... | collective-permute-start | bytes 1572872 | tf_op jit(solution)/shard_map/upstream_core/ppermute | solution.py:143
  97.5 1.1 copy-start.14
  104.6 15.8 %collective-permute-start.11 = (bf16[512,256]{1,0:T(8,128)(2,1)}, bf16[512,256]{1,0:T(8,128)(2,1)S(1)}, u32[]{:S(2)}, u32[]{:S(2)}) collective-permute-start(bf16[512,256]{1,0:T(8,128)(2,1)} %get-tuple-element.9), channel_id=1, source_target_pairs={{0,32},{32,64},{64,96},{96,0},{1,33},{33,65},{65,97},{97,1},{2,34}... | collective-permute-start | bytes 786440 | tf_op jit(solution)/shard_map/grad_masked_sum/ppermute | solution.py:80
  107.0 21.0 %collective-permute-start.12 = (bf16[512,256]{1,0:T(8,128)(2,1)}, bf16[512,256]{1,0:T(8,128)(2,1)S(1)}, u32[]{:S(2)}, u32[]{:S(2)}) collective-permute-start(bf16[512,256]{1,0:T(8,128)(2,1)} %get-tuple-element.10), channel_id=1, source_target_pairs={{0,64},{32,96},{64,0},{96,32},{1,65},{33,97},{65,1},{97,33},{2,66}... | collective-permute-start | bytes 786440 | tf_op jit(solution)/shard_map/grad_masked_sum/ppermute | solution.py:80
  111.1 16.8 %collective-permute-start.13 = (bf16[512,256]{1,0:T(8,128)(2,1)}, bf16[512,256]{1,0:T(8,128)(2,1)S(1)}, u32[]{:S(2)}, u32[]{:S(2)}) collective-permute-start(bf16[512,256]{1,0:T(8,128)(2,1)} %get-tuple-element.11), channel_id=1, source_target_pairs={{0,96},{32,0},{64,32},{96,64},{1,97},{33,1},{65,33},{97,65},{2,98}... | collective-permute-start | bytes 786440 | tf_op jit(solution)/shard_map/grad_masked_sum/ppermute | solution.py:80
  120.4 7.6 %copy-start.15 = (bf16[512,256]{1,0:T(8,128)(2,1)}, bf16[512,256]{1,0:T(8,128)(2,1)S(1)}, u32[]{:S(2)}) copy-start(bf16[512,256]{1,0:T(8,128)(2,1)S(1)} %collective-permute-done.11.g1) | copy-start | bytes 786436
  127.9 0.7 copy-start.16
  127.9 0.8 copy-start.17
Sparse Core Ops, SparseCore 0:
  35.4 54.1 all-gather.2
  120.5 36.2 reduce-scatter.1

commit v4 on v3

--- a/solution.py
+++ b/solution.py
@@ -16,24 +16,31 @@
         out[d] = piece[...]
 
 
-def grad_masked_kernel(
-    place, hid, a0, a1, a2, a3, b0, b1, b2, b3, o0, o1, o2, o3
-):
-    l, x, c, y, h = (place[i] for i in range(5))
-    own, other = (a0, a1, a2, a3), (b0, b1, b2, b3)
-    for e, out in enumerate((o0, o1, o2, o3)):
+def grad_masked_block(place, hid, own, other, col):
+    x, c, y = place[1], place[2], place[3]
+    total = None
+    for k in range(4):
+        tok = lax.rem(x + 16 - y - k - 2 * c, 4)
+        mine, theirs = own[k][col], other[(k + 2) % 4][col]
+        first = jnp.where(c == 0, mine, theirs)
+        second = jnp.where(c == 0, theirs, mine)
+        part = jnp.dot(
+            hid[tok], jnp.concatenate([first, second], axis=1), preferred_element_type=jnp.float32
+        )
+        total = part if total is None else total + part
+    return total
+
+
+def grad_masked_far_kernel(place, hid, a0, a1, a2, a3, b0, b1, b2, b3, out):
+    out[...] = grad_masked_block(place, hid, (a0, a1, a2, a3), (b0, b1, b2, b3), 0).astype(out.dtype)
+
+
+def grad_masked_kernel(place, hid, a0, a1, a2, a3, b0, b1, b2, b3, far, o0, o1, o3):
+    del far
+    l, h = place[0], place[4]
+    for e, out in ((1, o1), (3, o3), (0, o0)):
         col = lax.rem(h + 8 - l - e, 4)
-        total = None
-        for k in range(4):
-            tok = lax.rem(x + 16 - y - k - 2 * c, 4)
-            mine, theirs = own[k][col], other[(k + 2) % 4][col]
-            first = jnp.where(c == 0, mine, theirs)
-            second = jnp.where(c == 0, theirs, mine)
-            part = jnp.dot(
-                hid[tok], jnp.concatenate([first, second], axis=1), preferred_element_type=jnp.float32
-            )
-            total = part if total is None else total + part
-        out[...] = total.astype(out.dtype)
+        out[...] = grad_masked_block(place, hid, (a0, a1, a2, a3), (b0, b1, b2, b3), col).astype(out.dtype)
 
 
 def grad_hidden_kernel(place, m, a0, a1, a2, a3, b0, b1, b2, b3, ahead, out, mt):
@@ -145,17 +152,32 @@
     smem = pl.BlockSpec(memory_space=pltpu.SMEM)
     tall, block = whole(512, 512), whole(4, 512, 128)
     params = pltpu.CompilerParams(vmem_limit_bytes=VMEM)
-    g = pl.pallas_call(
+    piece = pl.BlockSpec((1, 512, 128), lambda i, place: (lax.rem(place[4] + 6 - place[0], 4), 0, 0))
+    far = pl.pallas_call(
+        grad_masked_far_kernel,
+        out_shape=jax.ShapeDtypeStruct((512, 256), jnp.bfloat16),
+        grid_spec=pltpu.PrefetchScalarGridSpec(
+            num_scalar_prefetch=1,
+            grid=(1,),
+            in_specs=[pl.BlockSpec((4, 512, 512), lambda i, place: (0, 0, 0))] + [piece] * 8,
+            out_specs=pl.BlockSpec((512, 256), lambda i, place: (0, 0)),
+        ),
+        compiler_params=params,
+        cost_estimate=pl.CostEstimate(flops=2 * 512 * 512 * 1024, bytes_accessed=3 << 20, transcendentals=0),
+        name="grad_masked_far",
+    )(place, hid_all, *own, *other)
+    near = pl.pallas_call(
         grad_masked_kernel,
         out_shape=[jax.ShapeDtypeStruct((512, 256), jnp.float32)]
-        + [jax.ShapeDtypeStruct((512, 256), jnp.bfloat16)] * 3,
-        grid=(1,),
-        in_specs=[smem, whole(4, 512, 512)] + [block] * 8,
-        out_specs=[whole(512, 256)] * 4,
-        compiler_params=params,
-        cost_estimate=pl.CostEstimate(flops=2 * 512 * 2048 * 1024, bytes_accessed=7 << 20, transcendentals=0),
+        + [jax.ShapeDtypeStruct((512, 256), jnp.bfloat16)] * 2,
+        grid=(1,),
+        in_specs=[smem, whole(4, 512, 512)] + [block] * 8 + [pl.BlockSpec(memory_space=pl.ANY)],
+        out_specs=[whole(512, 256)] * 3,
+        compiler_params=params,
+        cost_estimate=pl.CostEstimate(flops=2 * 512 * 1536 * 1024, bytes_accessed=6 << 20, transcendentals=0),
         name="grad_masked",
-    )(place, hid_all, *own, *other)
+    )(place, hid_all, *own, *other, far)
+    g = [near[0], near[1], far, near[2]]
     with jax.named_scope("grad_masked_sum"):
         got = [shift(g[e], "l", e) for e in (1, 2, 3)]
 
@@ -169,7 +191,7 @@
         compiler_params=params,
         cost_estimate=pl.CostEstimate(flops=2 * 512 * 2048 * 1024, bytes_accessed=7 << 20, transcendentals=0),
         name="grad_hidden",
-    )(place, mt, *own, *other, g[0])
+    )(place, mt, *own, *other, got[1])
     with jax.named_scope("grad_hidden_sum"):
         grad_hidden = lax.psum_scatter(gh.reshape(2048, 512), "y", scatter_dimension=0, tiled=True)
 

time: 184 us -> 182 us (0.989)
  blocking collectives: 41.3 us -> 34.8 us
  Pallas kernels: 17 us -> 20.6 us
    all_to_all x1, blocking collectives: 24.4 us -> 17.8 us  [body(): squares = lax.all_to_all(squares, ('l', 'h'), 0, 0, tiled=True)]
    pallas_call x0 -> x1, Pallas kernels: none -> 4.02 us  [body(): pl.pallas_call(grad_masked_far_kernel, out_shape=jax.ShapeDtypeStruct((51...]
  transfers between devices with their start and end apart: 17 -> 17, of which waited for: 4 -> 4; matrix products, arithmetic and copies ran while one was open for 5% -> 5% of each run, Pallas kernels for 9% -> 11%
where the time goes in v4:
time: 182 us; the launch traced here: 181 us
  starting transfers between devices  76 us (42%)
  blocking collectives  34.8 us (19%)
  waiting for transfers between devices  21.6 us (12%)
  Pallas kernels  20.6 us (11%)
  between operations  15.2 us (8%)
  local copies, waits for them, and re-layouts  4.71 us (3%)
  other arithmetic  4.05 us (2%)
  matrix products  3.62 us (2%)
    ppermute x6, starting transfers between devices, shift(): return lax.ppermute(value, axis, [(i, (i + by) % 4) for i in range(4)])  36 us
    ppermute x4, starting transfers between devices, body(): lax.ppermute(up, ('y', 'x', 'c'), [((b * 4 + a) * 2 + core, (a * 4 + (a +...  17.8 us
    ppermute x4, starting transfers between devices, body(): other = [lax.ppermute(u, 'c', [(0, 1), (1, 0)]) for u in own]  17.8 us
    all_to_all x1, blocking collectives, body(): squares = lax.all_to_all(squares, ('l', 'h'), 0, 0, tiled=True)  17.8 us
    all_to_all x1, blocking collectives, body(): squares = lax.all_to_all(squares, ('x', 'y', 'c'), 0, 0, tiled=True)  17.1 us
    ppermute x4, waiting for transfers between devices, body(): lax.ppermute(up, ('y', 'x', 'c'), [((b * 4 + a) * 2 + core, (a * 4 + (a +...  10.5 us
    ppermute x6, waiting for transfers between devices, shift(): return lax.ppermute(value, axis, [(i, (i + by) % 4) for i in range(4)])  10 us
    pallas_call x1, Pallas kernels, body(): pl.pallas_call(grad_hidden_kernel, out_shape=jax.ShapeDtypeStruct((4, 512...  6.16 us
  transfers between devices with their start and end apart: 17, of which 4 were waited for; matrix products, arithmetic and copies ran while one was open for 5% of the time, Pallas kernels for 11%

profile of v4, /device:TPU:1, one launch (start us, length us, event | category | flops | bytes accessed | tf_op | source)
XLA Modules:
  0.0 180.6 jit_solution(6040344169105759320)
XLA Ops:
  7.2 0.0 copy-start
  7.2 0.0 all-gather.3.cloned.1.call-start
  7.2 16.4 %collective-permute-start.1 = (bf16[512,128]{1,0:T(8,128)(2,1)}, bf16[512,128]{1,0:T(8,128)(2,1)S(1)}, u32[]{:S(2)}, u32[]{:S(2)}) collective-permute-start(bf16[512,128]{1,0:T(8,128)(2,1)} %r0.1), channel_id=1, source_target_pairs={{0,4},{2,6},{4,0},{6,2},{1,5},{3,7},{5,1},{7,3},{8,12},{10,14},{12... | collective-permute-start | bytes 393224 | tf_op jit(solution)/shard_map/up/ppermute | solution.py:87
  23.7 4.0 %collective-permute-start = (bf16[512,128]{1,0:T(8,128)(2,1)}, bf16[512,128]{1,0:T(8,128)(2,1)S(1)}, u32[]{:S(2)}, u32[]{:S(2)}) collective-permute-start(bf16[512,128]{1,0:T(8,128)(2,1)} %r0.1), channel_id=1, source_target_pairs={{0,2},{2,4},{4,6},{6,0},{1,3},{3,5},{5,7},{7,1},{8,10},{10,12},{12... | collective-permute-start | bytes 393224 | tf_op jit(solution)/shard_map/up/ppermute | solution.py:87
  27.7 5.2 %collective-permute-start.2 = (bf16[512,128]{1,0:T(8,128)(2,1)}, bf16[512,128]{1,0:T(8,128)(2,1)S(1)}, u32[]{:S(2)}, u32[]{:S(2)}) collective-permute-start(bf16[512,128]{1,0:T(8,128)(2,1)} %r0.1), channel_id=1, source_target_pairs={{0,6},{2,0},{4,2},{6,4},{1,7},{3,1},{5,3},{7,5},{8,14},{10,8},{12,... | collective-permute-start | bytes 393224 | tf_op jit(solution)/shard_map/up/ppermute | solution.py:87
  32.9 2.3 %convolution_convert_fusion = bf16[512,512]{1,0:T(8,128)(2,1)} fusion(bf16[512,512]{1,0:T(8,128)(2,1)} %constant.34.clone, bf16[512,512]{1,0:T(8,128)(2,1)S(1)} %copy-done), kind=kOutput, calls=%fused_computation | convolution fusion | flops 268697600 | bytes 1572864 | tf_op jit(solution)/shard_map/dot_general | solution.py:115
  35.2 0.0 all-gather.3.cloned.1.call-update
  35.3 0.1 bitcast_reduce_fusion
  35.4 0.2 fusion.3
  35.5 0.7 copy-done.3
  36.2 0.1 copy-done.10
  36.3 0.3 convolution_convert_fusion.1.w
  36.6 0.0 copy-start.14
  36.6 0.0 copy-start.13
  36.7 1.0 convert_convert_fusion
  37.7 0.2 fusion.8
  38.0 0.3 convolution_add_fusion.2
  38.2 0.3 convolution_add_fusion.1
  38.5 0.1 copy-done.11
  38.6 0.2 fusion
  38.9 1.0 broadcast_in_dim.4
  39.9 4.2 %all-to-all-start = ((bf16[4,256,512]{2,1,0:T(8,128)(2,1)}), bf16[4,256,512]{2,1,0:T(8,128)(2,1)}, u32[]{:S(2)}, u32[]{:S(2)}) async-start(bf16[4,256,512]{2,1,0:T(8,128)(2,1)} %broadcast_in_dim.4), calls=%async_computation | async-start | bytes 2097152 | tf_op jit(solution)/shard_map/masked/all_to_all | solution.py:133
  44.2 0.0 reduce-scatter.2.cloned.1.call-start
  44.2 0.0 collective-permute-done.1.r2
  44.2 0.0 collective-permute-done.r1
  44.3 3.7 %collective-permute-done.2.r3 = bf16[512,128]{1,0:T(8,128)(2,1)S(1)} collective-permute-done((bf16[512,128]{1,0:T(8,128)(2,1)}, bf16[512,128]{1,0:T(8,128)(2,1)S(1)}, u32[]{:S(2)}, u32[]{:S(2)}) %collective-permute-start.2) | collective-permute-done | bytes 131104 | tf_op jit(solution)/shard_map/up/ppermute | solution.py:87
  48.0 0.6 copy-done.20
  48.6 2.0 %stack_upstream.1 = bf16[4,512,128]{2,1,0:T(8,128)(2,1)} custom-call(bf16[512,128]{1,0:T(8,128)(2,1)} %r0.1, bf16[512,128]{1,0:T(8,128)(2,1)} %copy-done.19, bf16[512,128]{1,0:T(8,128)(2,1)} %copy-done.18, bf16[512,128]{1,0:T(8,128)(2,1)} %copy-done.20), custom_call_target="tpu_custom_call" | custom-call | flops 999999995904 | bytes 1073741824 | tf_op jit(solution)/shard_map/stack_upstream/pallas_call | solution.py:100
  50.6 3.0 %collective-permute-start.6 = (bf16[4,512,128]{2,1,0:T(8,128)(2,1)}, bf16[4,512,128]{2,1,0:T(8,128)(2,1)S(1)}, u32[]{:S(2)}, u32[]{:S(2)}) collective-permute-start(bf16[4,512,128]{2,1,0:T(8,128)(2,1)} %stack_upstream.1), channel_id=1, source_target_pairs={{0,24},{1,9},{8,128},{9,145},{16,264},{17,281},{24,400},{25,385},{... | collective-permute-start | bytes 1572872 | tf_op jit(solution)/shard_map/upstream_xy/ppermute | solution.py:137
  53.7 1.7 collective-permute-start.5
  55.4 6.1 %collective-permute-start.4 = (bf16[4,512,128]{2,1,0:T(8,128)(2,1)}, bf16[4,512,128]{2,1,0:T(8,128)(2,1)S(1)}, u32[]{:S(2)}, u32[]{:S(2)}) collective-permute-start(bf16[4,512,128]{2,1,0:T(8,128)(2,1)} %stack_upstream.1), channel_id=1, source_target_pairs={{0,8},{1,25},{8,144},{9,129},{16,280},{17,265},{24,384},{25,401},{... | collective-permute-start | bytes 1572872 | tf_op jit(solution)/shard_map/upstream_xy/ppermute | solution.py:137
  61.5 7.0 %collective-permute-start.3 = (bf16[4,512,128]{2,1,0:T(8,128)(2,1)}, bf16[4,512,128]{2,1,0:T(8,128)(2,1)S(1)}, u32[]{:S(2)}, u32[]{:S(2)}) collective-permute-start(bf16[4,512,128]{2,1,0:T(8,128)(2,1)} %stack_upstream.1), channel_id=1, source_target_pairs={{0,0},{1,17},{8,136},{9,153},{16,272},{17,257},{24,408},{25,393},{... | collective-permute-start | bytes 1572872 | tf_op jit(solution)/shard_map/upstream_xy/ppermute | solution.py:137
  68.5 10.5 %collective-permute-done.6.a3 = bf16[4,512,128]{2,1,0:T(8,128)(2,1)S(1)} collective-permute-done((bf16[4,512,128]{2,1,0:T(8,128)(2,1)}, bf16[4,512,128]{2,1,0:T(8,128)(2,1)S(1)}, u32[]{:S(2)}, u32[]{:S(2)}) %collective-permute-start.6) | collective-permute-done | bytes 524320 | tf_op jit(solution)/shard_map/upstream_xy/ppermute | solution.py:137
  79.0 9.8 %collective-permute-start.10 = (bf16[4,512,128]{2,1,0:T(8,128)(2,1)S(1)}, bf16[4,512,128]{2,1,0:T(8,128)(2,1)S(1)}, u32[]{:S(2)}, u32[]{:S(2)}) collective-permute-start(bf16[4,512,128]{2,1,0:T(8,128)(2,1)S(1)} %collective-permute-done.6.a3), channel_id=1, source_target_pairs={{0,1},{1,0},{2,3},{3,2},{4,5},{5,4},{6,7},{7,6},{8,9},{9,8},{10,11... | collective-permute-start | bytes 1572872 | tf_op jit(solution)/shard_map/upstream_core/ppermute | solution.py:150
  88.8 0.0 collective-permute-done.5.a2
  88.8 3.7 %collective-permute-start.9 = (bf16[4,512,128]{2,1,0:T(8,128)(2,1)S(1)}, bf16[4,512,128]{2,1,0:T(8,128)(2,1)}, u32[]{:S(2)}, u32[]{:S(2)}) collective-permute-start(bf16[4,512,128]{2,1,0:T(8,128)(2,1)S(1)} %collective-permute-done.5.a2), channel_id=1, source_target_pairs={{0,1},{1,0},{2,3},{3,2},{4,5},{5,4},{6,7},{7,6},{8,9},{9,8},{10,11... | collective-permute-start | bytes 1572872 | tf_op jit(solution)/shard_map/upstream_core/ppermute | solution.py:150
  92.5 0.0 collective-permute-done.4.a1
  92.6 1.9 %collective-permute-start.8 = (bf16[4,512,128]{2,1,0:T(8,128)(2,1)S(1)}, bf16[4,512,128]{2,1,0:T(8,128)(2,1)}, u32[]{:S(2)}, u32[]{:S(2)}) collective-permute-start(bf16[4,512,128]{2,1,0:T(8,128)(2,1)S(1)} %collective-permute-done.4.a1), channel_id=1, source_target_pairs={{0,1},{1,0},{2,3},{3,2},{4,5},{5,4},{6,7},{7,6},{8,9},{9,8},{10,11... | collective-permute-start | bytes 1572872 | tf_op jit(solution)/shard_map/upstream_core/ppermute | solution.py:150
  94.5 0.0 collective-permute-done.3.a0
  94.5 0.0 copy-start.7
  94.5 2.4 %collective-permute-start.7 = (bf16[4,512,128]{2,1,0:T(8,128)(2,1)S(1)}, bf16[4,512,128]{2,1,0:T(8,128)(2,1)}, u32[]{:S(2)}, u32[]{:S(2)}) collective-permute-start(bf16[4,512,128]{2,1,0:T(8,128)(2,1)S(1)} %collective-permute-done.3.a0), channel_id=1, source_target_pairs={{0,1},{1,0},{2,3},{3,2},{4,5},{5,4},{6,7},{7,6},{8,9},{9,8},{10,11... | collective-permute-start | bytes 1572872 | tf_op jit(solution)/shard_map/upstream_core/ppermute | solution.py:150
  96.9 0.6 stack.23.place
  97.5 0.0 collective-permute-done.10.b3
  97.5 0.0 collective-permute-done.9.b2
  97.5 0.0 collective-permute-done.8.b1
  97.5 1.0 collective-permute-done.7.b0
  98.6 4.0 %grad_masked_far.1.far = bf16[512,256]{1,0:T(8,128)(2,1)} custom-call(s32[5]{0:T(128)} %stack.23.place, bf16[4,512,512]{2,1,0:T(8,128)(2,1)} %bitcast.51, bf16[4,512,128]{2,1,0:T(8,128)(2,1)} %copy-done.7, bf16[4,512,128]{2,1,0:T(8,128)(2,1)} %copy-done.6, bf16[4,512,128]{2,1,0:T(8,128)(2,1)} %copy-done.5, bf16[4,512,128]{2,1,0:T(8,128)(2,1)} %copy-done.4, ...), custom_call_target="tpu_custom_call" | custom-call | flops 536870912 | bytes 3145728 | tf_op jit(solution)/shard_map/grad_masked_far/pallas_call | solution.py:156
  102.6 3.4 %collective-permute-start.11 = (bf16[512,256]{1,0:T(8,128)(2,1)}, bf16[512,256]{1,0:T(8,128)(2,1)S(1)}, u32[]{:S(2)}, u32[]{:S(2)}) collective-permute-start(bf16[512,256]{1,0:T(8,128)(2,1)} %grad_masked_far.1.far), channel_id=1, source_target_pairs={{0,64},{32,96},{64,0},{96,32},{1,65},{33,97},{65,1},{97,33},{2,66}... | collective-permute-start | bytes 786440 | tf_op jit(solution)/shard_map/grad_masked_sum/ppermute | solution.py:87
  106.0 5.5 %grad_masked.1 = (f32[512,256]{1,0:T(8,128)}, bf16[512,256]{1,0:T(8,128)(2,1)}, bf16[512,256]{1,0:T(8,128)(2,1)}) custom-call(s32[5]{0:T(128)} %stack.23.place, bf16[4,512,512]{2,1,0:T(8,128)(2,1)} %bitcast.52, bf16[4,512,128]{2,1,0:T(8,128)(2,1)} %copy-done.7, bf16[4,512,128]{2,1,0:T(8,128)(2,1)} %copy-done.6, bf16[4,512,128]{2,1,0:T(8,128)(2,1)} %copy-done.5, ...), custom_call_target="tpu_custom_call" | custom-call | flops 1610612736 | bytes 6291456 | tf_op jit(solution)/shard_map/grad_masked/pallas_call | solution.py:169
  111.5 3.2 %collective-permute-start.12 = (bf16[512,256]{1,0:T(8,128)(2,1)}, bf16[512,256]{1,0:T(8,128)(2,1)S(1)}, u32[]{:S(2)}, u32[]{:S(2)}) collective-permute-start(bf16[512,256]{1,0:T(8,128)(2,1)} %get-tuple-element.8), channel_id=1, source_target_pairs={{0,32},{32,64},{64,96},{96,0},{1,33},{33,65},{65,97},{97,1},{2,34}... | collective-permute-start | bytes 786440 | tf_op jit(solution)/shard_map/grad_masked_sum/ppermute | solution.py:87
  114.7 3.9 %collective-permute-start.13 = (bf16[512,256]{1,0:T(8,128)(2,1)}, bf16[512,256]{1,0:T(8,128)(2,1)S(1)}, u32[]{:S(2)}, u32[]{:S(2)}) collective-permute-start(bf16[512,256]{1,0:T(8,128)(2,1)} %get-tuple-element.9), channel_id=1, source_target_pairs={{0,96},{32,0},{64,32},{96,64},{1,97},{33,1},{65,33},{97,65},{2,98}... | collective-permute-start | bytes 786440 | tf_op jit(solution)/shard_map/grad_masked_sum/ppermute | solution.py:87
  118.6 0.0 all-to-all-done.m
  118.6 6.3 %collective-permute-done.11.ahead.g2 = bf16[512,256]{1,0:T(8,128)(2,1)S(1)} collective-permute-done((bf16[512,256]{1,0:T(8,128)(2,1)}, bf16[512,256]{1,0:T(8,128)(2,1)S(1)}, u32[]{:S(2)}, u32[]{:S(2)}) %collective-permute-start.11) | collective-permute-done | bytes 262176 | tf_op jit(solution)/shard_map/grad_masked_sum/ppermute | solution.py:87
  124.9 0.7 copy-done.15
  125.6 6.2 %grad_hidden.1 = bf16[4,512,512]{2,1,0:T(8,128)(2,1)} custom-call(s32[5]{0:T(128)} %stack.23.place, bf16[4,256,512]{2,1,0:T(8,128)(2,1)} %all-to-all-done.m, bf16[4,512,128]{2,1,0:T(8,128)(2,1)} %copy-done.7, bf16[4,512,128]{2,1,0:T(8,128)(2,1)} %copy-done.6, bf16[4,512,128]{2,1,0:T(8,128)(2,1)} %copy-done.5, bf16[4,512,128]{2,1,0:T(8,128)(2,1)} %copy-done.4, ...), custom_call_target="tpu_custom_call" | custom-call | flops 2147483648 | bytes 7340032 | tf_op jit(solution)/shard_map/grad_hidden/pallas_call | solution.py:184
  131.8 0.0 reduce-scatter.2.cloned.1.call-update
  131.8 0.0 collective-permute-done.13.g3
  131.9 0.7 copy-done.16
  132.5 0.1 copy-done.17
  132.6 2.9 %grad_logits.1 = (f32[6,128,256]{2,1,0:T(8,128)}, f32[16,128]{1,0:T(8,128)}) custom-call(f32[512,256]{1,0:T(8,128)} %get-tuple-element.7.g0.ahead, bf16[512,256]{1,0:T(8,128)(2,1)} %copy-done.16, bf16[512,256]{1,0:T(8,128)(2,1)} %copy-done.15, bf16[512,256]{1,0:T(8,128)(2,1)} %copy-done.17, bf16[512,256]{1,0:T(8,128)(2,1)} %copy-done.9, ...), custom_call_target="tpu_custom_call" | custom-call | flops 999999995904 | bytes 1073741824 | tf_op jit(solution)/shard_map/grad_logits/pallas_call | solution.py:198
  135.5 17.8 %all_to_all.20 = f32[16,1,128]{2,1,0:T(1,128)S(1)} all-to-all(f32[16,1,128]{2,1,0:T(1,128)} %bitcast.55), channel_id=1, replica_groups=mesh['y'=4,'l'=4,'x'=4,'h'=4,'c'=2] {'l','h'}, dimensions={0} | all-to-all | bytes 16384 | tf_op jit(solution)/shard_map/mean_square/all_to_all | solution.py:212
  153.3 17.1 %all_to_all.21 = f32[32,1,128]{2,1,0:T(1,128)S(1)} all-to-all(f32[32,1,128]{2,1,0:T(1,128)S(1)} %broadcast_in_dim.5), channel_id=1, replica_groups=mesh['y'=4,'l'=4,'x'=4,'h'=4,'c'=2] {'x','y','c'}, dimensions={0} | all-to-all | bytes 32768 | tf_op jit(solution)/shard_map/mean_square/all_to_all | solution.py:214
  170.4 0.6 reduce_sum.29
  171.7 2.1 %multiply_bitcast_fusion = f32[128,6,256]{2,0,1:T(8,128)} fusion(f32[6,128,256]{2,1,0:T(8,128)} %get-tuple-element.10, f32[]{:T(128)S(6)} %rsqrt.3), kind=kLoop, calls=%fused_computation.9 | loop fusion | flops 196608 | bytes 1572868 | tf_op jit(solution)/shard_map/transpose | solution.py:216
  (36 shorter events, 0.1 us)
Async XLA Ops:
  7.2 25.7 %copy-start = (bf16[512,512]{1,0:T(8,128)(2,1)S(1)}, bf16[512,512]{1,0:T(8,128)(2,1)}, u32[]{:S(2)}) copy-start(bf16[512,512]{1,0:T(8,128)(2,1)} %param.6) | copy-start | bytes 1572868
  7.2 28.1 %copy-start.2 = (f32[128,6,256]{2,0,1:T(8,128)S(1)}, f32[128,6,256]{2,0,1:T(8,128)}, u32[]{:S(2)}) copy-start(f32[128,6,256]{2,0,1:T(8,128)} %param.10) | copy-start | bytes 2359300
  7.2 28.1 %copy-start.1 = (f32[128,6,256]{2,0,1:T(8,128)S(1)}, f32[128,6,256]{2,0,1:T(8,128)}, u32[]{:S(2)}) copy-start(f32[128,6,256]{2,0,1:T(8,128)} %param.9) | copy-start | bytes 2359300
  7.2 91.4 %all-gather.3.cloned.1.call-start = ((), (), s32[]{:S(2)}) async-start(), calls=%async_computation.5 | async-start | bytes 2621440 | tf_op jit(solution)/shard_map/hidden/all_gather | solution.py:119
  7.2 37.0 %collective-permute-start.1 = (bf16[512,128]{1,0:T(8,128)(2,1)}, bf16[512,128]{1,0:T(8,128)(2,1)S(1)}, u32[]{:S(2)}, u32[]{:S(2)}) collective-permute-start(bf16[512,128]{1,0:T(8,128)(2,1)} %r0.1), channel_id=1, source_target_pairs={{0,4},{2,6},{4,0},{6,2},{1,5},{3,7},{5,1},{7,3},{8,12},{10,14},{12... | collective-permute-start | bytes 393224 | tf_op jit(solution)/shard_map/up/ppermute | solution.py:87
  23.7 20.6 %collective-permute-start = (bf16[512,128]{1,0:T(8,128)(2,1)}, bf16[512,128]{1,0:T(8,128)(2,1)S(1)}, u32[]{:S(2)}, u32[]{:S(2)}) collective-permute-start(bf16[512,128]{1,0:T(8,128)(2,1)} %r0.1), channel_id=1, source_target_pairs={{0,2},{2,4},{4,6},{6,0},{1,3},{3,5},{5,7},{7,1},{8,10},{10,12},{12... | collective-permute-start | bytes 393224 | tf_op jit(solution)/shard_map/up/ppermute | solution.py:87
  27.7 20.3 %collective-permute-start.2 = (bf16[512,128]{1,0:T(8,128)(2,1)}, bf16[512,128]{1,0:T(8,128)(2,1)S(1)}, u32[]{:S(2)}, u32[]{:S(2)}) collective-permute-start(bf16[512,128]{1,0:T(8,128)(2,1)} %r0.1), channel_id=1, source_target_pairs={{0,6},{2,0},{4,2},{6,4},{1,7},{3,1},{5,3},{7,5},{8,14},{10,8},{12,... | collective-permute-start | bytes 393224 | tf_op jit(solution)/shard_map/up/ppermute | solution.py:87
  35.2 1.0 copy-start.3
  35.2 1.1 copy-start.10
  36.3 1.4 copy-start.12
  36.6 1.9 %copy-start.9 = (bf16[512,256]{1,0:T(8,128)(2,1)}, bf16[512,256]{1,0:T(8,128)(2,1)S(1)}, u32[]{:S(2)}) copy-start(bf16[512,256]{1,0:T(8,128)(2,1)S(1)} %convolution_convert_fusion.1.w) | copy-start | bytes 786436
  36.6 1.3 copy-start.14
  36.6 1.6 copy-start.13
  37.7 0.9 copy-start.11
  39.9 78.7 %all-to-all-start = ((bf16[4,256,512]{2,1,0:T(8,128)(2,1)}), bf16[4,256,512]{2,1,0:T(8,128)(2,1)}, u32[]{:S(2)}, u32[]{:S(2)}) async-start(bf16[4,256,512]{2,1,0:T(8,128)(2,1)} %broadcast_in_dim.4), calls=%async_computation | async-start | bytes 2097152 | tf_op jit(solution)/shard_map/masked/all_to_all | solution.py:133
  44.2 129.6 %reduce-scatter.2.cloned.1.call-start = ((), (), s32[]{:S(2)}) async-start(), calls=%async_computation.4 | async-start | bytes 2621440 | tf_op jit(solution)/shard_map/grad_hidden_sum/reduce_scatter | solution.py:196
  44.2 3.7 %copy-start.18 = (bf16[512,128]{1,0:T(8,128)(2,1)}, bf16[512,128]{1,0:T(8,128)(2,1)S(1)}, u32[]{:S(2)}) copy-start(bf16[512,128]{1,0:T(8,128)(2,1)S(1)} %collective-permute-done.1.r2) | copy-start | bytes 393220
  44.2 3.7 %copy-start.19 = (bf16[512,128]{1,0:T(8,128)(2,1)}, bf16[512,128]{1,0:T(8,128)(2,1)S(1)}, u32[]{:S(2)}) copy-start(bf16[512,128]{1,0:T(8,128)(2,1)S(1)} %collective-permute-done.r1) | copy-start | bytes 393220
  48.0 0.6 copy-start.20
  50.6 28.4 %collective-permute-start.6 = (bf16[4,512,128]{2,1,0:T(8,128)(2,1)}, bf16[4,512,128]{2,1,0:T(8,128)(2,1)S(1)}, u32[]{:S(2)}, u32[]{:S(2)}) collective-permute-start(bf16[4,512,128]{2,1,0:T(8,128)(2,1)} %stack_upstream.1), channel_id=1, source_target_pairs={{0,24},{1,9},{8,128},{9,145},{16,264},{17,281},{24,400},{25,385},{... | collective-permute-start | bytes 1572872 | tf_op jit(solution)/shard_map/upstream_xy/ppermute | solution.py:137
  53.7 35.1 %collective-permute-start.5 = (bf16[4,512,128]{2,1,0:T(8,128)(2,1)}, bf16[4,512,128]{2,1,0:T(8,128)(2,1)S(1)}, u32[]{:S(2)}, u32[]{:S(2)}) collective-permute-start(bf16[4,512,128]{2,1,0:T(8,128)(2,1)} %stack_upstream.1), channel_id=1, source_target_pairs={{0,16},{1,1},{8,152},{9,137},{16,256},{17,273},{24,392},{25,409},{... | collective-permute-start | bytes 1572872 | tf_op jit(solution)/shard_map/upstream_xy/ppermute | solution.py:137
  55.4 37.2 %collective-permute-start.4 = (bf16[4,512,128]{2,1,0:T(8,128)(2,1)}, bf16[4,512,128]{2,1,0:T(8,128)(2,1)S(1)}, u32[]{:S(2)}, u32[]{:S(2)}) collective-permute-start(bf16[4,512,128]{2,1,0:T(8,128)(2,1)} %stack_upstream.1), channel_id=1, source_target_pairs={{0,8},{1,25},{8,144},{9,129},{16,280},{17,265},{24,384},{25,401},{... | collective-permute-start | bytes 1572872 | tf_op jit(solution)/shard_map/upstream_xy/ppermute | solution.py:137
  61.5 33.0 %collective-permute-start.3 = (bf16[4,512,128]{2,1,0:T(8,128)(2,1)}, bf16[4,512,128]{2,1,0:T(8,128)(2,1)S(1)}, u32[]{:S(2)}, u32[]{:S(2)}) collective-permute-start(bf16[4,512,128]{2,1,0:T(8,128)(2,1)} %stack_upstream.1), channel_id=1, source_target_pairs={{0,0},{1,17},{8,136},{9,153},{16,272},{17,257},{24,408},{25,393},{... | collective-permute-start | bytes 1572872 | tf_op jit(solution)/shard_map/upstream_xy/ppermute | solution.py:137
  79.0 19.6 %copy-start.4 = (bf16[4,512,128]{2,1,0:T(8,128)(2,1)}, bf16[4,512,128]{2,1,0:T(8,128)(2,1)S(1)}, u32[]{:S(2)}) copy-start(bf16[4,512,128]{2,1,0:T(8,128)(2,1)S(1)} %collective-permute-done.6.a3) | copy-start | bytes 1572868
  79.0 18.5 %collective-permute-start.10 = (bf16[4,512,128]{2,1,0:T(8,128)(2,1)S(1)}, bf16[4,512,128]{2,1,0:T(8,128)(2,1)S(1)}, u32[]{:S(2)}, u32[]{:S(2)}) collective-permute-start(bf16[4,512,128]{2,1,0:T(8,128)(2,1)S(1)} %collective-permute-done.6.a3), channel_id=1, source_target_pairs={{0,1},{1,0},{2,3},{3,2},{4,5},{5,4},{6,7},{7,6},{8,9},{9,8},{10,11... | collective-permute-start | bytes 1572872 | tf_op jit(solution)/shard_map/upstream_core/ppermute | solution.py:150
  88.8 9.8 %copy-start.5 = (bf16[4,512,128]{2,1,0:T(8,128)(2,1)}, bf16[4,512,128]{2,1,0:T(8,128)(2,1)S(1)}, u32[]{:S(2)}) copy-start(bf16[4,512,128]{2,1,0:T(8,128)(2,1)S(1)} %collective-permute-done.5.a2) | copy-start | bytes 1572868
  88.8 8.7 %collective-permute-start.9 = (bf16[4,512,128]{2,1,0:T(8,128)(2,1)S(1)}, bf16[4,512,128]{2,1,0:T(8,128)(2,1)}, u32[]{:S(2)}, u32[]{:S(2)}) collective-permute-start(bf16[4,512,128]{2,1,0:T(8,128)(2,1)S(1)} %collective-permute-done.5.a2), channel_id=1, source_target_pairs={{0,1},{1,0},{2,3},{3,2},{4,5},{5,4},{6,7},{7,6},{8,9},{9,8},{10,11... | collective-permute-start | bytes 1572872 | tf_op jit(solution)/shard_map/upstream_core/ppermute | solution.py:150
  92.6 6.0 %copy-start.6 = (bf16[4,512,128]{2,1,0:T(8,128)(2,1)}, bf16[4,512,128]{2,1,0:T(8,128)(2,1)S(1)}, u32[]{:S(2)}) copy-start(bf16[4,512,128]{2,1,0:T(8,128)(2,1)S(1)} %collective-permute-done.4.a1) | copy-start | bytes 1572868
  92.6 5.0 %collective-permute-start.8 = (bf16[4,512,128]{2,1,0:T(8,128)(2,1)S(1)}, bf16[4,512,128]{2,1,0:T(8,128)(2,1)}, u32[]{:S(2)}, u32[]{:S(2)}) collective-permute-start(bf16[4,512,128]{2,1,0:T(8,128)(2,1)S(1)} %collective-permute-done.4.a1), channel_id=1, source_target_pairs={{0,1},{1,0},{2,3},{3,2},{4,5},{5,4},{6,7},{7,6},{8,9},{9,8},{10,11... | collective-permute-start | bytes 1572872 | tf_op jit(solution)/shard_map/upstream_core/ppermute | solution.py:150
  94.5 4.1 %copy-start.7 = (bf16[4,512,128]{2,1,0:T(8,128)(2,1)}, bf16[4,512,128]{2,1,0:T(8,128)(2,1)S(1)}, u32[]{:S(2)}) copy-start(bf16[4,512,128]{2,1,0:T(8,128)(2,1)S(1)} %collective-permute-done.3.a0) | copy-start | bytes 1572868
  94.5 4.1 %collective-permute-start.7 = (bf16[4,512,128]{2,1,0:T(8,128)(2,1)S(1)}, bf16[4,512,128]{2,1,0:T(8,128)(2,1)}, u32[]{:S(2)}, u32[]{:S(2)}) collective-permute-start(bf16[4,512,128]{2,1,0:T(8,128)(2,1)S(1)} %collective-permute-done.3.a0), channel_id=1, source_target_pairs={{0,1},{1,0},{2,3},{3,2},{4,5},{5,4},{6,7},{7,6},{8,9},{9,8},{10,11... | collective-permute-start | bytes 1572872 | tf_op jit(solution)/shard_map/upstream_core/ppermute | solution.py:150
  97.5 1.1 copy-start.8
  102.6 22.3 %collective-permute-start.11 = (bf16[512,256]{1,0:T(8,128)(2,1)}, bf16[512,256]{1,0:T(8,128)(2,1)S(1)}, u32[]{:S(2)}, u32[]{:S(2)}) collective-permute-start(bf16[512,256]{1,0:T(8,128)(2,1)} %grad_masked_far.1.far), channel_id=1, source_target_pairs={{0,64},{32,96},{64,0},{96,32},{1,65},{33,97},{65,1},{97,33},{2,66}... | collective-permute-start | bytes 786440 | tf_op jit(solution)/shard_map/grad_masked_sum/ppermute | solution.py:87
  111.5 20.3 %collective-permute-start.12 = (bf16[512,256]{1,0:T(8,128)(2,1)}, bf16[512,256]{1,0:T(8,128)(2,1)S(1)}, u32[]{:S(2)}, u32[]{:S(2)}) collective-permute-start(bf16[512,256]{1,0:T(8,128)(2,1)} %get-tuple-element.8), channel_id=1, source_target_pairs={{0,32},{32,64},{64,96},{96,0},{1,33},{33,65},{65,97},{97,1},{2,34}... | collective-permute-start | bytes 786440 | tf_op jit(solution)/shard_map/grad_masked_sum/ppermute | solution.py:87
  114.7 17.1 %collective-permute-start.13 = (bf16[512,256]{1,0:T(8,128)(2,1)}, bf16[512,256]{1,0:T(8,128)(2,1)S(1)}, u32[]{:S(2)}, u32[]{:S(2)}) collective-permute-start(bf16[512,256]{1,0:T(8,128)(2,1)} %get-tuple-element.9), channel_id=1, source_target_pairs={{0,96},{32,0},{64,32},{96,64},{1,97},{33,1},{65,33},{97,65},{2,98}... | collective-permute-start | bytes 786440 | tf_op jit(solution)/shard_map/grad_masked_sum/ppermute | solution.py:87
  124.9 0.7 copy-start.15
  131.8 0.7 copy-start.16
  131.9 0.8 copy-start.17
Sparse Core Ops, SparseCore 0:
  35.4 54.1 all-gather.2
  131.9 34.6 reduce-scatter.1

commit v5 on v4

--- a/solution.py
+++ b/solution.py
@@ -20,7 +20,7 @@
     x, c, y = place[1], place[2], place[3]
     total = None
     for k in range(4):
-        tok = lax.rem(x + 16 - y - k - 2 * c, 4)
+        tok = lax.rem(x + 16 - 2 * y - k - 2 * c, 4)
         mine, theirs = own[k][col], other[(k + 2) % 4][col]
         first = jnp.where(c == 0, mine, theirs)
         second = jnp.where(c == 0, theirs, mine)
@@ -50,7 +50,7 @@
     for d in range(4):
         mt[256 * d : 256 * d + 256, :] = m[lax.rem(h + 4 - d, 4)]
     for k in range(4):
-        tok = lax.rem(x + 16 - y - k - 2 * c, 4)
+        tok = lax.rem(x + 16 - 2 * y - k - 2 * c, 4)
         pieces = []
         for d in range(4):
             mine, theirs = own[k][d], other[(k + 2) % 4][d]
@@ -60,15 +60,13 @@
         ).astype(out.dtype)
 
 
-def grad_logits_kernel(g0, g1, g2, g3, w, probs, ahead, out, squares):
-    del ahead
+def grad_logits_kernel(g0, g1, g3, w, probs, out, squares):
     prod = []
     for j in range(4):
         rows = pl.ds(128 * j, 128)
         total = (
             g0[rows, :]
             + g1[rows, :].astype(jnp.float32)
-            + g2[rows, :].astype(jnp.float32)
             + g3[rows, :].astype(jnp.float32)
         )
         prod.append(total * w[rows, :].astype(jnp.float32))
@@ -132,13 +130,14 @@
     with jax.named_scope("masked"):
         mt = lax.all_to_all(jnp.broadcast_to(masked_t[None], (4, 256, 512)), "l", 0, 0)
 
+    up, place = lax.optimization_barrier((up, place))
     with jax.named_scope("upstream_xy"):
         own = [
             lax.ppermute(
                 up,
                 ("y", "x", "c"),
                 [
-                    ((b * 4 + a) * 2 + core, (a * 4 + (a + b + k + 2 * core) % 4) * 2 + core)
+                    ((b * 4 + a) * 2 + core, (a * 4 + (2 * a + b + k + 2 * core) % 4) * 2 + core)
                     for b in range(4)
                     for a in range(4)
                     for core in range(2)
@@ -191,10 +190,11 @@
         compiler_params=params,
         cost_estimate=pl.CostEstimate(flops=2 * 512 * 2048 * 1024, bytes_accessed=7 << 20, transcendentals=0),
         name="grad_hidden",
-    )(place, mt, *own, *other, got[1])
+    )(place, mt, *own, *other, g[0])
     with jax.named_scope("grad_hidden_sum"):
         grad_hidden = lax.psum_scatter(gh.reshape(2048, 512), "y", scatter_dimension=0, tiled=True)
 
+    part = g[0] + got[1].astype(jnp.float32)
     grad_logits, squares = pl.pallas_call(
         grad_logits_kernel,
         out_shape=[
@@ -202,12 +202,12 @@
             jax.ShapeDtypeStruct((16, 128), jnp.float32),
         ],
         grid=(1,),
-        in_specs=[whole(512, 256)] * 5 + [whole(6, 128, 256), pl.BlockSpec(memory_space=pl.ANY)],
+        in_specs=[whole(512, 256)] * 4 + [whole(6, 128, 256)],
         out_specs=[whole(6, 128, 256), whole(16, 128)],
         compiler_params=params,
         cost_estimate=pl.CostEstimate(flops=10**12, bytes_accessed=1 << 30, transcendentals=0),
         name="grad_logits",
-    )(g[0], *got, weight, probs, g[0])
+    )(part, got[0], got[2], weight, probs)
     with jax.named_scope("mean_square"):
         squares = lax.all_to_all(squares, ("l", "h"), 0, 0, tiled=True)
         squares = jnp.broadcast_to(jnp.sum(squares, axis=0, keepdims=True), (32, 128))

time: 182 us -> 180 us (0.989)
  starting transfers between devices: 76 us -> 68.7 us
  waiting for transfers between devices: 21.6 us -> 24.1 us
  local copies, waits for them, and re-layouts: 4.71 us -> 6.71 us
    ppermute x4, waiting for transfers between devices: 10.5 us -> 17.6 us  [body(): lax.ppermute(up, ('y', 'x', 'c'), [((b * 4 + a) * 2 + core, (a * 4 + (2 *...]
    ppermute x4, starting transfers between devices: 17.8 us -> 11.8 us  [body(): other = [lax.ppermute(u, 'c', [(0, 1), (1, 0)]) for u in own]]
    ppermute x6, waiting for transfers between devices: 10 us -> 6.24 us  [shift(): return lax.ppermute(value, axis, [(i, (i + by) % 4) for i in range(4)])]
    all_to_all x1, blocking collectives: 17.8 us -> 21 us  [body(): squares = lax.all_to_all(squares, ('l', 'h'), 0, 0, tiled=True)]
    all_to_all x1, blocking collectives: 17.1 us -> 14.1 us  [body(): squares = lax.all_to_all(squares, ('x', 'y', 'c'), 0, 0, tiled=True)]
    ppermute x4, starting transfers between devices: 17.8 us -> 15.8 us  [body(): lax.ppermute(up, ('y', 'x', 'c'), [((b * 4 + a) * 2 + core, (a * 4 + (2 *...]
    unnamed x42 -> x46, local copies, waits for them, and re-layouts: 3.09 us -> 4.96 us
  transfers between devices with their start and end apart: 17 -> 17, of which waited for: 4 -> 4; matrix products, arithmetic and copies ran while one was open for 5% -> 6% of each run, Pallas kernels for 11% -> 11%
where the time goes in v5:
time: 180 us; the launch traced here: 179 us
  starting transfers between devices  68.7 us (38%)
  blocking collectives  35 us (19%)
  waiting for transfers between devices  24.1 us (13%)
  Pallas kernels  20.4 us (11%)
  between operations  15.1 us (8%)
  local copies, waits for them, and re-layouts  6.71 us (4%)
  other arithmetic  4.89 us (3%)
  matrix products  3.61 us (2%)
    ppermute x6, starting transfers between devices, shift(): return lax.ppermute(value, axis, [(i, (i + by) % 4) for i in range(4)])  36.8 us
    all_to_all x1, blocking collectives, body(): squares = lax.all_to_all(squares, ('l', 'h'), 0, 0, tiled=True)  21 us
    ppermute x4, waiting for transfers between devices, body(): lax.ppermute(up, ('y', 'x', 'c'), [((b * 4 + a) * 2 + core, (a * 4 + (2 *...  17.6 us
    ppermute x4, starting transfers between devices, body(): lax.ppermute(up, ('y', 'x', 'c'), [((b * 4 + a) * 2 + core, (a * 4 + (2 *...  15.8 us
    all_to_all x1, blocking collectives, body(): squares = lax.all_to_all(squares, ('x', 'y', 'c'), 0, 0, tiled=True)  14.1 us
    ppermute x4, starting transfers between devices, body(): other = [lax.ppermute(u, 'c', [(0, 1), (1, 0)]) for u in own]  11.8 us
    ppermute x6, waiting for transfers between devices, shift(): return lax.ppermute(value, axis, [(i, (i + by) % 4) for i in range(4)])  6.24 us
    pallas_call x1, Pallas kernels, body(): pl.pallas_call(grad_hidden_kernel, out_shape=jax.ShapeDtypeStruct((4, 512...  6.18 us
  transfers between devices with their start and end apart: 17, of which 4 were waited for; matrix products, arithmetic and copies ran while one was open for 6% of the time, Pallas kernels for 11%

profile of v5, /device:TPU:1, one launch (start us, length us, event | category | flops | bytes accessed | tf_op | source)
XLA Modules:
  0.0 178.7 jit_solution(7438344822031012040)
XLA Ops:
  7.2 0.0 copy-start
  7.2 0.0 all-gather.3.cloned.1.call-start
  7.2 16.4 %collective-permute-start.1 = (bf16[512,128]{1,0:T(8,128)(2,1)}, bf16[512,128]{1,0:T(8,128)(2,1)S(1)}, u32[]{:S(2)}, u32[]{:S(2)}) collective-permute-start(bf16[512,128]{1,0:T(8,128)(2,1)} %r0.1), channel_id=1, source_target_pairs={{0,4},{2,6},{4,0},{6,2},{1,5},{3,7},{5,1},{7,3},{8,12},{10,14},{12... | collective-permute-start | bytes 393224 | tf_op jit(solution)/shard_map/up/ppermute | solution.py:85
  23.7 4.0 %collective-permute-start = (bf16[512,128]{1,0:T(8,128)(2,1)}, bf16[512,128]{1,0:T(8,128)(2,1)S(1)}, u32[]{:S(2)}, u32[]{:S(2)}) collective-permute-start(bf16[512,128]{1,0:T(8,128)(2,1)} %r0.1), channel_id=1, source_target_pairs={{0,2},{2,4},{4,6},{6,0},{1,3},{3,5},{5,7},{7,1},{8,10},{10,12},{12... | collective-permute-start | bytes 393224 | tf_op jit(solution)/shard_map/up/ppermute | solution.py:85
  27.7 5.2 %collective-permute-start.2 = (bf16[512,128]{1,0:T(8,128)(2,1)}, bf16[512,128]{1,0:T(8,128)(2,1)S(1)}, u32[]{:S(2)}, u32[]{:S(2)}) collective-permute-start(bf16[512,128]{1,0:T(8,128)(2,1)} %r0.1), channel_id=1, source_target_pairs={{0,6},{2,0},{4,2},{6,4},{1,7},{3,1},{5,3},{7,5},{8,14},{10,8},{12,... | collective-permute-start | bytes 393224 | tf_op jit(solution)/shard_map/up/ppermute | solution.py:85
  32.9 2.3 %convolution_convert_fusion = bf16[512,512]{1,0:T(8,128)(2,1)} fusion(bf16[512,512]{1,0:T(8,128)(2,1)} %constant.34.clone, bf16[512,512]{1,0:T(8,128)(2,1)S(1)} %copy-done), kind=kOutput, calls=%fused_computation | convolution fusion | flops 268697600 | bytes 1572864 | tf_op jit(solution)/shard_map/dot_general | solution.py:113
  35.2 0.0 all-gather.3.cloned.1.call-update
  35.3 0.1 bitcast_reduce_fusion
  35.4 0.2 fusion.3
  35.5 0.7 copy-done.3
  36.2 0.1 copy-done.13
  36.3 0.3 convolution_convert_fusion.1.w
  36.6 0.0 copy-start.17
  36.6 0.0 copy-start.16
  36.6 1.0 convert_convert_fusion
  37.7 0.3 fusion.8
  38.0 0.3 convolution_add_fusion.2
  38.2 0.3 convolution_add_fusion.1
  38.5 0.1 copy-done.14
  38.6 0.2 fusion
  38.9 1.1 broadcast_in_dim.4
  39.9 4.3 %all-to-all-start = ((bf16[4,256,512]{2,1,0:T(8,128)(2,1)}), bf16[4,256,512]{2,1,0:T(8,128)(2,1)}, u32[]{:S(2)}, u32[]{:S(2)}) async-start(bf16[4,256,512]{2,1,0:T(8,128)(2,1)} %broadcast_in_dim.4), calls=%async_computation | async-start | bytes 2097152 | tf_op jit(solution)/shard_map/masked/all_to_all | solution.py:131
  44.2 0.0 reduce-scatter.2.cloned.1.call-start
  44.2 0.7 stack.23.place
  44.9 0.0 collective-permute-done.1.r2
  44.9 0.0 collective-permute-done.r1
  44.9 3.0 %collective-permute-done.2.r3 = bf16[512,128]{1,0:T(8,128)(2,1)S(1)} collective-permute-done((bf16[512,128]{1,0:T(8,128)(2,1)}, bf16[512,128]{1,0:T(8,128)(2,1)S(1)}, u32[]{:S(2)}, u32[]{:S(2)}) %collective-permute-start.2) | collective-permute-done | bytes 131104 | tf_op jit(solution)/shard_map/up/ppermute | solution.py:85
  48.0 0.7 copy-done.22
  48.6 2.0 %stack_upstream.1 = bf16[4,512,128]{2,1,0:T(8,128)(2,1)} custom-call(bf16[512,128]{1,0:T(8,128)(2,1)} %r0.1, bf16[512,128]{1,0:T(8,128)(2,1)} %copy-done.21, bf16[512,128]{1,0:T(8,128)(2,1)} %copy-done.20, bf16[512,128]{1,0:T(8,128)(2,1)} %copy-done.22), custom_call_target="tpu_custom_call" | custom-call | flops 999999995904 | bytes 1073741824 | tf_op jit(solution)/shard_map/stack_upstream/pallas_call | solution.py:98
  50.6 3.1 %collective-permute-start.6 = (bf16[4,512,128]{2,1,0:T(8,128)(2,1)}, bf16[4,512,128]{2,1,0:T(8,128)(2,1)S(1)}, u32[]{:S(2)}, u32[]{:S(2)}) collective-permute-start(bf16[4,512,128]{2,1,0:T(8,128)(2,1)} %stack_upstream.1), channel_id=1, source_target_pairs={{0,24},{1,9},{8,136},{9,153},{16,280},{17,265},{24,392},{25,409},{... | collective-permute-start | bytes 1572872 | tf_op jit(solution)/shard_map/upstream_xy/ppermute | solution.py:136
  53.7 1.7 collective-permute-start.5
  55.4 6.8 %collective-permute-start.4 = (bf16[4,512,128]{2,1,0:T(8,128)(2,1)}, bf16[4,512,128]{2,1,0:T(8,128)(2,1)S(1)}, u32[]{:S(2)}, u32[]{:S(2)}) collective-permute-start(bf16[4,512,128]{2,1,0:T(8,128)(2,1)} %stack_upstream.1), channel_id=1, source_target_pairs={{0,8},{1,25},{8,152},{9,137},{16,264},{17,281},{24,408},{25,393},{... | collective-permute-start | bytes 1572872 | tf_op jit(solution)/shard_map/upstream_xy/ppermute | solution.py:136
  62.2 4.2 %collective-permute-start.3 = (bf16[4,512,128]{2,1,0:T(8,128)(2,1)}, bf16[4,512,128]{2,1,0:T(8,128)(2,1)S(1)}, u32[]{:S(2)}, u32[]{:S(2)}) collective-permute-start(bf16[4,512,128]{2,1,0:T(8,128)(2,1)} %stack_upstream.1), channel_id=1, source_target_pairs={{0,0},{1,17},{8,144},{9,129},{16,256},{17,273},{24,400},{25,385},{... | collective-permute-start | bytes 1572872 | tf_op jit(solution)/shard_map/upstream_xy/ppermute | solution.py:136
  66.4 17.6 %collective-permute-done.6.a3 = bf16[4,512,128]{2,1,0:T(8,128)(2,1)S(1)} collective-permute-done((bf16[4,512,128]{2,1,0:T(8,128)(2,1)}, bf16[4,512,128]{2,1,0:T(8,128)(2,1)S(1)}, u32[]{:S(2)}, u32[]{:S(2)}) %collective-permute-start.6) | collective-permute-done | bytes 524320 | tf_op jit(solution)/shard_map/upstream_xy/ppermute | solution.py:136
  84.0 4.8 %collective-permute-start.10 = (bf16[4,512,128]{2,1,0:T(8,128)(2,1)S(1)}, bf16[4,512,128]{2,1,0:T(8,128)(2,1)S(1)}, u32[]{:S(2)}, u32[]{:S(2)}) collective-permute-start(bf16[4,512,128]{2,1,0:T(8,128)(2,1)S(1)} %collective-permute-done.6.a3), channel_id=1, source_target_pairs={{0,1},{1,0},{2,3},{3,2},{4,5},{5,4},{6,7},{7,6},{8,9},{9,8},{10,11... | collective-permute-start | bytes 1572872 | tf_op jit(solution)/shard_map/upstream_core/ppermute | solution.py:149
  88.8 0.0 collective-permute-done.5.a2
  88.9 2.6 %collective-permute-start.9 = (bf16[4,512,128]{2,1,0:T(8,128)(2,1)S(1)}, bf16[4,512,128]{2,1,0:T(8,128)(2,1)S(1)}, u32[]{:S(2)}, u32[]{:S(2)}) collective-permute-start(bf16[4,512,128]{2,1,0:T(8,128)(2,1)S(1)} %collective-permute-done.5.a2), channel_id=1, source_target_pairs={{0,1},{1,0},{2,3},{3,2},{4,5},{5,4},{6,7},{7,6},{8,9},{9,8},{10,11... | collective-permute-start | bytes 1572872 | tf_op jit(solution)/shard_map/upstream_core/ppermute | solution.py:149
  91.5 0.0 collective-permute-done.4.a1
  91.5 2.3 %collective-permute-start.8 = (bf16[4,512,128]{2,1,0:T(8,128)(2,1)S(1)}, bf16[4,512,128]{2,1,0:T(8,128)(2,1)S(1)}, u32[]{:S(2)}, u32[]{:S(2)}) collective-permute-start(bf16[4,512,128]{2,1,0:T(8,128)(2,1)S(1)} %collective-permute-done.4.a1), channel_id=1, source_target_pairs={{0,1},{1,0},{2,3},{3,2},{4,5},{5,4},{6,7},{7,6},{8,9},{9,8},{10,11... | collective-permute-start | bytes 1572872 | tf_op jit(solution)/shard_map/upstream_core/ppermute | solution.py:149
  93.8 0.0 copy-start.7
  93.8 2.0 %collective-permute-start.7 = (bf16[4,512,128]{2,1,0:T(8,128)(2,1)S(1)}, bf16[4,512,128]{2,1,0:T(8,128)(2,1)}, u32[]{:S(2)}, u32[]{:S(2)}) collective-permute-start(bf16[4,512,128]{2,1,0:T(8,128)(2,1)S(1)} %collective-permute-done.3.a0), channel_id=1, source_target_pairs={{0,1},{1,0},{2,3},{3,2},{4,5},{5,4},{6,7},{7,6},{8,9},{9,8},{10,11... | collective-permute-start | bytes 1572872 | tf_op jit(solution)/shard_map/upstream_core/ppermute | solution.py:149
  95.9 0.0 collective-permute-done.9.b2
  95.9 0.0 collective-permute-done.8.b1
  95.9 0.8 copy-done.9
  96.8 0.8 copy-done.10
  97.6 0.2 collective-permute-done.7.b0
  97.8 4.0 %grad_masked_far.1.far = bf16[512,256]{1,0:T(8,128)(2,1)} custom-call(s32[5]{0:T(128)} %stack.23.place, bf16[4,512,512]{2,1,0:T(8,128)(2,1)} %bitcast.51, bf16[4,512,128]{2,1,0:T(8,128)(2,1)} %copy-done.7, bf16[4,512,128]{2,1,0:T(8,128)(2,1)} %copy-done.6, bf16[4,512,128]{2,1,0:T(8,128)(2,1)} %copy-done.5, bf16[4,512,128]{2,1,0:T(8,128)(2,1)} %copy-done.4, ...), custom_call_target="tpu_custom_call" | custom-call | flops 536870912 | bytes 3145728 | tf_op jit(solution)/shard_map/grad_masked_far/pallas_call | solution.py:155
  101.8 4.2 %collective-permute-start.11 = (bf16[512,256]{1,0:T(8,128)(2,1)}, bf16[512,256]{1,0:T(8,128)(2,1)S(1)}, u32[]{:S(2)}, u32[]{:S(2)}) collective-permute-start(bf16[512,256]{1,0:T(8,128)(2,1)} %grad_masked_far.1.far), channel_id=1, source_target_pairs={{0,64},{32,96},{64,0},{96,32},{1,65},{33,97},{65,1},{97,33},{2,66}... | collective-permute-start | bytes 786440 | tf_op jit(solution)/shard_map/grad_masked_sum/ppermute | solution.py:85
  106.0 5.5 %grad_masked.1 = (f32[512,256]{1,0:T(8,128)}, bf16[512,256]{1,0:T(8,128)(2,1)}, bf16[512,256]{1,0:T(8,128)(2,1)}) custom-call(s32[5]{0:T(128)} %stack.23.place, bf16[4,512,512]{2,1,0:T(8,128)(2,1)} %bitcast.52, bf16[4,512,128]{2,1,0:T(8,128)(2,1)} %copy-done.7, bf16[4,512,128]{2,1,0:T(8,128)(2,1)} %copy-done.6, bf16[4,512,128]{2,1,0:T(8,128)(2,1)} %copy-done.5, ...), custom_call_target="tpu_custom_call" | custom-call | flops 1610612736 | bytes 6291456 | tf_op jit(solution)/shard_map/grad_masked/pallas_call | solution.py:168
  111.5 3.2 %collective-permute-start.12 = (bf16[512,256]{1,0:T(8,128)(2,1)}, bf16[512,256]{1,0:T(8,128)(2,1)S(1)}, u32[]{:S(2)}, u32[]{:S(2)}) collective-permute-start(bf16[512,256]{1,0:T(8,128)(2,1)} %get-tuple-element.12), channel_id=1, source_target_pairs={{0,32},{32,64},{64,96},{96,0},{1,33},{33,65},{65,97},{97,1},{2,34}... | collective-permute-start | bytes 786440 | tf_op jit(solution)/shard_map/grad_masked_sum/ppermute | solution.py:85
  114.7 3.9 %collective-permute-start.13 = (bf16[512,256]{1,0:T(8,128)(2,1)}, bf16[512,256]{1,0:T(8,128)(2,1)S(1)}, u32[]{:S(2)}, u32[]{:S(2)}) collective-permute-start(bf16[512,256]{1,0:T(8,128)(2,1)} %get-tuple-element.13), channel_id=1, source_target_pairs={{0,96},{32,0},{64,32},{96,64},{1,97},{33,1},{65,33},{97,65},{2,98}... | collective-permute-start | bytes 786440 | tf_op jit(solution)/shard_map/grad_masked_sum/ppermute | solution.py:85
  118.6 0.0 all-to-all-done.m
  118.6 6.2 %grad_hidden.1 = bf16[4,512,512]{2,1,0:T(8,128)(2,1)} custom-call(s32[5]{0:T(128)} %stack.23.place, bf16[4,256,512]{2,1,0:T(8,128)(2,1)} %all-to-all-done.m, bf16[4,512,128]{2,1,0:T(8,128)(2,1)} %copy-done.7, bf16[4,512,128]{2,1,0:T(8,128)(2,1)} %copy-done.6, bf16[4,512,128]{2,1,0:T(8,128)(2,1)} %copy-done.5, bf16[4,512,128]{2,1,0:T(8,128)(2,1)} %copy-done.4, ...), custom_call_target="tpu_custom_call" | custom-call | flops 2147483648 | bytes 7340032 | tf_op jit(solution)/shard_map/grad_hidden/pallas_call | solution.py:183
  124.8 0.0 reduce-scatter.2.cloned.1.call-update
  124.8 1.0 copy-done.12
  125.8 0.8 convert_add_fusion.g0
  126.7 0.0 collective-permute-done.12.g1
  126.7 3.2 %collective-permute-done.13.g3 = bf16[512,256]{1,0:T(8,128)(2,1)S(1)} collective-permute-done((bf16[512,256]{1,0:T(8,128)(2,1)}, bf16[512,256]{1,0:T(8,128)(2,1)S(1)}, u32[]{:S(2)}, u32[]{:S(2)}) %collective-permute-start.13) | collective-permute-done | bytes 262176 | tf_op jit(solution)/shard_map/grad_masked_sum/ppermute | solution.py:85
  129.9 0.7 copy-done.19
  130.6 2.7 %grad_logits.1 = (f32[6,128,256]{2,1,0:T(8,128)}, f32[16,128]{1,0:T(8,128)}) custom-call(f32[512,256]{1,0:T(8,128)} %convert_add_fusion.g0, bf16[512,256]{1,0:T(8,128)(2,1)} %copy-done.18, bf16[512,256]{1,0:T(8,128)(2,1)} %copy-done.19, bf16[512,256]{1,0:T(8,128)(2,1)} %copy-done.11, f32[6,128,256]{2,1,0:T(8,128)} %get-tuple-element.17.probs), custom_call_target="tpu_custom_call" | custom-call | flops 999999995904 | bytes 1073741824 | tf_op jit(solution)/shard_map/grad_logits/pallas_call | solution.py:198
  133.3 21.0 %all_to_all.20 = f32[16,1,128]{2,1,0:T(1,128)S(1)} all-to-all(f32[16,1,128]{2,1,0:T(1,128)} %bitcast.55), channel_id=1, replica_groups=mesh['y'=4,'l'=4,'x'=4,'h'=4,'c'=2] {'l','h'}, dimensions={0} | all-to-all | bytes 16384 | tf_op jit(solution)/shard_map/mean_square/all_to_all | solution.py:212
  154.3 14.1 %all_to_all.21 = f32[32,1,128]{2,1,0:T(1,128)S(1)} all-to-all(f32[32,1,128]{2,1,0:T(1,128)S(1)} %broadcast_in_dim.5), channel_id=1, replica_groups=mesh['y'=4,'l'=4,'x'=4,'h'=4,'c'=2] {'x','y','c'}, dimensions={0} | all-to-all | bytes 32768 | tf_op jit(solution)/shard_map/mean_square/all_to_all | solution.py:214
  168.4 0.6 reduce_sum.29
  169.7 2.1 %multiply_bitcast_fusion = f32[128,6,256]{2,0,1:T(8,128)} fusion(f32[6,128,256]{2,1,0:T(8,128)} %get-tuple-element.14, f32[]{:T(128)S(6)} %rsqrt.3), kind=kLoop, calls=%fused_computation.9 | loop fusion | flops 196608 | bytes 1572868 | tf_op jit(solution)/shard_map/transpose | solution.py:216
  (41 shorter events, 0.1 us)
Async XLA Ops:
  7.2 25.7 %copy-start = (bf16[512,512]{1,0:T(8,128)(2,1)S(1)}, bf16[512,512]{1,0:T(8,128)(2,1)}, u32[]{:S(2)}) copy-start(bf16[512,512]{1,0:T(8,128)(2,1)} %param.6) | copy-start | bytes 1572868
  7.2 28.1 %copy-start.2 = (f32[128,6,256]{2,0,1:T(8,128)S(1)}, f32[128,6,256]{2,0,1:T(8,128)}, u32[]{:S(2)}) copy-start(f32[128,6,256]{2,0,1:T(8,128)} %param.10) | copy-start | bytes 2359300
  7.2 28.1 %copy-start.1 = (f32[128,6,256]{2,0,1:T(8,128)S(1)}, f32[128,6,256]{2,0,1:T(8,128)}, u32[]{:S(2)}) copy-start(f32[128,6,256]{2,0,1:T(8,128)} %param.9) | copy-start | bytes 2359300
  7.2 90.6 %all-gather.3.cloned.1.call-start = ((), (), s32[]{:S(2)}) async-start(), calls=%async_computation.5 | async-start | bytes 2621440 | tf_op jit(solution)/shard_map/hidden/all_gather | solution.py:117
  7.2 37.7 %collective-permute-start.1 = (bf16[512,128]{1,0:T(8,128)(2,1)}, bf16[512,128]{1,0:T(8,128)(2,1)S(1)}, u32[]{:S(2)}, u32[]{:S(2)}) collective-permute-start(bf16[512,128]{1,0:T(8,128)(2,1)} %r0.1), channel_id=1, source_target_pairs={{0,4},{2,6},{4,0},{6,2},{1,5},{3,7},{5,1},{7,3},{8,12},{10,14},{12... | collective-permute-start | bytes 393224 | tf_op jit(solution)/shard_map/up/ppermute | solution.py:85
  23.7 21.3 %collective-permute-start = (bf16[512,128]{1,0:T(8,128)(2,1)}, bf16[512,128]{1,0:T(8,128)(2,1)S(1)}, u32[]{:S(2)}, u32[]{:S(2)}) collective-permute-start(bf16[512,128]{1,0:T(8,128)(2,1)} %r0.1), channel_id=1, source_target_pairs={{0,2},{2,4},{4,6},{6,0},{1,3},{3,5},{5,7},{7,1},{8,10},{10,12},{12... | collective-permute-start | bytes 393224 | tf_op jit(solution)/shard_map/up/ppermute | solution.py:85
  27.7 20.3 %collective-permute-start.2 = (bf16[512,128]{1,0:T(8,128)(2,1)}, bf16[512,128]{1,0:T(8,128)(2,1)S(1)}, u32[]{:S(2)}, u32[]{:S(2)}) collective-permute-start(bf16[512,128]{1,0:T(8,128)(2,1)} %r0.1), channel_id=1, source_target_pairs={{0,6},{2,0},{4,2},{6,4},{1,7},{3,1},{5,3},{7,5},{8,14},{10,8},{12,... | collective-permute-start | bytes 393224 | tf_op jit(solution)/shard_map/up/ppermute | solution.py:85
  35.2 1.0 copy-start.3
  35.2 1.1 copy-start.13
  36.3 1.4 copy-start.15
  36.6 1.9 %copy-start.11 = (bf16[512,256]{1,0:T(8,128)(2,1)}, bf16[512,256]{1,0:T(8,128)(2,1)S(1)}, u32[]{:S(2)}) copy-start(bf16[512,256]{1,0:T(8,128)(2,1)S(1)} %convolution_convert_fusion.1.w) | copy-start | bytes 786436
  36.6 1.3 copy-start.17
  36.6 1.6 copy-start.16
  37.7 0.9 copy-start.14
  39.9 78.7 %all-to-all-start = ((bf16[4,256,512]{2,1,0:T(8,128)(2,1)}), bf16[4,256,512]{2,1,0:T(8,128)(2,1)}, u32[]{:S(2)}, u32[]{:S(2)}) async-start(bf16[4,256,512]{2,1,0:T(8,128)(2,1)} %broadcast_in_dim.4), calls=%async_computation | async-start | bytes 2097152 | tf_op jit(solution)/shard_map/masked/all_to_all | solution.py:131
  44.2 127.6 %reduce-scatter.2.cloned.1.call-start = ((), (), s32[]{:S(2)}) async-start(), calls=%async_computation.4 | async-start | bytes 2621440 | tf_op jit(solution)/shard_map/grad_hidden_sum/reduce_scatter | solution.py:195
  44.9 3.0 %copy-start.20 = (bf16[512,128]{1,0:T(8,128)(2,1)}, bf16[512,128]{1,0:T(8,128)(2,1)S(1)}, u32[]{:S(2)}) copy-start(bf16[512,128]{1,0:T(8,128)(2,1)S(1)} %collective-permute-done.1.r2) | copy-start | bytes 393220
  44.9 3.0 %copy-start.21 = (bf16[512,128]{1,0:T(8,128)(2,1)}, bf16[512,128]{1,0:T(8,128)(2,1)S(1)}, u32[]{:S(2)}) copy-start(bf16[512,128]{1,0:T(8,128)(2,1)S(1)} %collective-permute-done.r1) | copy-start | bytes 393220
  48.0 0.7 copy-start.22
  50.6 33.4 %collective-permute-start.6 = (bf16[4,512,128]{2,1,0:T(8,128)(2,1)}, bf16[4,512,128]{2,1,0:T(8,128)(2,1)S(1)}, u32[]{:S(2)}, u32[]{:S(2)}) collective-permute-start(bf16[4,512,128]{2,1,0:T(8,128)(2,1)} %stack_upstream.1), channel_id=1, source_target_pairs={{0,24},{1,9},{8,136},{9,153},{16,280},{17,265},{24,392},{25,409},{... | collective-permute-start | bytes 1572872 | tf_op jit(solution)/shard_map/upstream_xy/ppermute | solution.py:136
  53.7 35.1 %collective-permute-start.5 = (bf16[4,512,128]{2,1,0:T(8,128)(2,1)}, bf16[4,512,128]{2,1,0:T(8,128)(2,1)S(1)}, u32[]{:S(2)}, u32[]{:S(2)}) collective-permute-start(bf16[4,512,128]{2,1,0:T(8,128)(2,1)} %stack_upstream.1), channel_id=1, source_target_pairs={{0,16},{1,1},{8,128},{9,145},{16,272},{17,257},{24,384},{25,401},{... | collective-permute-start | bytes 1572872 | tf_op jit(solution)/shard_map/upstream_xy/ppermute | solution.py:136
  55.4 36.1 %collective-permute-start.4 = (bf16[4,512,128]{2,1,0:T(8,128)(2,1)}, bf16[4,512,128]{2,1,0:T(8,128)(2,1)S(1)}, u32[]{:S(2)}, u32[]{:S(2)}) collective-permute-start(bf16[4,512,128]{2,1,0:T(8,128)(2,1)} %stack_upstream.1), channel_id=1, source_target_pairs={{0,8},{1,25},{8,152},{9,137},{16,264},{17,281},{24,408},{25,393},{... | collective-permute-start | bytes 1572872 | tf_op jit(solution)/shard_map/upstream_xy/ppermute | solution.py:136
  62.2 31.6 %collective-permute-start.3 = (bf16[4,512,128]{2,1,0:T(8,128)(2,1)}, bf16[4,512,128]{2,1,0:T(8,128)(2,1)S(1)}, u32[]{:S(2)}, u32[]{:S(2)}) collective-permute-start(bf16[4,512,128]{2,1,0:T(8,128)(2,1)} %stack_upstream.1), channel_id=1, source_target_pairs={{0,0},{1,17},{8,144},{9,129},{16,256},{17,273},{24,400},{25,385},{... | collective-permute-start | bytes 1572872 | tf_op jit(solution)/shard_map/upstream_xy/ppermute | solution.py:136
  84.0 13.8 %copy-start.4 = (bf16[4,512,128]{2,1,0:T(8,128)(2,1)}, bf16[4,512,128]{2,1,0:T(8,128)(2,1)S(1)}, u32[]{:S(2)}) copy-start(bf16[4,512,128]{2,1,0:T(8,128)(2,1)S(1)} %collective-permute-done.6.a3) | copy-start | bytes 1572868
  84.0 11.9 %collective-permute-start.10 = (bf16[4,512,128]{2,1,0:T(8,128)(2,1)S(1)}, bf16[4,512,128]{2,1,0:T(8,128)(2,1)S(1)}, u32[]{:S(2)}, u32[]{:S(2)}) collective-permute-start(bf16[4,512,128]{2,1,0:T(8,128)(2,1)S(1)} %collective-permute-done.6.a3), channel_id=1, source_target_pairs={{0,1},{1,0},{2,3},{3,2},{4,5},{5,4},{6,7},{7,6},{8,9},{9,8},{10,11... | collective-permute-start | bytes 1572872 | tf_op jit(solution)/shard_map/upstream_core/ppermute | solution.py:149
  88.8 8.9 %copy-start.5 = (bf16[4,512,128]{2,1,0:T(8,128)(2,1)}, bf16[4,512,128]{2,1,0:T(8,128)(2,1)S(1)}, u32[]{:S(2)}) copy-start(bf16[4,512,128]{2,1,0:T(8,128)(2,1)S(1)} %collective-permute-done.5.a2) | copy-start | bytes 1572868
  88.9 7.1 %collective-permute-start.9 = (bf16[4,512,128]{2,1,0:T(8,128)(2,1)S(1)}, bf16[4,512,128]{2,1,0:T(8,128)(2,1)S(1)}, u32[]{:S(2)}, u32[]{:S(2)}) collective-permute-start(bf16[4,512,128]{2,1,0:T(8,128)(2,1)S(1)} %collective-permute-done.5.a2), channel_id=1, source_target_pairs={{0,1},{1,0},{2,3},{3,2},{4,5},{5,4},{6,7},{7,6},{8,9},{9,8},{10,11... | collective-permute-start | bytes 1572872 | tf_op jit(solution)/shard_map/upstream_core/ppermute | solution.py:149
  91.5 6.3 %copy-start.6 = (bf16[4,512,128]{2,1,0:T(8,128)(2,1)}, bf16[4,512,128]{2,1,0:T(8,128)(2,1)S(1)}, u32[]{:S(2)}) copy-start(bf16[4,512,128]{2,1,0:T(8,128)(2,1)S(1)} %collective-permute-done.4.a1) | copy-start | bytes 1572868
  91.5 4.4 %collective-permute-start.8 = (bf16[4,512,128]{2,1,0:T(8,128)(2,1)S(1)}, bf16[4,512,128]{2,1,0:T(8,128)(2,1)S(1)}, u32[]{:S(2)}, u32[]{:S(2)}) collective-permute-start(bf16[4,512,128]{2,1,0:T(8,128)(2,1)S(1)} %collective-permute-done.4.a1), channel_id=1, source_target_pairs={{0,1},{1,0},{2,3},{3,2},{4,5},{5,4},{6,7},{7,6},{8,9},{9,8},{10,11... | collective-permute-start | bytes 1572872 | tf_op jit(solution)/shard_map/upstream_core/ppermute | solution.py:149
  93.8 4.0 %copy-start.7 = (bf16[4,512,128]{2,1,0:T(8,128)(2,1)}, bf16[4,512,128]{2,1,0:T(8,128)(2,1)S(1)}, u32[]{:S(2)}) copy-start(bf16[4,512,128]{2,1,0:T(8,128)(2,1)S(1)} %collective-permute-done.3.a0) | copy-start | bytes 1572868
  93.8 3.9 %collective-permute-start.7 = (bf16[4,512,128]{2,1,0:T(8,128)(2,1)S(1)}, bf16[4,512,128]{2,1,0:T(8,128)(2,1)}, u32[]{:S(2)}, u32[]{:S(2)}) collective-permute-start(bf16[4,512,128]{2,1,0:T(8,128)(2,1)S(1)} %collective-permute-done.3.a0), channel_id=1, source_target_pairs={{0,1},{1,0},{2,3},{3,2},{4,5},{5,4},{6,7},{7,6},{8,9},{9,8},{10,11... | collective-permute-start | bytes 1572872 | tf_op jit(solution)/shard_map/upstream_core/ppermute | solution.py:149
  95.9 1.9 %copy-start.8 = (bf16[4,512,128]{2,1,0:T(8,128)(2,1)}, bf16[4,512,128]{2,1,0:T(8,128)(2,1)S(1)}, u32[]{:S(2)}) copy-start(bf16[4,512,128]{2,1,0:T(8,128)(2,1)S(1)} %collective-permute-done.10.b3) | copy-start | bytes 1572868
  95.9 0.9 copy-start.9
  96.8 0.8 copy-start.10
  101.8 23.0 %collective-permute-start.11 = (bf16[512,256]{1,0:T(8,128)(2,1)}, bf16[512,256]{1,0:T(8,128)(2,1)S(1)}, u32[]{:S(2)}, u32[]{:S(2)}) collective-permute-start(bf16[512,256]{1,0:T(8,128)(2,1)} %grad_masked_far.1.far), channel_id=1, source_target_pairs={{0,64},{32,96},{64,0},{96,32},{1,65},{33,97},{65,1},{97,33},{2,66}... | collective-permute-start | bytes 786440 | tf_op jit(solution)/shard_map/grad_masked_sum/ppermute | solution.py:85
  111.5 15.2 %collective-permute-start.12 = (bf16[512,256]{1,0:T(8,128)(2,1)}, bf16[512,256]{1,0:T(8,128)(2,1)S(1)}, u32[]{:S(2)}, u32[]{:S(2)}) collective-permute-start(bf16[512,256]{1,0:T(8,128)(2,1)} %get-tuple-element.12), channel_id=1, source_target_pairs={{0,32},{32,64},{64,96},{96,0},{1,33},{33,65},{65,97},{97,1},{2,34}... | collective-permute-start | bytes 786440 | tf_op jit(solution)/shard_map/grad_masked_sum/ppermute | solution.py:85
  114.7 15.2 %collective-permute-start.13 = (bf16[512,256]{1,0:T(8,128)(2,1)}, bf16[512,256]{1,0:T(8,128)(2,1)S(1)}, u32[]{:S(2)}, u32[]{:S(2)}) collective-permute-start(bf16[512,256]{1,0:T(8,128)(2,1)} %get-tuple-element.13), channel_id=1, source_target_pairs={{0,96},{32,0},{64,32},{96,64},{1,97},{33,1},{65,33},{97,65},{2,98}... | collective-permute-start | bytes 786440 | tf_op jit(solution)/shard_map/grad_masked_sum/ppermute | solution.py:85
  124.8 1.0 copy-start.12
  126.7 3.2 %copy-start.18 = (bf16[512,256]{1,0:T(8,128)(2,1)}, bf16[512,256]{1,0:T(8,128)(2,1)S(1)}, u32[]{:S(2)}) copy-start(bf16[512,256]{1,0:T(8,128)(2,1)S(1)} %collective-permute-done.12.g1) | copy-start | bytes 786436
  129.9 0.7 copy-start.19
Sparse Core Ops, SparseCore 0:
  35.4 54.1 all-gather.2
  124.9 34.1 reduce-scatter.1

commit v6 on v5

--- a/solution.py
+++ b/solution.py
@@ -201,10 +201,9 @@
             jax.ShapeDtypeStruct((6, 128, 256), jnp.float32),
             jax.ShapeDtypeStruct((16, 128), jnp.float32),
         ],
-        grid=(1,),
-        in_specs=[whole(512, 256)] * 4 + [whole(6, 128, 256)],
-        out_specs=[whole(6, 128, 256), whole(16, 128)],
-        compiler_params=params,
+        in_specs=[pl.BlockSpec(memory_space=pltpu.VMEM)] * 5,
+        out_specs=[pl.BlockSpec(memory_space=pltpu.VMEM)] * 2,
+        compiler_params=pltpu.CompilerParams(vmem_limit_bytes=16 << 20),
         cost_estimate=pl.CostEstimate(flops=10**12, bytes_accessed=1 << 30, transcendentals=0),
         name="grad_logits",
     )(part, got[0], got[2], weight, probs)

time: 180 us -> 175 us (0.972)
  other arithmetic: 4.89 us -> 2.07 us
  Pallas kernels: 20.4 us -> 18 us
    pallas_call x1, Pallas kernels: 2.73 us -> 0.32 us  [body(): pl.pallas_call(grad_logits_kernel, out_shape=[jax.ShapeDtypeStruct((6, 12...]
    unnamed x46 -> x44, local copies, waits for them, and re-layouts: 4.96 us -> 4.83 us
  transfers between devices with their start and end apart: 17 -> 17, of which waited for: 4 -> 4; matrix products, arithmetic and copies ran while one was open for 6% -> 4% of each run, Pallas kernels for 11% -> 10%
where the time goes in v6:
time: 175 us; the launch traced here: 174 us
  starting transfers between devices  68.8 us (39%)
  blocking collectives  34.8 us (20%)
  waiting for transfers between devices  25.1 us (14%)
  Pallas kernels  18 us (10%)
  between operations  15.2 us (9%)
  local copies, waits for them, and re-layouts  6.57 us (4%)
  matrix products  3.63 us (2%)
  other arithmetic  2.07 us (1%)
    ppermute x6, starting transfers between devices, shift(): return lax.ppermute(value, axis, [(i, (i + by) % 4) for i in range(4)])  36.8 us
    all_to_all x1, blocking collectives, body(): squares = lax.all_to_all(squares, ('l', 'h'), 0, 0, tiled=True)  21 us
    ppermute x4, waiting for transfers between devices, body(): lax.ppermute(up, ('y', 'x', 'c'), [((b * 4 + a) * 2 + core, (a * 4 + (2 *...  17.6 us
    ppermute x4, starting transfers between devices, body(): lax.ppermute(up, ('y', 'x', 'c'), [((b * 4 + a) * 2 + core, (a * 4 + (2 *...  15.8 us
    all_to_all x1, blocking collectives, body(): squares = lax.all_to_all(squares, ('x', 'y', 'c'), 0, 0, tiled=True)  13.8 us
    ppermute x4, starting transfers between devices, body(): other = [lax.ppermute(u, 'c', [(0, 1), (1, 0)]) for u in own]  11.8 us
    ppermute x6, waiting for transfers between devices, shift(): return lax.ppermute(value, axis, [(i, (i + by) % 4) for i in range(4)])  7.42 us
    pallas_call x1, Pallas kernels, body(): pl.pallas_call(grad_hidden_kernel, out_shape=jax.ShapeDtypeStruct((4, 512...  6.18 us
  transfers between devices with their start and end apart: 17, of which 4 were waited for; matrix products, arithmetic and copies ran while one was open for 4% of the time, Pallas kernels for 10%

profile of v6, /device:TPU:1, one launch (start us, length us, event | category | flops | bytes accessed | tf_op | source)
XLA Modules:
  0.0 174.1 jit_solution(14553305069451633399)
XLA Ops:
  7.2 0.0 copy-start
  7.2 0.0 all-gather.3.cloned.1.call-start
  7.2 16.4 %collective-permute-start.1 = (bf16[512,128]{1,0:T(8,128)(2,1)}, bf16[512,128]{1,0:T(8,128)(2,1)S(1)}, u32[]{:S(2)}, u32[]{:S(2)}) collective-permute-start(bf16[512,128]{1,0:T(8,128)(2,1)} %r0.1), channel_id=1, source_target_pairs={{0,4},{2,6},{4,0},{6,2},{1,5},{3,7},{5,1},{7,3},{8,12},{10,14},{12... | collective-permute-start | bytes 393224 | tf_op jit(solution)/shard_map/up/ppermute | solution.py:85
  23.7 4.0 %collective-permute-start = (bf16[512,128]{1,0:T(8,128)(2,1)}, bf16[512,128]{1,0:T(8,128)(2,1)S(1)}, u32[]{:S(2)}, u32[]{:S(2)}) collective-permute-start(bf16[512,128]{1,0:T(8,128)(2,1)} %r0.1), channel_id=1, source_target_pairs={{0,2},{2,4},{4,6},{6,0},{1,3},{3,5},{5,7},{7,1},{8,10},{10,12},{12... | collective-permute-start | bytes 393224 | tf_op jit(solution)/shard_map/up/ppermute | solution.py:85
  27.7 5.2 %collective-permute-start.2 = (bf16[512,128]{1,0:T(8,128)(2,1)}, bf16[512,128]{1,0:T(8,128)(2,1)S(1)}, u32[]{:S(2)}, u32[]{:S(2)}) collective-permute-start(bf16[512,128]{1,0:T(8,128)(2,1)} %r0.1), channel_id=1, source_target_pairs={{0,6},{2,0},{4,2},{6,4},{1,7},{3,1},{5,3},{7,5},{8,14},{10,8},{12,... | collective-permute-start | bytes 393224 | tf_op jit(solution)/shard_map/up/ppermute | solution.py:85
  32.9 2.3 %convolution_convert_fusion = bf16[512,512]{1,0:T(8,128)(2,1)} fusion(bf16[512,512]{1,0:T(8,128)(2,1)} %constant.34.clone, bf16[512,512]{1,0:T(8,128)(2,1)S(1)} %copy-done), kind=kOutput, calls=%fused_computation | convolution fusion | flops 268697600 | bytes 1572864 | tf_op jit(solution)/shard_map/dot_general | solution.py:113
  35.2 0.0 all-gather.3.cloned.1.call-update
  35.3 0.1 bitcast_reduce_fusion
  35.4 0.2 fusion.3
  35.5 0.7 copy-done.5
  36.3 0.1 copy-done.14
  36.3 0.3 convolution_convert_fusion.1.w
  36.6 0.0 copy-start.18
  36.6 0.0 copy-start.17
  36.7 0.2 convert_convert_fusion
  36.8 0.0 copy-start.15
  36.8 0.4 copy-done.16
  37.2 0.2 fusion.8
  37.5 0.2 copy-done.18
  37.6 0.3 convolution_add_fusion.2
  37.9 0.3 convolution_add_fusion.1
  38.2 0.2 fusion
  38.5 1.1 broadcast_in_dim.4
  39.5 4.3 %all-to-all-start = ((bf16[4,256,512]{2,1,0:T(8,128)(2,1)}), bf16[4,256,512]{2,1,0:T(8,128)(2,1)}, u32[]{:S(2)}, u32[]{:S(2)}) async-start(bf16[4,256,512]{2,1,0:T(8,128)(2,1)} %broadcast_in_dim.4), calls=%async_computation | async-start | bytes 2097152 | tf_op jit(solution)/shard_map/masked/all_to_all | solution.py:131
  43.8 0.0 reduce-scatter.2.cloned.1.call-start
  43.8 0.7 stack.23.place
  44.5 0.0 collective-permute-done.r1
  44.5 0.0 copy-start.20
  44.5 3.4 %collective-permute-done.2.r3 = bf16[512,128]{1,0:T(8,128)(2,1)S(1)} collective-permute-done((bf16[512,128]{1,0:T(8,128)(2,1)}, bf16[512,128]{1,0:T(8,128)(2,1)S(1)}, u32[]{:S(2)}, u32[]{:S(2)}) %collective-permute-start.2) | collective-permute-done | bytes 131104 | tf_op jit(solution)/shard_map/up/ppermute | solution.py:85
  48.0 0.7 copy-done.21
  48.6 2.0 %stack_upstream.1 = bf16[4,512,128]{2,1,0:T(8,128)(2,1)} custom-call(bf16[512,128]{1,0:T(8,128)(2,1)} %r0.1, bf16[512,128]{1,0:T(8,128)(2,1)} %copy-done.20, bf16[512,128]{1,0:T(8,128)(2,1)} %copy-done.19, bf16[512,128]{1,0:T(8,128)(2,1)} %copy-done.21), custom_call_target="tpu_custom_call" | custom-call | flops 999999995904 | bytes 1073741824 | tf_op jit(solution)/shard_map/stack_upstream/pallas_call | solution.py:98
  50.6 3.1 %collective-permute-start.6 = (bf16[4,512,128]{2,1,0:T(8,128)(2,1)}, bf16[4,512,128]{2,1,0:T(8,128)(2,1)S(1)}, u32[]{:S(2)}, u32[]{:S(2)}) collective-permute-start(bf16[4,512,128]{2,1,0:T(8,128)(2,1)} %stack_upstream.1), channel_id=1, source_target_pairs={{0,24},{1,9},{8,136},{9,153},{16,280},{17,265},{24,392},{25,409},{... | collective-permute-start | bytes 1572872 | tf_op jit(solution)/shard_map/upstream_xy/ppermute | solution.py:136
  53.7 1.7 collective-permute-start.5
  55.4 6.8 %collective-permute-start.4 = (bf16[4,512,128]{2,1,0:T(8,128)(2,1)}, bf16[4,512,128]{2,1,0:T(8,128)(2,1)S(1)}, u32[]{:S(2)}, u32[]{:S(2)}) collective-permute-start(bf16[4,512,128]{2,1,0:T(8,128)(2,1)} %stack_upstream.1), channel_id=1, source_target_pairs={{0,8},{1,25},{8,152},{9,137},{16,264},{17,281},{24,408},{25,393},{... | collective-permute-start | bytes 1572872 | tf_op jit(solution)/shard_map/upstream_xy/ppermute | solution.py:136
  62.2 4.2 %collective-permute-start.3 = (bf16[4,512,128]{2,1,0:T(8,128)(2,1)}, bf16[4,512,128]{2,1,0:T(8,128)(2,1)S(1)}, u32[]{:S(2)}, u32[]{:S(2)}) collective-permute-start(bf16[4,512,128]{2,1,0:T(8,128)(2,1)} %stack_upstream.1), channel_id=1, source_target_pairs={{0,0},{1,17},{8,144},{9,129},{16,256},{17,273},{24,400},{25,385},{... | collective-permute-start | bytes 1572872 | tf_op jit(solution)/shard_map/upstream_xy/ppermute | solution.py:136
  66.4 17.6 %collective-permute-done.6.a3 = bf16[4,512,128]{2,1,0:T(8,128)(2,1)S(1)} collective-permute-done((bf16[4,512,128]{2,1,0:T(8,128)(2,1)}, bf16[4,512,128]{2,1,0:T(8,128)(2,1)S(1)}, u32[]{:S(2)}, u32[]{:S(2)}) %collective-permute-start.6) | collective-permute-done | bytes 524320 | tf_op jit(solution)/shard_map/upstream_xy/ppermute | solution.py:136
  84.0 4.8 %collective-permute-start.10 = (bf16[4,512,128]{2,1,0:T(8,128)(2,1)S(1)}, bf16[4,512,128]{2,1,0:T(8,128)(2,1)S(1)}, u32[]{:S(2)}, u32[]{:S(2)}) collective-permute-start(bf16[4,512,128]{2,1,0:T(8,128)(2,1)S(1)} %collective-permute-done.6.a3), channel_id=1, source_target_pairs={{0,1},{1,0},{2,3},{3,2},{4,5},{5,4},{6,7},{7,6},{8,9},{9,8},{10,11... | collective-permute-start | bytes 1572872 | tf_op jit(solution)/shard_map/upstream_core/ppermute | solution.py:149
  88.9 2.7 %collective-permute-start.9 = (bf16[4,512,128]{2,1,0:T(8,128)(2,1)S(1)}, bf16[4,512,128]{2,1,0:T(8,128)(2,1)S(1)}, u32[]{:S(2)}, u32[]{:S(2)}) collective-permute-start(bf16[4,512,128]{2,1,0:T(8,128)(2,1)S(1)} %collective-permute-done.5.a2), channel_id=1, source_target_pairs={{0,1},{1,0},{2,3},{3,2},{4,5},{5,4},{6,7},{7,6},{8,9},{9,8},{10,11... | collective-permute-start | bytes 1572872 | tf_op jit(solution)/shard_map/upstream_core/ppermute | solution.py:149
  91.5 0.0 collective-permute-done.4.a1
  91.5 0.0 copy-start.8
  91.6 2.3 %collective-permute-start.8 = (bf16[4,512,128]{2,1,0:T(8,128)(2,1)S(1)}, bf16[4,512,128]{2,1,0:T(8,128)(2,1)S(1)}, u32[]{:S(2)}, u32[]{:S(2)}) collective-permute-start(bf16[4,512,128]{2,1,0:T(8,128)(2,1)S(1)} %collective-permute-done.4.a1), channel_id=1, source_target_pairs={{0,1},{1,0},{2,3},{3,2},{4,5},{5,4},{6,7},{7,6},{8,9},{9,8},{10,11... | collective-permute-start | bytes 1572872 | tf_op jit(solution)/shard_map/upstream_core/ppermute | solution.py:149
  93.8 0.0 collective-permute-done.3.a0
  93.8 0.0 copy-start.9
  93.9 2.1 %collective-permute-start.7 = (bf16[4,512,128]{2,1,0:T(8,128)(2,1)S(1)}, bf16[4,512,128]{2,1,0:T(8,128)(2,1)}, u32[]{:S(2)}, u32[]{:S(2)}) collective-permute-start(bf16[4,512,128]{2,1,0:T(8,128)(2,1)S(1)} %collective-permute-done.3.a0), channel_id=1, source_target_pairs={{0,1},{1,0},{2,3},{3,2},{4,5},{5,4},{6,7},{7,6},{8,9},{9,8},{10,11... | collective-permute-start | bytes 1572872 | tf_op jit(solution)/shard_map/upstream_core/ppermute | solution.py:149
  95.9 0.0 collective-permute-done.10.b3
  96.0 0.8 copy-done.10
  96.8 0.1 copy-done.11
  96.9 0.8 copy-done.12
  97.7 0.1 collective-permute-done.7.b0
  97.8 4.0 %grad_masked_far.1.far = bf16[512,256]{1,0:T(8,128)(2,1)} custom-call(s32[5]{0:T(128)} %stack.23.place, bf16[4,512,512]{2,1,0:T(8,128)(2,1)} %bitcast.52, bf16[4,512,128]{2,1,0:T(8,128)(2,1)} %copy-done.9, bf16[4,512,128]{2,1,0:T(8,128)(2,1)} %copy-done.8, bf16[4,512,128]{2,1,0:T(8,128)(2,1)} %copy-done.7, bf16[4,512,128]{2,1,0:T(8,128)(2,1)} %copy-done.6, ...), custom_call_target="tpu_custom_call" | custom-call | flops 536870912 | bytes 3145728 | tf_op jit(solution)/shard_map/grad_masked_far/pallas_call | solution.py:155
  101.8 4.2 %collective-permute-start.11 = (bf16[512,256]{1,0:T(8,128)(2,1)}, bf16[512,256]{1,0:T(8,128)(2,1)S(1)}, u32[]{:S(2)}, u32[]{:S(2)}) collective-permute-start(bf16[512,256]{1,0:T(8,128)(2,1)} %grad_masked_far.1.far), channel_id=1, source_target_pairs={{0,64},{32,96},{64,0},{96,32},{1,65},{33,97},{65,1},{97,33},{2,66}... | collective-permute-start | bytes 786440 | tf_op jit(solution)/shard_map/grad_masked_sum/ppermute | solution.py:85
  106.0 5.5 %grad_masked.1 = (f32[512,256]{1,0:T(8,128)}, bf16[512,256]{1,0:T(8,128)(2,1)}, bf16[512,256]{1,0:T(8,128)(2,1)}) custom-call(s32[5]{0:T(128)} %stack.23.place, bf16[4,512,512]{2,1,0:T(8,128)(2,1)} %bitcast.53, bf16[4,512,128]{2,1,0:T(8,128)(2,1)} %copy-done.9, bf16[4,512,128]{2,1,0:T(8,128)(2,1)} %copy-done.8, bf16[4,512,128]{2,1,0:T(8,128)(2,1)} %copy-done.7, ...), custom_call_target="tpu_custom_call" | custom-call | flops 1610612736 | bytes 6291456 | tf_op jit(solution)/shard_map/grad_masked/pallas_call | solution.py:168
  111.5 3.2 %collective-permute-start.12 = (bf16[512,256]{1,0:T(8,128)(2,1)}, bf16[512,256]{1,0:T(8,128)(2,1)S(1)}, u32[]{:S(2)}, u32[]{:S(2)}) collective-permute-start(bf16[512,256]{1,0:T(8,128)(2,1)} %get-tuple-element.12), channel_id=1, source_target_pairs={{0,32},{32,64},{64,96},{96,0},{1,33},{33,65},{65,97},{97,1},{2,34}... | collective-permute-start | bytes 786440 | tf_op jit(solution)/shard_map/grad_masked_sum/ppermute | solution.py:85
  114.7 3.9 %collective-permute-start.13 = (bf16[512,256]{1,0:T(8,128)(2,1)}, bf16[512,256]{1,0:T(8,128)(2,1)S(1)}, u32[]{:S(2)}, u32[]{:S(2)}) collective-permute-start(bf16[512,256]{1,0:T(8,128)(2,1)} %get-tuple-element.13), channel_id=1, source_target_pairs={{0,96},{32,0},{64,32},{96,64},{1,97},{33,1},{65,33},{97,65},{2,98}... | collective-permute-start | bytes 786440 | tf_op jit(solution)/shard_map/grad_masked_sum/ppermute | solution.py:85
  118.6 6.2 %grad_hidden.1 = bf16[4,512,512]{2,1,0:T(8,128)(2,1)} custom-call(s32[5]{0:T(128)} %stack.23.place, bf16[4,256,512]{2,1,0:T(8,128)(2,1)} %all-to-all-done.m, bf16[4,512,128]{2,1,0:T(8,128)(2,1)} %copy-done.9, bf16[4,512,128]{2,1,0:T(8,128)(2,1)} %copy-done.8, bf16[4,512,128]{2,1,0:T(8,128)(2,1)} %copy-done.7, bf16[4,512,128]{2,1,0:T(8,128)(2,1)} %copy-done.6, ...), custom_call_target="tpu_custom_call" | custom-call | flops 2147483648 | bytes 7340032 | tf_op jit(solution)/shard_map/grad_hidden/pallas_call | solution.py:183
  124.8 0.0 reduce-scatter.2.cloned.1.call-update
  124.8 1.0 copy-done.13
  125.8 0.1 convert_add_fusion.g0
  125.9 4.0 %collective-permute-done.13.g3 = bf16[512,256]{1,0:T(8,128)(2,1)S(1)} collective-permute-done((bf16[512,256]{1,0:T(8,128)(2,1)}, bf16[512,256]{1,0:T(8,128)(2,1)S(1)}, u32[]{:S(2)}, u32[]{:S(2)}) %collective-permute-start.13) | collective-permute-done | bytes 262176 | tf_op jit(solution)/shard_map/grad_masked_sum/ppermute | solution.py:85
  129.9 0.3 grad_logits.1
  130.2 21.0 %all_to_all.20 = f32[16,1,128]{2,1,0:T(1,128)S(1)} all-to-all(f32[16,1,128]{2,1,0:T(1,128)S(1)} %bitcast.51), channel_id=1, replica_groups=mesh['y'=4,'l'=4,'x'=4,'h'=4,'c'=2] {'l','h'}, dimensions={0} | all-to-all | bytes 16384 | tf_op jit(solution)/shard_map/mean_square/all_to_all | solution.py:211
  151.3 13.8 %all_to_all.21 = f32[32,1,128]{2,1,0:T(1,128)S(1)} all-to-all(f32[32,1,128]{2,1,0:T(1,128)S(1)} %broadcast_in_dim.5), channel_id=1, replica_groups=mesh['y'=4,'l'=4,'x'=4,'h'=4,'c'=2] {'x','y','c'}, dimensions={0} | all-to-all | bytes 32768 | tf_op jit(solution)/shard_map/mean_square/all_to_all | solution.py:213
  165.0 0.6 reduce_sum.29
  166.3 0.9 multiply_bitcast_fusion
  (39 shorter events, 0.1 us)
Async XLA Ops:
  7.2 25.7 %copy-start = (bf16[512,512]{1,0:T(8,128)(2,1)S(1)}, bf16[512,512]{1,0:T(8,128)(2,1)}, u32[]{:S(2)}) copy-start(bf16[512,512]{1,0:T(8,128)(2,1)} %param.6) | copy-start | bytes 1572868
  7.2 28.1 %copy-start.4 = (f32[128,6,256]{2,0,1:T(8,128)S(1)}, f32[128,6,256]{2,0,1:T(8,128)}, u32[]{:S(2)}) copy-start(f32[128,6,256]{2,0,1:T(8,128)} %param.10) | copy-start | bytes 2359300
  7.2 28.1 %copy-start.3 = (f32[128,6,256]{2,0,1:T(8,128)S(1)}, f32[128,6,256]{2,0,1:T(8,128)}, u32[]{:S(2)}) copy-start(f32[128,6,256]{2,0,1:T(8,128)} %param.9) | copy-start | bytes 2359300
  7.2 90.6 %all-gather.3.cloned.1.call-start = ((), (), s32[]{:S(2)}) async-start(), calls=%async_computation.5 | async-start | bytes 2621440 | tf_op jit(solution)/shard_map/hidden/all_gather | solution.py:117
  7.2 37.3 %collective-permute-start.1 = (bf16[512,128]{1,0:T(8,128)(2,1)}, bf16[512,128]{1,0:T(8,128)(2,1)S(1)}, u32[]{:S(2)}, u32[]{:S(2)}) collective-permute-start(bf16[512,128]{1,0:T(8,128)(2,1)} %r0.1), channel_id=1, source_target_pairs={{0,4},{2,6},{4,0},{6,2},{1,5},{3,7},{5,1},{7,3},{8,12},{10,14},{12... | collective-permute-start | bytes 393224 | tf_op jit(solution)/shard_map/up/ppermute | solution.py:85
  23.7 20.9 %collective-permute-start = (bf16[512,128]{1,0:T(8,128)(2,1)}, bf16[512,128]{1,0:T(8,128)(2,1)S(1)}, u32[]{:S(2)}, u32[]{:S(2)}) collective-permute-start(bf16[512,128]{1,0:T(8,128)(2,1)} %r0.1), channel_id=1, source_target_pairs={{0,2},{2,4},{4,6},{6,0},{1,3},{3,5},{5,7},{7,1},{8,10},{10,12},{12... | collective-permute-start | bytes 393224 | tf_op jit(solution)/shard_map/up/ppermute | solution.py:85
  27.7 20.3 %collective-permute-start.2 = (bf16[512,128]{1,0:T(8,128)(2,1)}, bf16[512,128]{1,0:T(8,128)(2,1)S(1)}, u32[]{:S(2)}, u32[]{:S(2)}) collective-permute-start(bf16[512,128]{1,0:T(8,128)(2,1)} %r0.1), channel_id=1, source_target_pairs={{0,6},{2,0},{4,2},{6,4},{1,7},{3,1},{5,3},{7,5},{8,14},{10,8},{12,... | collective-permute-start | bytes 393224 | tf_op jit(solution)/shard_map/up/ppermute | solution.py:85
  35.2 1.0 copy-start.5
  35.2 1.1 copy-start.14
  36.3 0.9 copy-start.16
  36.6 1.6 copy-start.1
  36.6 1.0 copy-start.18
  36.6 1.3 copy-start.17
  36.8 1.4 copy-start.15
  39.5 79.1 %all-to-all-start = ((bf16[4,256,512]{2,1,0:T(8,128)(2,1)}), bf16[4,256,512]{2,1,0:T(8,128)(2,1)}, u32[]{:S(2)}, u32[]{:S(2)}) async-start(bf16[4,256,512]{2,1,0:T(8,128)(2,1)} %broadcast_in_dim.4), calls=%async_computation | async-start | bytes 2097152 | tf_op jit(solution)/shard_map/masked/all_to_all | solution.py:131
  43.8 123.5 %reduce-scatter.2.cloned.1.call-start = ((), (), s32[]{:S(2)}) async-start(), calls=%async_computation.4 | async-start | bytes 2621440 | tf_op jit(solution)/shard_map/grad_hidden_sum/reduce_scatter | solution.py:195
  44.5 3.4 %copy-start.19 = (bf16[512,128]{1,0:T(8,128)(2,1)}, bf16[512,128]{1,0:T(8,128)(2,1)S(1)}, u32[]{:S(2)}) copy-start(bf16[512,128]{1,0:T(8,128)(2,1)S(1)} %collective-permute-done.1.r2) | copy-start | bytes 393220
  44.5 3.4 %copy-start.20 = (bf16[512,128]{1,0:T(8,128)(2,1)}, bf16[512,128]{1,0:T(8,128)(2,1)S(1)}, u32[]{:S(2)}) copy-start(bf16[512,128]{1,0:T(8,128)(2,1)S(1)} %collective-permute-done.r1) | copy-start | bytes 393220
  48.0 0.7 copy-start.21
  50.6 33.4 %collective-permute-start.6 = (bf16[4,512,128]{2,1,0:T(8,128)(2,1)}, bf16[4,512,128]{2,1,0:T(8,128)(2,1)S(1)}, u32[]{:S(2)}, u32[]{:S(2)}) collective-permute-start(bf16[4,512,128]{2,1,0:T(8,128)(2,1)} %stack_upstream.1), channel_id=1, source_target_pairs={{0,24},{1,9},{8,136},{9,153},{16,280},{17,265},{24,392},{25,409},{... | collective-permute-start | bytes 1572872 | tf_op jit(solution)/shard_map/upstream_xy/ppermute | solution.py:136
  53.7 35.2 %collective-permute-start.5 = (bf16[4,512,128]{2,1,0:T(8,128)(2,1)}, bf16[4,512,128]{2,1,0:T(8,128)(2,1)S(1)}, u32[]{:S(2)}, u32[]{:S(2)}) collective-permute-start(bf16[4,512,128]{2,1,0:T(8,128)(2,1)} %stack_upstream.1), channel_id=1, source_target_pairs={{0,16},{1,1},{8,128},{9,145},{16,272},{17,257},{24,384},{25,401},{... | collective-permute-start | bytes 1572872 | tf_op jit(solution)/shard_map/upstream_xy/ppermute | solution.py:136
  55.4 36.1 %collective-permute-start.4 = (bf16[4,512,128]{2,1,0:T(8,128)(2,1)}, bf16[4,512,128]{2,1,0:T(8,128)(2,1)S(1)}, u32[]{:S(2)}, u32[]{:S(2)}) collective-permute-start(bf16[4,512,128]{2,1,0:T(8,128)(2,1)} %stack_upstream.1), channel_id=1, source_target_pairs={{0,8},{1,25},{8,152},{9,137},{16,264},{17,281},{24,408},{25,393},{... | collective-permute-start | bytes 1572872 | tf_op jit(solution)/shard_map/upstream_xy/ppermute | solution.py:136
  62.2 31.6 %collective-permute-start.3 = (bf16[4,512,128]{2,1,0:T(8,128)(2,1)}, bf16[4,512,128]{2,1,0:T(8,128)(2,1)S(1)}, u32[]{:S(2)}, u32[]{:S(2)}) collective-permute-start(bf16[4,512,128]{2,1,0:T(8,128)(2,1)} %stack_upstream.1), channel_id=1, source_target_pairs={{0,0},{1,17},{8,144},{9,129},{16,256},{17,273},{24,400},{25,385},{... | collective-permute-start | bytes 1572872 | tf_op jit(solution)/shard_map/upstream_xy/ppermute | solution.py:136
  84.0 13.8 %copy-start.6 = (bf16[4,512,128]{2,1,0:T(8,128)(2,1)}, bf16[4,512,128]{2,1,0:T(8,128)(2,1)S(1)}, u32[]{:S(2)}) copy-start(bf16[4,512,128]{2,1,0:T(8,128)(2,1)S(1)} %collective-permute-done.6.a3) | copy-start | bytes 1572868
  84.0 11.9 %collective-permute-start.10 = (bf16[4,512,128]{2,1,0:T(8,128)(2,1)S(1)}, bf16[4,512,128]{2,1,0:T(8,128)(2,1)S(1)}, u32[]{:S(2)}, u32[]{:S(2)}) collective-permute-start(bf16[4,512,128]{2,1,0:T(8,128)(2,1)S(1)} %collective-permute-done.6.a3), channel_id=1, source_target_pairs={{0,1},{1,0},{2,3},{3,2},{4,5},{5,4},{6,7},{7,6},{8,9},{9,8},{10,11... | collective-permute-start | bytes 1572872 | tf_op jit(solution)/shard_map/upstream_core/ppermute | solution.py:149
  88.9 8.9 %copy-start.7 = (bf16[4,512,128]{2,1,0:T(8,128)(2,1)}, bf16[4,512,128]{2,1,0:T(8,128)(2,1)S(1)}, u32[]{:S(2)}) copy-start(bf16[4,512,128]{2,1,0:T(8,128)(2,1)S(1)} %collective-permute-done.5.a2) | copy-start | bytes 1572868
  88.9 7.1 %collective-permute-start.9 = (bf16[4,512,128]{2,1,0:T(8,128)(2,1)S(1)}, bf16[4,512,128]{2,1,0:T(8,128)(2,1)S(1)}, u32[]{:S(2)}, u32[]{:S(2)}) collective-permute-start(bf16[4,512,128]{2,1,0:T(8,128)(2,1)S(1)} %collective-permute-done.5.a2), channel_id=1, source_target_pairs={{0,1},{1,0},{2,3},{3,2},{4,5},{5,4},{6,7},{7,6},{8,9},{9,8},{10,11... | collective-permute-start | bytes 1572872 | tf_op jit(solution)/shard_map/upstream_core/ppermute | solution.py:149
  91.5 6.3 %copy-start.8 = (bf16[4,512,128]{2,1,0:T(8,128)(2,1)}, bf16[4,512,128]{2,1,0:T(8,128)(2,1)S(1)}, u32[]{:S(2)}) copy-start(bf16[4,512,128]{2,1,0:T(8,128)(2,1)S(1)} %collective-permute-done.4.a1) | copy-start | bytes 1572868
  91.6 4.4 %collective-permute-start.8 = (bf16[4,512,128]{2,1,0:T(8,128)(2,1)S(1)}, bf16[4,512,128]{2,1,0:T(8,128)(2,1)S(1)}, u32[]{:S(2)}, u32[]{:S(2)}) collective-permute-start(bf16[4,512,128]{2,1,0:T(8,128)(2,1)S(1)} %collective-permute-done.4.a1), channel_id=1, source_target_pairs={{0,1},{1,0},{2,3},{3,2},{4,5},{5,4},{6,7},{7,6},{8,9},{9,8},{10,11... | collective-permute-start | bytes 1572872 | tf_op jit(solution)/shard_map/upstream_core/ppermute | solution.py:149
  93.8 4.0 %copy-start.9 = (bf16[4,512,128]{2,1,0:T(8,128)(2,1)}, bf16[4,512,128]{2,1,0:T(8,128)(2,1)S(1)}, u32[]{:S(2)}) copy-start(bf16[4,512,128]{2,1,0:T(8,128)(2,1)S(1)} %collective-permute-done.3.a0) | copy-start | bytes 1572868
  93.9 3.9 %collective-permute-start.7 = (bf16[4,512,128]{2,1,0:T(8,128)(2,1)S(1)}, bf16[4,512,128]{2,1,0:T(8,128)(2,1)}, u32[]{:S(2)}, u32[]{:S(2)}) collective-permute-start(bf16[4,512,128]{2,1,0:T(8,128)(2,1)S(1)} %collective-permute-done.3.a0), channel_id=1, source_target_pairs={{0,1},{1,0},{2,3},{3,2},{4,5},{5,4},{6,7},{7,6},{8,9},{9,8},{10,11... | collective-permute-start | bytes 1572872 | tf_op jit(solution)/shard_map/upstream_core/ppermute | solution.py:149
  95.9 0.8 copy-start.10
  96.0 0.9 copy-start.11
  96.9 0.8 copy-start.12
  101.8 23.0 %collective-permute-start.11 = (bf16[512,256]{1,0:T(8,128)(2,1)}, bf16[512,256]{1,0:T(8,128)(2,1)S(1)}, u32[]{:S(2)}, u32[]{:S(2)}) collective-permute-start(bf16[512,256]{1,0:T(8,128)(2,1)} %grad_masked_far.1.far), channel_id=1, source_target_pairs={{0,64},{32,96},{64,0},{96,32},{1,65},{33,97},{65,1},{97,33},{2,66}... | collective-permute-start | bytes 786440 | tf_op jit(solution)/shard_map/grad_masked_sum/ppermute | solution.py:85
  111.5 14.4 %collective-permute-start.12 = (bf16[512,256]{1,0:T(8,128)(2,1)}, bf16[512,256]{1,0:T(8,128)(2,1)S(1)}, u32[]{:S(2)}, u32[]{:S(2)}) collective-permute-start(bf16[512,256]{1,0:T(8,128)(2,1)} %get-tuple-element.12), channel_id=1, source_target_pairs={{0,32},{32,64},{64,96},{96,0},{1,33},{33,65},{65,97},{97,1},{2,34}... | collective-permute-start | bytes 786440 | tf_op jit(solution)/shard_map/grad_masked_sum/ppermute | solution.py:85
  114.7 15.2 %collective-permute-start.13 = (bf16[512,256]{1,0:T(8,128)(2,1)}, bf16[512,256]{1,0:T(8,128)(2,1)S(1)}, u32[]{:S(2)}, u32[]{:S(2)}) collective-permute-start(bf16[512,256]{1,0:T(8,128)(2,1)} %get-tuple-element.13), channel_id=1, source_target_pairs={{0,96},{32,0},{64,32},{96,64},{1,97},{33,1},{65,33},{97,65},{2,98}... | collective-permute-start | bytes 786440 | tf_op jit(solution)/shard_map/grad_masked_sum/ppermute | solution.py:85
  124.8 1.0 copy-start.13
  124.8 5.1 %copy-start.2 = (bf16[512,256]{1,0:T(8,128)(2,1)S(1)}, bf16[512,256]{1,0:T(8,128)(2,1)}, u32[]{:S(2)}) copy-start(bf16[512,256]{1,0:T(8,128)(2,1)} %copy-done.1) | copy-start | bytes 786436
Sparse Core Ops, SparseCore 0:
  35.4 54.1 all-gather.2
  124.9 34.3 reduce-scatter.1
